TPU v7x, 128 devices: a whole 4x4x4 slice. The times are simulated.
128 devices in a mesh: short: 16 (over z, y), long: 8 (over x, core).
Axes of the slice: x: 4, y: 4, z: 4, core: 2. Of those that a mesh axis runs over, the one named last changes fastest.
Arguments:
- query: bfloat16 [131072, 8, 128], P(('long', 'short')), may hold values from -6 to 6
- key: bfloat16 [131072, 8, 128], P(('long', 'short')), may hold values from -6 to 6
- value: bfloat16 [131072, 8, 128], P(('long', 'short')), may hold values from -6 to 6
- level_weight: float32 [8, 20, 131072], P(None, None, ('long', 'short')), may hold values from 0.25 to 1.75
Outputs:
- attended: bfloat16 [131072, 8, 128], P(('long', 'short'))
All inputs are finite; a program needn't handle non-finite values.
Results may differ from a plain program's by a relative error of at most 0.0019.
Values sent between devices are 32-bit elements; how exact they have to be, the bound alone decides.
No kernel may reach another device: no remote copies, remote signals or barrier semaphores. Data moves between devices by JAX's collectives and lax.ppermute only.
A program may use at most 128 MiB of HBM per device.

v0:
```python
import jax
import jax.numpy as jnp
from jax import lax
from jax.sharding import PartitionSpec as P

EPSILON = 1e-06


def from_partner(value, axis, stride):
    return lax.ppermute(value, axis, [(i, i ^ 1 << stride) for i in range(lax.axis_size(axis))])


def level_table(row_ids, col_ids, local_bits):
    differ = jnp.bitwise_xor(row_ids[:, None], col_ids[None, :])
    levels = jnp.zeros(differ.shape, jnp.int32)
    for bit_no in range(local_bits):
        levels = levels + (differ >= 1 << bit_no).astype(jnp.int32)
    return levels


def near_part(query, key, value, level_weight):
    length = query.shape[0]
    local_bits = length.bit_length() - 1
    block_rows = min(512, length)
    col_ids = jnp.arange(length, dtype=jnp.int32)
    outputs = []
    for row_start in range(0, length, block_rows):
        row_ids = row_start + jnp.arange(block_rows, dtype=jnp.int32)
        levels = level_table(row_ids, col_ids, local_bits)
        causal = col_ids[None, :] <= row_ids[:, None]
        scores = jnp.einsum(
            "thd,shd->hts",
            query[row_start : row_start + block_rows],
            key,
            preferred_element_type=jnp.float32,
        )
        mixing = jnp.zeros(scores.shape, jnp.float32)
        for level_no in range(local_bits + 1):
            chosen = jnp.where(levels == level_no, 1.0, 0.0).astype(jnp.float32)
            mixing = (
                mixing
                + chosen[None]
                * level_weight[:, level_no, row_start : row_start + block_rows][:, :, None]
            )
        weighted = jnp.where(causal[None], mixing * scores, 0.0).astype(jnp.bfloat16)
        outputs.append(
            jnp.einsum("hts,she->the", weighted, value, preferred_element_type=jnp.float32)
        )
    return jnp.concatenate(outputs, 0)


def per_device(query, key, value, level_weight):
    length = query.shape[0]
    local_bits = length.bit_length() - 1
    state = jnp.einsum("thd,the->hde", key, value, preferred_element_type=jnp.float32)
    short_bits = lax.axis_size("short").bit_length() - 1
    long_bits = lax.axis_size("long").bit_length() - 1
    short_pos = lax.axis_index("short")
    long_pos = lax.axis_index("long")
    group = state
    found = []
    for bit_no in range(short_bits):
        other = from_partner(group, "short", bit_no)
        found.append(jnp.where(short_pos >> bit_no & 1 == 1, other, 0.0))
        group = group + other
    near_buckets = jnp.stack(found, 0)
    outer = group
    found_far = []
    for bit_no in range(long_bits):
        other_far = from_partner(outer, "long", bit_no)
        found_far.append(jnp.where(long_pos >> bit_no & 1 == 1, other_far, 0.0))
        if bit_no + 1 < long_bits:
            outer = outer + other_far
    far_buckets = jnp.stack(found_far, 0)
    buckets = jnp.concatenate([near_buckets, far_buckets], 0)
    near = near_part(query, key, value, level_weight)
    bit_count = buckets.shape[0]
    products = jnp.einsum(
        "thd,bhde->bthe", query.astype(jnp.float32), buckets, precision=lax.Precision.HIGHEST
    )
    gains = jnp.transpose(
        level_weight[:, local_bits + 1 : local_bits + 1 + bit_count, :], (1, 2, 0)
    )
    total = near + jnp.sum(products * gains[..., None], 0)
    scale = lax.rsqrt(jnp.mean(total * total, -1, keepdims=True) + EPSILON)
    return (total * scale).astype(jnp.bfloat16)


def solution(mesh):
    return jax.shard_map(
        per_device,
        mesh=mesh,
        in_specs=(
            P(("long", "short"), None, None),
            P(("long", "short"), None, None),
            P(("long", "short"), None, None),
            P(None, None, ("long", "short")),
        ),
        out_specs=P(("long", "short"), None, None),
        check_vma=False,
    )
```

profile of v0, /device:TPU:1, one launch (start us, length us, event | category | flops | bytes accessed | tf_op | source)
XLA Modules:
  0.0 161.9 jit_solution(3465950274178693703)
XLA Ops:
  0.0 0.0 copy-start
  0.0 4.2 %copy.15 = bf16[1024,8,128]{0,2,1:T(8,128)(2,1)} copy(bf16[1024,8,128]{2,1,0:T(8,128)(2,1)} %param.5) | data formatting | bytes 4194304 | tf_op args[1]
  4.3 0.0 copy-done
  4.3 0.0 copy-start.7
  4.3 3.5 %fusion.23 = f32[8,128,128]{2,1,0:T(8,128)} fusion(bf16[1024,8,128]{0,2,1:T(8,128)(2,1)} %copy.15, bf16[1024,8,128]{2,1,0:T(8,128)(2,1)S(1)} %copy-done), kind=kOutput, calls=%fused_computation.59 | convolution fusion | flops 268435456 | bytes 4718592 | tf_op jit(solution)/shard_map/thd,the->hde/dot_general | solution.py:55
  7.7 2.1 %collective-permute-start = (f32[8,128,128]{2,1,0:T(8,128)}, f32[8,128,128]{2,1,0:T(8,128)}, u32[]{:S(2)}, u32[]{:S(2)}) collective-permute-start(f32[8,128,128]{2,1,0:T(8,128)} %fusion.23), channel_id=1, source_target_pairs={{0,8},{8,0},{16,24},{24,16},{32,40},{40,32},{48,56},{56,48},{64,72... | collective-permute-start | bytes 1572872 | tf_op jit(solution)/shard_map/ppermute | solution.py:10
  9.9 0.0 copy-done.7
  9.9 4.5 %compare_select_fusion.10 = (f32[512,1024]{1,0:T(8,128)S(1)}, f32[512,1024]{1,0:T(8,128)S(1)}, f32[512,1024]{1,0:T(8,128)S(1)}, f32[512,1024]{1,0:T(8,128)S(1)},...) fusion(s32[512]{0:T(512)S(1)} %iota_add_fusion), kind=kLoop, calls=%fused_computation.45 | loop fusion | flops 27262976 | bytes 23070720 | tf_op jit(solution)/shard_map/jit(_where)/select_n | solution.py:39
  14.4 0.4 iota_compare_fusion
  14.7 0.7 compare_select_fusion.11
  15.4 0.0 copy-start.5
  15.4 0.7 compare_select_fusion.13
  16.1 0.9 copy-done.5
  17.0 0.1 fusion.33
  17.1 22.2 %select_convert_fusion.clone.4 = bf16[8,512,1024]{2,1,0:T(8,128)(2,1)} fusion(bf16[1024,8,128]{0,2,1:T(8,128)(2,1)} %copy.15, f32[8,512]{1,0:T(8,128)S(1)} %get-tuple-element.28, f32[512,1024]{1,0:T(8,128)S(1)} %get-tuple-element.39, f32[8,512]{1,0:T(8,128)S(1)} %get-tuple-element.8, f32[512,1024]{1,0:T(8,128)S(1)} %get-tuple-element.38, ...), kind=kOutput, calls=%fused_computation.2.clone.clone.clone.1 | convolution fusion | flops 1174405120 | bytes 35307520 | tf_op jit(solution)/shard_map/thd,shd->hts/dot_general | solution.py:31
  39.3 0.7 compare_select_fusion.15
  40.0 0.7 compare_select_fusion.17
  40.7 0.0 collective-permute-done
  40.7 1.3 add.1190
  41.9 2.7 %collective-permute-start.1 = (f32[8,128,128]{2,1,0:T(8,128)S(1)}, f32[8,128,128]{2,1,0:T(8,128)S(1)}, u32[]{:S(2)}, u32[]{:S(2)}) collective-permute-start(f32[8,128,128]{2,1,0:T(8,128)S(1)} %add.1190), channel_id=1, source_target_pairs={{0,16},{8,24},{16,0},{24,8},{32,48},{40,56},{48,32},{56,40},{64,80... | collective-permute-start | bytes 1572872 | tf_op jit(solution)/shard_map/ppermute | solution.py:10
  44.6 0.4 compare_select_fusion.21
  45.0 0.1 iota_compare_fusion.1
  45.2 0.0 copy-start.2
  45.2 0.7 compare_select_fusion.19
  45.9 10.1 %collective-permute-done.1 = f32[8,128,128]{2,1,0:T(8,128)S(1)} collective-permute-done((f32[8,128,128]{2,1,0:T(8,128)S(1)}, f32[8,128,128]{2,1,0:T(8,128)S(1)}, u32[]{:S(2)}, u32[]{:S(2)}) %collective-permute-start.1) | collective-permute-done | bytes 524320 | tf_op jit(solution)/shard_map/ppermute | solution.py:10
  56.0 0.1 add.1191
  56.1 1.7 %collective-permute-start.2 = (f32[8,128,128]{2,1,0:T(8,128)S(1)}, f32[8,128,128]{2,1,0:T(8,128)}, u32[]{:S(2)}, u32[]{:S(2)}) collective-permute-start(f32[8,128,128]{2,1,0:T(8,128)S(1)} %add.1191), channel_id=1, source_target_pairs={{0,32},{8,40},{16,48},{24,56},{32,0},{40,8},{48,16},{56,24},{64,96... | collective-permute-start | bytes 1572872 | tf_op jit(solution)/shard_map/ppermute | solution.py:10
  57.8 0.0 copy-done.2
  57.8 21.8 %select_convert_fusion.1.clone.2 = bf16[8,512,1024]{2,1,0:T(8,128)(2,1)} fusion(bf16[1024,8,128]{0,2,1:T(8,128)(2,1)S(1)} %copy-done.2, f32[8,512]{1,0:T(8,128)S(1)} %get-tuple-element.18, f32[512,1024]{1,0:T(8,128)S(1)} %get-tuple-element.40, f32[8,512]{1,0:T(8,128)S(1)} %get-tuple-element.19, f32[512,1024]{1,0:T(8,128)S(1)} %get-tuple-element.41, ...), kind=kOutput, calls=%fused_computation.3.clone.clone.clone | convolution fusion | flops 1174405120 | bytes 35307520 | tf_op jit(solution)/shard_map/thd,shd->hts/dot_general | solution.py:31
  79.6 1.0 slice_bitcast_fusion
  80.6 0.1 copy.19
  80.7 0.0 collective-permute-done.2
  80.7 0.0 slice-start
  80.7 1.2 add.1192
  82.0 0.0 slice-start.1
  82.0 3.6 %collective-permute-start.3 = (f32[8,128,128]{2,1,0:T(8,128)S(1)}, f32[8,128,128]{2,1,0:T(8,128)S(1)}, u32[]{:S(2)}, u32[]{:S(2)}) collective-permute-start(f32[8,128,128]{2,1,0:T(8,128)S(1)} %add.1192), channel_id=1, source_target_pairs={{0,64},{8,72},{16,80},{24,88},{32,96},{40,104},{48,112},{56,120},{... | collective-permute-start | bytes 1572872 | tf_op jit(solution)/shard_map/ppermute | solution.py:10
  85.5 7.0 %convolution_bitcast_fusion = f32[512,8,128]{2,0,1:T(8,128)} fusion(bf16[1024,8,128]{2,1,0:T(8,128)(2,1)S(1)} %copy-done, bf16[8,512,1024]{2,1,0:T(8,128)(2,1)} %select_convert_fusion.clone.4), kind=kOutput, calls=%fused_computation.57 | convolution fusion | flops 1073741824 | bytes 12582912 | tf_op jit(solution)/shard_map/hts,she->the/dot_general | solution.py:47
  92.6 3.0 %collective-permute-done.3 = f32[8,128,128]{2,1,0:T(8,128)S(1)} collective-permute-done((f32[8,128,128]{2,1,0:T(8,128)S(1)}, f32[8,128,128]{2,1,0:T(8,128)S(1)}, u32[]{:S(2)}, u32[]{:S(2)}) %collective-permute-start.3) | collective-permute-done | bytes 524320 | tf_op jit(solution)/shard_map/ppermute | solution.py:10
  95.6 0.1 add.1193
  95.7 2.9 %collective-permute-start.4 = (f32[8,128,128]{2,1,0:T(8,128)S(1)}, f32[8,128,128]{2,1,0:T(8,128)S(1)}, u32[]{:S(2)}, u32[]{:S(2)}) collective-permute-start(f32[8,128,128]{2,1,0:T(8,128)S(1)} %add.1193), channel_id=1, source_target_pairs={{0,1},{1,0},{2,3},{3,2},{4,5},{5,4},{6,7},{7,6},{8,9},{9,8},{10,11... | collective-permute-start | bytes 1572872 | tf_op jit(solution)/shard_map/ppermute | solution.py:10
  98.6 0.0 slice-done
  98.6 0.0 slice-done.1
  98.6 3.7 %convolution_bitcast_fusion.1 = f32[512,8,128]{2,0,1:T(8,128)} fusion(bf16[1024,8,128]{2,1,0:T(8,128)(2,1)S(1)} %copy-done, bf16[8,512,1024]{2,1,0:T(8,128)(2,1)S(1)} %bitcast.80), kind=kOutput, calls=%fused_computation.58 | convolution fusion | flops 1073741824 | bytes 12582912 | tf_op jit(solution)/shard_map/hts,she->the/dot_general | solution.py:47
  102.3 0.0 collective-permute-done.4
  102.3 0.1 add.1194
  102.4 1.3 collective-permute-start.5
  103.8 12.1 %collective-permute-done.5 = f32[8,128,128]{2,1,0:T(8,128)S(1)} collective-permute-done((f32[8,128,128]{2,1,0:T(8,128)S(1)}, f32[8,128,128]{2,1,0:T(8,128)S(1)}, u32[]{:S(2)}, u32[]{:S(2)}) %collective-permute-start.5) | collective-permute-done | bytes 524320 | tf_op jit(solution)/shard_map/ppermute | solution.py:10
  116.0 0.1 add.1195
  116.1 0.0 copy-start.6
  116.1 2.8 %collective-permute-start.6 = (f32[8,128,128]{2,1,0:T(8,128)S(1)}, f32[8,128,128]{2,1,0:T(8,128)S(1)}, u32[]{:S(2)}, u32[]{:S(2)}) collective-permute-start(f32[8,128,128]{2,1,0:T(8,128)S(1)} %add.1195), channel_id=1, source_target_pairs={{0,4},{1,5},{2,6},{3,7},{4,0},{5,1},{6,2},{7,3},{8,12},{9,13},{10,... | collective-permute-start | bytes 1572872 | tf_op jit(solution)/shard_map/ppermute | solution.py:10
  119.0 11.2 %collective-permute-done.6 = f32[8,128,128]{2,1,0:T(8,128)S(1)} collective-permute-done((f32[8,128,128]{2,1,0:T(8,128)S(1)}, f32[8,128,128]{2,1,0:T(8,128)S(1)}, u32[]{:S(2)}, u32[]{:S(2)}) %collective-permute-start.6) | collective-permute-done | bytes 524320 | tf_op jit(solution)/shard_map/ppermute | solution.py:10
  130.3 0.0 copy-done.6
  130.3 16.1 %fusion = f32[1024,8,128]{0,2,1:T(8,128)} fusion(f32[7,1024,8]{1,0,2:T(8,128)S(1)} %copy.19, f32[7,8,128,128]{3,2,1,0:T(8,128)S(1)} %bitcast_dynamic-update-slice_fusion, bf16[1024,8,128,1]{2,1,0,3:T(8,128)(2,1)S(1)} %bitcast.81), kind=kOutput, calls=%fused_computation.1 | convolution fusion | flops 11287920640 | bytes 10190848 | tf_op jit(solution)/shard_map/thd,bhde->bthe/dot_general | solution.py:78
  146.5 5.4 %copy.20 = f32[1024,8,128]{2,0,1:T(8,128)} copy(f32[1024,8,128]{0,2,1:T(8,128)} %fusion) | data formatting | bytes 8388608 | tf_op jit(solution)/shard_map/reduce_sum | solution.py:84
  151.9 0.0 copy-start.1
  151.9 0.0 copy-start.3
  151.9 0.0 copy-start.4
  151.9 4.8 %multiply_reduce_fusion = f32[1024,8]{0,1:T(8,128)S(1)} fusion(f32[1024,8,128]{2,0,1:T(8,128)} %copy.20, f32[512,8,128]{2,0,1:T(8,128)} %convolution_bitcast_fusion, f32[512,8,128]{2,0,1:T(8,128)} %convolution_bitcast_fusion.1), kind=kLoop, calls=%fused_computation.6 | loop fusion | flops 4186112 | bytes 8421376 | tf_op jit(solution)/shard_map/reduce_sum | solution.py:85
  156.7 0.0 copy-done.1
  156.7 0.5 copy-done.3
  157.2 0.6 copy-done.4
  157.8 1.4 multiply_convert_fusion
  159.2 2.7 %copy.21 = bf16[1024,8,128]{2,1,0:T(8,128)(2,1)} copy(bf16[1024,8,128]{2,0,1:T(8,128)(2,1)S(1)} %multiply_convert_fusion) | data formatting | bytes 4194304 | tf_op jit(solution)/shard_map/convert_element_type | solution.py:86
  (12 shorter events, 0.3 us)
Async XLA Ops:
  0.0 4.3 %copy-start = (bf16[1024,8,128]{2,1,0:T(8,128)(2,1)S(1)}, bf16[1024,8,128]{2,1,0:T(8,128)(2,1)}, u32[]{:S(2)}) copy-start(bf16[1024,8,128]{2,1,0:T(8,128)(2,1)} %param.6) | copy-start | bytes 6291460
  4.3 5.6 %copy-start.7 = (f32[8,20,1024]{2,0,1:T(8,128)S(1)}, f32[8,20,1024]{2,0,1:T(8,128)}, u32[]{:S(2)}) copy-start(f32[8,20,1024]{2,0,1:T(8,128)} %param.7) | copy-start | bytes 1966084
  7.7 32.9 %collective-permute-start = (f32[8,128,128]{2,1,0:T(8,128)}, f32[8,128,128]{2,1,0:T(8,128)}, u32[]{:S(2)}, u32[]{:S(2)}) collective-permute-start(f32[8,128,128]{2,1,0:T(8,128)} %fusion.23), channel_id=1, source_target_pairs={{0,8},{8,0},{16,24},{24,16},{32,40},{40,32},{48,56},{56,48},{64,72... | collective-permute-start | bytes 1572872 | tf_op jit(solution)/shard_map/ppermute | solution.py:10
  15.4 1.6 copy-start.5
  41.9 14.1 %collective-permute-start.1 = (f32[8,128,128]{2,1,0:T(8,128)S(1)}, f32[8,128,128]{2,1,0:T(8,128)S(1)}, u32[]{:S(2)}, u32[]{:S(2)}) collective-permute-start(f32[8,128,128]{2,1,0:T(8,128)S(1)} %add.1190), channel_id=1, source_target_pairs={{0,16},{8,24},{16,0},{24,8},{32,48},{40,56},{48,32},{56,40},{64,80... | collective-permute-start | bytes 1572872 | tf_op jit(solution)/shard_map/ppermute | solution.py:10
  45.2 12.6 %copy-start.2 = (bf16[1024,8,128]{0,2,1:T(8,128)(2,1)S(1)}, bf16[1024,8,128]{0,2,1:T(8,128)(2,1)}, u32[]{:S(2)}) copy-start(bf16[1024,8,128]{0,2,1:T(8,128)(2,1)} %copy.15) | copy-start | bytes 6291460
  56.1 24.6 %collective-permute-start.2 = (f32[8,128,128]{2,1,0:T(8,128)S(1)}, f32[8,128,128]{2,1,0:T(8,128)}, u32[]{:S(2)}, u32[]{:S(2)}) collective-permute-start(f32[8,128,128]{2,1,0:T(8,128)S(1)} %add.1191), channel_id=1, source_target_pairs={{0,32},{8,40},{16,48},{24,56},{32,0},{40,8},{48,16},{56,24},{64,96... | collective-permute-start | bytes 1572872 | tf_op jit(solution)/shard_map/ppermute | solution.py:10
  80.7 17.9 %slice-start = ((s8[8388608]{0:T(1024)(128)(4,1)}), s8[4194304]{0:T(1024)(128)(4,1)S(1)}, s32[]{:S(2)}) async-start(s8[8388608]{0:T(1024)(128)(4,1)} %bitcast.79), calls=%async_computation | async-start | bytes 8388608
  82.0 16.6 %slice-start.1 = ((s8[8388608]{0:T(1024)(128)(4,1)}), s8[4194304]{0:T(1024)(128)(4,1)S(1)}, s32[]{:S(2)}) async-start(s8[8388608]{0:T(1024)(128)(4,1)} %bitcast.79), calls=%async_computation.1 | async-start | bytes 8388608
  82.0 13.6 %collective-permute-start.3 = (f32[8,128,128]{2,1,0:T(8,128)S(1)}, f32[8,128,128]{2,1,0:T(8,128)S(1)}, u32[]{:S(2)}, u32[]{:S(2)}) collective-permute-start(f32[8,128,128]{2,1,0:T(8,128)S(1)} %add.1192), channel_id=1, source_target_pairs={{0,64},{8,72},{16,80},{24,88},{32,96},{40,104},{48,112},{56,120},{... | collective-permute-start | bytes 1572872 | tf_op jit(solution)/shard_map/ppermute | solution.py:10
  95.7 6.6 %collective-permute-start.4 = (f32[8,128,128]{2,1,0:T(8,128)S(1)}, f32[8,128,128]{2,1,0:T(8,128)S(1)}, u32[]{:S(2)}, u32[]{:S(2)}) collective-permute-start(f32[8,128,128]{2,1,0:T(8,128)S(1)} %add.1193), channel_id=1, source_target_pairs={{0,1},{1,0},{2,3},{3,2},{4,5},{5,4},{6,7},{7,6},{8,9},{9,8},{10,11... | collective-permute-start | bytes 1572872 | tf_op jit(solution)/shard_map/ppermute | solution.py:10
  102.4 13.6 %collective-permute-start.5 = (f32[8,128,128]{2,1,0:T(8,128)S(1)}, f32[8,128,128]{2,1,0:T(8,128)S(1)}, u32[]{:S(2)}, u32[]{:S(2)}) collective-permute-start(f32[8,128,128]{2,1,0:T(8,128)S(1)} %add.1194), channel_id=1, source_target_pairs={{0,2},{1,3},{2,0},{3,1},{4,6},{5,7},{6,4},{7,5},{8,10},{9,11},{10,... | collective-permute-start | bytes 1572872 | tf_op jit(solution)/shard_map/ppermute | solution.py:10
  116.1 14.3 %copy-start.6 = (bf16[1024,8,128]{2,1,0:T(8,128)(2,1)S(1)}, bf16[1024,8,128]{2,1,0:T(8,128)(2,1)}, u32[]{:S(2)}) copy-start(bf16[1024,8,128]{2,1,0:T(8,128)(2,1)} %param.4) | copy-start | bytes 6291460
  116.1 14.2 %collective-permute-start.6 = (f32[8,128,128]{2,1,0:T(8,128)S(1)}, f32[8,128,128]{2,1,0:T(8,128)S(1)}, u32[]{:S(2)}, u32[]{:S(2)}) collective-permute-start(f32[8,128,128]{2,1,0:T(8,128)S(1)} %add.1195), channel_id=1, source_target_pairs={{0,4},{1,5},{2,6},{3,7},{4,0},{5,1},{6,2},{7,3},{8,12},{9,13},{10,... | collective-permute-start | bytes 1572872 | tf_op jit(solution)/shard_map/ppermute | solution.py:10
  151.9 4.8 %copy-start.1 = (f32[1024,8,128]{2,0,1:T(8,128)S(1)}, f32[1024,8,128]{2,0,1:T(8,128)}, u32[]{:S(2)}) copy-start(f32[1024,8,128]{2,0,1:T(8,128)} %copy.20) | copy-start | bytes 12582916
  151.9 5.3 %copy-start.3 = (f32[512,8,128]{2,0,1:T(8,128)S(1)}, f32[512,8,128]{2,0,1:T(8,128)}, u32[]{:S(2)}) copy-start(f32[512,8,128]{2,0,1:T(8,128)} %convolution_bitcast_fusion) | copy-start | bytes 6291460
  151.9 5.9 %copy-start.4 = (f32[512,8,128]{2,0,1:T(8,128)S(1)}, f32[512,8,128]{2,0,1:T(8,128)}, u32[]{:S(2)}) copy-start(f32[512,8,128]{2,0,1:T(8,128)} %convolution_bitcast_fusion.1) | copy-start | bytes 6291460
where the time goes:
time: 163 us; the launch traced here: 162 us
  matrix products  74.4 us (46%)
  waiting for transfers between devices  36.6 us (22%)
  other arithmetic  17.9 us (11%)
  starting transfers between devices  17.1 us (10%)
  local copies, waits for them, and re-layouts  15.7 us (10%)
    dot_general x2, matrix products, near_part(): jnp.einsum('thd,shd->hts', query[row_start:row_start + block_rows], key,...  44 us
    ppermute x7, waiting for transfers between devices, from_partner(): lax.ppermute(value, axis, [(i, i ^ 1 << stride) for i in range(lax.axis_s...  36.6 us
    ppermute x7, starting transfers between devices, from_partner(): lax.ppermute(value, axis, [(i, i ^ 1 << stride) for i in range(lax.axis_s...  17.1 us
    dot_general x1, matrix products, per_device(): jnp.einsum('thd,bhde->bthe', query.astype(jnp.float32), buckets, precisio...  16.1 us
    dot_general x2, matrix products, near_part(): jnp.einsum('hts,she->the', weighted, value, preferred_element_type=jnp.fl...  10.8 us
    select_n x7, other arithmetic, near_part(): chosen = jnp.where(levels == level_no, 1.0, 0.0).astype(jnp.float32)  8.12 us
    unnamed x21, local copies, waits for them, and re-layouts  6.35 us
    reduce_sum x1, local copies, waits for them, and re-layouts, per_device(): total = near + jnp.sum(products * gains[..., None], 0)  5.39 us
  transfers between devices with their start and end apart: 7, of which 4 were waited for; matrix products, arithmetic and copies ran while one was open for 40% of the time, Pallas kernels for 0%

commit v1 on v0

v1 whole, which is shorter than its diff:
```python
import jax
import jax.numpy as jnp
from jax import lax
from jax.experimental import pallas as pl
from jax.experimental.pallas import tpu as pltpu
from jax.sharding import PartitionSpec as P

EPSILON = 1e-06
VMEM_LIMIT = 56 * 1024 * 1024
NT = (((1,), (1,)), ((), ()))
NN = (((1,), (0,)), ((), ()))


def dot(lhs, rhs, dims):
    return lax.dot_general(lhs, rhs, dims, preferred_element_type=jnp.float32)


def state_kernel(key_ref, value_ref, state_ref, key_out, value_out, key_f, value_f):
    @pl.when(pl.program_id(0) == 0)
    def _():
        state_ref[...] = jnp.zeros_like(state_ref)

    key_f[...] = key_ref[...].astype(jnp.float32)
    value_f[...] = value_ref[...].astype(jnp.float32)
    for head in range(key_ref.shape[1]):
        key_h = key_f[:, head, :].astype(jnp.bfloat16)
        value_t = value_f[:, head, :].T.astype(jnp.bfloat16)
        key_out[head] = key_h
        value_out[head] = value_t
        state_ref[head] += dot(value_t, key_h, NN)


def states(key, value, rows=256):
    length, heads, width = key.shape
    whole = pl.BlockSpec((rows, heads, width), lambda i: (i, 0, 0))
    return pl.pallas_call(
        state_kernel,
        grid=(length // rows,),
        in_specs=[whole, whole],
        out_specs=[
            pl.BlockSpec((heads, width, width), lambda i: (0, 0, 0)),
            pl.BlockSpec((heads, rows, width), lambda i: (0, i, 0)),
            pl.BlockSpec((heads, width, rows), lambda i: (0, 0, i)),
        ],
        out_shape=[
            jax.ShapeDtypeStruct((heads, width, width), jnp.float32),
            jax.ShapeDtypeStruct((heads, length, width), jnp.bfloat16),
            jax.ShapeDtypeStruct((heads, width, length), jnp.bfloat16),
        ],
        scratch_shapes=[pltpu.VMEM((rows, heads, width), jnp.float32)] * 2,
        compiler_params=pltpu.CompilerParams(vmem_limit_bytes=VMEM_LIMIT),
        cost_estimate=pl.CostEstimate(flops=10**9, bytes_accessed=8 * 2**20, transcendentals=0),
        name="states",
    )(key, value)


def query_kernel(query_ref, query_out, query_f):
    query_f[...] = query_ref[...].astype(jnp.float32)
    for head in range(query_ref.shape[1]):
        query_out[head] = query_f[:, head, :].astype(jnp.bfloat16)


def by_head(query, rows=256):
    length, heads, width = query.shape
    return pl.pallas_call(
        query_kernel,
        grid=(length // rows,),
        in_specs=[pl.BlockSpec((rows, heads, width), lambda i: (i, 0, 0))],
        out_specs=pl.BlockSpec((heads, rows, width), lambda i: (0, i, 0)),
        out_shape=jax.ShapeDtypeStruct((heads, length, width), jnp.bfloat16),
        scratch_shapes=[pltpu.VMEM((rows, heads, width), jnp.float32)],
        compiler_params=pltpu.CompilerParams(vmem_limit_bytes=VMEM_LIMIT),
        cost_estimate=pl.CostEstimate(flops=10**6, bytes_accessed=4 * 2**20, transcendentals=0),
        name="by_head",
    )(query)


TILE = 256


def near_kernel(query_ref, key_ref, value_ref, weight_ref, near_ref):
    length = query_ref.shape[1]
    head = pl.program_id(0)
    groups = TILE // 8
    group_r = lax.broadcasted_iota(jnp.int32, (groups, TILE), 0)
    group_t = lax.broadcasted_iota(jnp.int32, (groups, TILE), 1) >> 3
    apart = group_r ^ group_t
    later = group_t > group_r
    inner_s = lax.broadcasted_iota(jnp.int32, (8, TILE), 0)
    inner_t = lax.broadcasted_iota(jnp.int32, (8, TILE), 1) & 7
    inner = inner_s ^ inner_t
    same = (
        lax.broadcasted_iota(jnp.int32, (groups, 8, TILE), 0)
        == lax.broadcasted_iota(jnp.int32, (groups, 8, TILE), 2) >> 3
    )
    for tile in range(length // TILE):
        cols = slice(tile * TILE, (tile + 1) * TILE)

        def gain(level):
            return weight_ref[level, pl.ds(head, 1), cols]

        query = query_ref[0, cols, :]
        parts = []
        for other in range(tile):
            scores = dot(key_ref[0, other * TILE : (other + 1) * TILE, :], query, NT)
            parts.append((scores * gain(8 + (tile ^ other).bit_length())).astype(jnp.bfloat16))
        outer = gain(4)
        for level in range(5, 9):
            outer = jnp.where(apart >= 1 << (level - 4), gain(level), outer)
        outer = jnp.where(later, outer, 0.0)
        small = gain(0)
        for level in range(1, 4):
            small = jnp.where(inner >= 1 << (level - 1), gain(level), small)
        small = jnp.where(inner_s <= inner_t, small, 0.0)
        mixing = jnp.where(same, small[None], outer[:, None, :]).reshape(TILE, TILE)
        scores = dot(key_ref[0, cols, :], query, NT)
        parts.append((scores * mixing).astype(jnp.bfloat16))
        weighted = jnp.concatenate(parts, 0)
        near_ref[0, :, cols] = dot(value_ref[0, :, : (tile + 1) * TILE], weighted, NN)


def near_part(query, key, value, level_weight):
    heads, length, width = query.shape
    levels = level_weight.shape[0]
    rows = pl.BlockSpec((1, length, width), lambda h: (h, 0, 0))
    flat = pl.BlockSpec((1, width, length), lambda h: (h, 0, 0))
    return pl.pallas_call(
        near_kernel,
        grid=(heads,),
        in_specs=[rows, rows, flat, pl.BlockSpec((levels, heads, length), lambda h: (0, 0, 0))],
        out_specs=flat,
        out_shape=jax.ShapeDtypeStruct((heads, width, length), jnp.float32),
        compiler_params=pltpu.CompilerParams(vmem_limit_bytes=VMEM_LIMIT),
        cost_estimate=pl.CostEstimate(
            flops=8 * 10**9, bytes_accessed=12 * 2**20, transcendentals=0
        ),
        name="near",
    )(query, key, value, level_weight)


def far_kernel(local_bits, block_ref, query_ref, near_ref, weight_ref, *rest):
    *bucket_refs, out_ref, split, total_f = rest
    bits = len(bucket_refs)
    heads, rows, width = query_ref.shape

    @pl.when(pl.program_id(0) == 0)
    def _():
        for bit in range(bits):
            for head in range(heads):
                bucket = bucket_refs[bit][head]
                high = bucket.astype(jnp.bfloat16)
                low = (bucket - high.astype(jnp.float32)).astype(jnp.bfloat16)
                split[head, bit * width : (bit + 1) * width, :width] = high
                split[head, bit * width : (bit + 1) * width, width:] = low

    block = block_ref[0]
    for head in range(heads):
        query = query_ref[head]
        products = dot(split[head], jnp.concatenate([query, query], 1), NT)
        total = near_ref[head]
        for bit in range(bits):
            level = local_bits + 1 + bit
            gain = weight_ref[level, head : head + 1, :]
            gain = jnp.where((block >> bit) & 1 == 1, gain, 0.0)
            total = total + products[bit * width : (bit + 1) * width, :] * gain
        mean = jnp.sum(total * total, 0, keepdims=True) * (1.0 / width)
        total = total * lax.rsqrt(mean + EPSILON)
        total_f[:, head, :] = total.T
    out_ref[...] = total_f[...].astype(jnp.bfloat16)


def finish(block, query, near, level_weight, buckets, rows=256):
    heads, length, width = query.shape
    levels = level_weight.shape[0]
    local_bits = length.bit_length() - 1
    bits = len(buckets)
    return pl.pallas_call(
        lambda *refs: far_kernel(local_bits, *refs),
        grid=(length // rows,),
        in_specs=[
            pl.BlockSpec(memory_space=pltpu.SMEM),
            pl.BlockSpec((heads, rows, width), lambda i: (0, i, 0)),
            pl.BlockSpec((heads, width, rows), lambda i: (0, 0, i)),
            pl.BlockSpec((levels, heads, rows), lambda i: (0, 0, i)),
        ]
        + [pl.BlockSpec((heads, width, width), lambda i: (0, 0, 0))] * bits,
        out_specs=pl.BlockSpec((rows, heads, width), lambda i: (i, 0, 0)),
        out_shape=jax.ShapeDtypeStruct((length, heads, width), jnp.bfloat16),
        scratch_shapes=[
            pltpu.VMEM((heads, bits * width, 2 * width), jnp.bfloat16),
            pltpu.VMEM((rows, heads, width), jnp.float32),
        ],
        compiler_params=pltpu.CompilerParams(vmem_limit_bytes=VMEM_LIMIT),
        cost_estimate=pl.CostEstimate(
            flops=8 * 10**9, bytes_accessed=12 * 2**20, transcendentals=0
        ),
        name="finish",
    )(block, query, near, level_weight, *buckets)


def swap(value, axis, bit):
    size = lax.axis_size(axis)
    return lax.ppermute(value, axis, [(i, partner(i, axis, bit)) for i in range(size)])


def partner(i, axis, bit):
    crossing = (1, 3) if axis == "short" else (2,)
    return i ^ (1 << bit) ^ (1 << (bit - 1)) if bit in crossing else i ^ (1 << bit)


def tree(state):
    buckets = []
    group = state
    for axis in ("short", "long"):
        for bit in range(lax.axis_size(axis).bit_length() - 1):
            other = swap(group, axis, bit)
            buckets.append(other)
            group = group + other
    return buckets


def per_device(query, key, value, level_weight):
    level_weight = jnp.transpose(level_weight, (1, 0, 2))
    state, key_h, value_t = states(key, value)
    block = lax.axis_index("long") * lax.axis_size("short") + lax.axis_index("short")
    buckets = tree(state)
    query_h = by_head(query)
    near = near_part(query_h, key_h, value_t, level_weight)
    return finish(block.astype(jnp.int32)[None], query_h, near, level_weight, buckets)


def solution(mesh):
    return jax.shard_map(
        per_device,
        mesh=mesh,
        in_specs=(
            P(("long", "short"), None, None),
            P(("long", "short"), None, None),
            P(("long", "short"), None, None),
            P(None, None, ("long", "short")),
        ),
        out_specs=P(("long", "short"), None, None),
        check_vma=False,
    )
```

time: 163 us -> 108 us (0.66)
  matrix products: 74.4 us -> 0 us
  Pallas kernels: 0 us -> 40.6 us
  other arithmetic: 17.9 us -> 1.64 us
  local copies, waits for them, and re-layouts: 15.7 us -> 0.81 us
  waiting for transfers between devices: 36.6 us -> 46.7 us
    dot_general x6 -> x0, matrix products: 74.4 us -> none  [the longest x2 44 us: near_part(): jnp.einsum('thd,shd->hts', query[row_start:row_start + block_rows], key,...]
    pallas_call x0 -> x4, Pallas kernels: none -> 40.6 us  [the longest x1 11.9 us: near_part(): pl.pallas_call(near_kernel, grid=(heads,), in_specs=[rows, rows, flat, pl...]
    ppermute x7, waiting for transfers between devices: 36.6 us -> 46.7 us  [swap(): lax.ppermute(value, axis, [(i, partner(i, axis, bit)) for i in range(size)])]
    select_n x7 -> x0, other arithmetic: 8.12 us -> none  [near_part(): chosen = jnp.where(levels == level_no, 1.0, 0.0).astype(jnp.float32)]
    unnamed x21 -> x14, local copies, waits for them, and re-layouts: 6.35 us -> 0.81 us
    reduce_sum x1 -> x0, local copies, waits for them, and re-layouts: 5.39 us -> none  [per_device(): total = near + jnp.sum(products * gains[..., None], 0)]
    reduce_sum x1 -> x0, other arithmetic: 4.76 us -> none  [per_device(): scale = lax.rsqrt(jnp.mean(total * total, -1, keepdims=True) + EPSILON)]
    convert_element_type x1 -> x0, local copies, waits for them, and re-layouts: 2.67 us -> none  [per_device(): return (total * scale).astype(jnp.bfloat16)]
  transfers between devices with their start and end apart: 7 -> 7, of which waited for: 4 -> 6; matrix products, arithmetic and copies ran while one was open for 40% -> 0% of each run, Pallas kernels for 0% -> 18%
where the time goes in v1:
time: 108 us
  waiting for transfers between devices  46.7 us (43%)
  Pallas kernels  40.6 us (38%)
  starting transfers between devices  18.1 us (17%)
  other arithmetic  1.64 us (2%)
    ppermute x7, waiting for transfers between devices, swap(): lax.ppermute(value, axis, [(i, partner(i, axis, bit)) for i in range(size)])  46.7 us
    ppermute x7, starting transfers between devices, swap(): lax.ppermute(value, axis, [(i, partner(i, axis, bit)) for i in range(size)])  18.1 us
    pallas_call x1, Pallas kernels, near_part(): pl.pallas_call(near_kernel, grid=(heads,), in_specs=[rows, rows, flat, pl...  11.9 us
    pallas_call x1, Pallas kernels, finish(): pl.pallas_call(lambda *refs: far_kernel(local_bits, *refs), grid=(length...  11 us
    pallas_call x1, Pallas kernels, states(): pl.pallas_call(state_kernel, grid=(length // rows,), in_specs=[whole, who...  10.2 us
    pallas_call x1, Pallas kernels, by_head(): pl.pallas_call(query_kernel, grid=(length // rows,), in_specs=[pl.BlockSp...  7.51 us
  transfers between devices with their start and end apart: 7, of which 6 were waited for; matrix products, arithmetic and copies ran while one was open for 0% of the time, Pallas kernels for 18%

profile of v1, /device:TPU:1, one launch (start us, length us, event | category | flops | bytes accessed | tf_op | source)
XLA Modules:
  0.0 107.9 jit_solution(1261724235199092132)
XLA Ops:
  0.0 10.2 %states.1 = (f32[8,128,128]{2,1,0:T(8,128)}, bf16[8,1024,128]{2,1,0:T(8,128)(2,1)}, bf16[8,128,1024]{2,1,0:T(8,128)(2,1)}) custom-call(bf16[1024,8,128]{2,1,0:T(8,128)(2,1)} %key_ref.1, bf16[1024,8,128]{2,1,0:T(8,128)(2,1)} %value_ref.1), custom_call_target="tpu_custom_call" | custom-call | flops 1000000000 | bytes 8388608 | tf_op jit(solution)/shard_map/states/pallas_call | solution.py:36
  10.2 2.1 %collective-permute-start = (f32[8,128,128]{2,1,0:T(8,128)}, f32[8,128,128]{2,1,0:T(8,128)S(1)}, u32[]{:S(2)}, u32[]{:S(2)}) collective-permute-start(f32[8,128,128]{2,1,0:T(8,128)} %get-tuple-element.10), channel_id=1, source_target_pairs={{0,8},{8,0},{16,24},{24,16},{32,40},{40,32},{48,56},{56,48},{64,72... | collective-permute-start | bytes 1572872 | tf_op jit(solution)/shard_map/ppermute | solution.py:203
  12.3 11.4 %collective-permute-done.refs_4_ = f32[8,128,128]{2,1,0:T(8,128)S(1)} collective-permute-done((f32[8,128,128]{2,1,0:T(8,128)}, f32[8,128,128]{2,1,0:T(8,128)S(1)}, u32[]{:S(2)}, u32[]{:S(2)}) %collective-permute-start) | collective-permute-done | bytes 524320 | tf_op jit(solution)/shard_map/ppermute | solution.py:203
  23.8 0.0 copy-start
  23.8 1.3 %add.22 = f32[8,128,128]{2,1,0:T(8,128)S(1)} add(f32[8,128,128]{2,1,0:T(8,128)} %get-tuple-element.10, f32[8,128,128]{2,1,0:T(8,128)S(1)} %collective-permute-done.refs_4_) | non-fusion elementwise | flops 131072 | bytes 1572864 | tf_op jit(solution)/shard_map/add | solution.py:218
  25.1 3.1 %collective-permute-start.1 = (f32[8,128,128]{2,1,0:T(8,128)S(1)}, f32[8,128,128]{2,1,0:T(8,128)S(1)}, u32[]{:S(2)}, u32[]{:S(2)}) collective-permute-start(f32[8,128,128]{2,1,0:T(8,128)S(1)} %add.22), channel_id=1, source_target_pairs={{0,24},{8,16},{16,8},{24,0},{32,56},{40,48},{48,40},{56,32},{64,88... | collective-permute-start | bytes 1572872 | tf_op jit(solution)/shard_map/ppermute | solution.py:203
  28.1 10.6 %collective-permute-done.1.refs_5_ = f32[8,128,128]{2,1,0:T(8,128)S(1)} collective-permute-done((f32[8,128,128]{2,1,0:T(8,128)S(1)}, f32[8,128,128]{2,1,0:T(8,128)S(1)}, u32[]{:S(2)}, u32[]{:S(2)}) %collective-permute-start.1) | collective-permute-done | bytes 524320 | tf_op jit(solution)/shard_map/ppermute | solution.py:203
  38.8 0.0 copy-start.1
  38.8 0.1 add.23
  38.9 1.6 %collective-permute-start.2 = (f32[8,128,128]{2,1,0:T(8,128)S(1)}, f32[8,128,128]{2,1,0:T(8,128)S(1)}, u32[]{:S(2)}, u32[]{:S(2)}) collective-permute-start(f32[8,128,128]{2,1,0:T(8,128)S(1)} %add.23), channel_id=1, source_target_pairs={{0,32},{8,40},{16,48},{24,56},{32,0},{40,8},{48,16},{56,24},{64,96... | collective-permute-start | bytes 1572872 | tf_op jit(solution)/shard_map/ppermute | solution.py:203
  40.4 9.7 %collective-permute-done.2.refs_6_ = f32[8,128,128]{2,1,0:T(8,128)S(1)} collective-permute-done((f32[8,128,128]{2,1,0:T(8,128)S(1)}, f32[8,128,128]{2,1,0:T(8,128)S(1)}, u32[]{:S(2)}, u32[]{:S(2)}) %collective-permute-start.2) | collective-permute-done | bytes 524320 | tf_op jit(solution)/shard_map/ppermute | solution.py:203
  50.1 0.0 copy-start.2
  50.1 0.1 add.24
  50.2 0.0 copy-done
  50.2 3.5 %collective-permute-start.3 = (f32[8,128,128]{2,1,0:T(8,128)S(1)}, f32[8,128,128]{2,1,0:T(8,128)S(1)}, u32[]{:S(2)}, u32[]{:S(2)}) collective-permute-start(f32[8,128,128]{2,1,0:T(8,128)S(1)} %add.24), channel_id=1, source_target_pairs={{0,96},{8,104},{16,112},{24,120},{32,64},{40,72},{48,80},{56,88},{... | collective-permute-start | bytes 1572872 | tf_op jit(solution)/shard_map/ppermute | solution.py:203
  53.7 8.9 %collective-permute-done.3.refs_7_ = f32[8,128,128]{2,1,0:T(8,128)S(1)} collective-permute-done((f32[8,128,128]{2,1,0:T(8,128)S(1)}, f32[8,128,128]{2,1,0:T(8,128)S(1)}, u32[]{:S(2)}, u32[]{:S(2)}) %collective-permute-start.3) | collective-permute-done | bytes 524320 | tf_op jit(solution)/shard_map/ppermute | solution.py:203
  62.6 0.0 copy-start.3
  62.6 0.1 add.25
  62.7 0.0 copy-done.1
  62.7 4.0 %collective-permute-start.4 = (f32[8,128,128]{2,1,0:T(8,128)S(1)}, f32[8,128,128]{2,1,0:T(8,128)S(1)}, u32[]{:S(2)}, u32[]{:S(2)}) collective-permute-start(f32[8,128,128]{2,1,0:T(8,128)S(1)} %add.25), channel_id=1, source_target_pairs={{0,1},{1,0},{2,3},{3,2},{4,5},{5,4},{6,7},{7,6},{8,9},{9,8},{10,11... | collective-permute-start | bytes 1572872 | tf_op jit(solution)/shard_map/ppermute | solution.py:203
  66.8 1.5 %collective-permute-done.4.refs_8_ = f32[8,128,128]{2,1,0:T(8,128)S(1)} collective-permute-done((f32[8,128,128]{2,1,0:T(8,128)S(1)}, f32[8,128,128]{2,1,0:T(8,128)S(1)}, u32[]{:S(2)}, u32[]{:S(2)}) %collective-permute-start.4) | collective-permute-done | bytes 524320 | tf_op jit(solution)/shard_map/ppermute | solution.py:203
  68.3 0.0 copy-start.4
  68.3 0.1 add.26
  68.4 0.0 copy-done.2
  68.4 1.3 %collective-permute-start.5 = (f32[8,128,128]{2,1,0:T(8,128)S(1)}, f32[8,128,128]{2,1,0:T(8,128)S(1)}, u32[]{:S(2)}, u32[]{:S(2)}) collective-permute-start(f32[8,128,128]{2,1,0:T(8,128)S(1)} %add.26), channel_id=1, source_target_pairs={{0,2},{1,3},{2,0},{3,1},{4,6},{5,7},{6,4},{7,5},{8,10},{9,11},{10,... | collective-permute-start | bytes 1572872 | tf_op jit(solution)/shard_map/ppermute | solution.py:203
  69.7 7.5 %by_head.1.query_ref.refs_1_ = bf16[8,1024,128]{2,1,0:T(8,128)(2,1)} custom-call(bf16[1024,8,128]{2,1,0:T(8,128)(2,1)} %query_ref.1), custom_call_target="tpu_custom_call" | custom-call | flops 1000000 | bytes 4194304 | tf_op jit(solution)/shard_map/by_head/pallas_call | solution.py:65
  77.2 0.0 copy-done.3
  77.2 0.0 copy-done.4
  77.2 4.4 %collective-permute-done.5.refs_9_ = f32[8,128,128]{2,1,0:T(8,128)S(1)} collective-permute-done((f32[8,128,128]{2,1,0:T(8,128)S(1)}, f32[8,128,128]{2,1,0:T(8,128)S(1)}, u32[]{:S(2)}, u32[]{:S(2)}) %collective-permute-start.5) | collective-permute-done | bytes 524320 | tf_op jit(solution)/shard_map/ppermute | solution.py:203
  81.6 0.0 copy-start.5
  81.6 0.1 add.27
  81.7 2.5 %collective-permute-start.6 = (f32[8,128,128]{2,1,0:T(8,128)S(1)}, f32[8,128,128]{2,1,0:T(8,128)S(1)}, u32[]{:S(2)}, u32[]{:S(2)}) collective-permute-start(f32[8,128,128]{2,1,0:T(8,128)S(1)} %add.27), channel_id=1, source_target_pairs={{0,6},{1,7},{2,4},{3,5},{4,2},{5,3},{6,0},{7,1},{8,14},{9,15},{10,... | collective-permute-start | bytes 1572872 | tf_op jit(solution)/shard_map/ppermute | solution.py:203
  84.2 11.9 %near.1.refs_2_ = f32[8,128,1024]{2,1,0:T(8,128)} custom-call(bf16[8,1024,128]{2,1,0:T(8,128)(2,1)} %by_head.1.query_ref.refs_1_, bf16[8,1024,128]{2,1,0:T(8,128)(2,1)} %get-tuple-element.8.key_ref, bf16[8,128,1024]{2,1,0:T(8,128)(2,1)} %get-tuple-element.9.value_ref, f32[20,8,1024]{2,1,0:T(8,128)} %bitcast.2), custom_call_target="tpu_custom_call" | custom-call | flops 8000000000 | bytes 12582912 | tf_op jit(solution)/shard_map/near/pallas_call | solution.py:127
  96.1 0.0 copy-done.5
  96.1 0.0 collective-permute-done.6.refs_10_
  96.1 0.0 copy-start.6
  96.1 0.8 copy-done.6
  96.9 11.0 %finish.1 = bf16[1024,8,128]{2,1,0:T(8,128)(2,1)} custom-call(s32[1]{0:T(128)} %bitcast.refs_0_, bf16[8,1024,128]{2,1,0:T(8,128)(2,1)} %by_head.1.query_ref.refs_1_, f32[8,128,1024]{2,1,0:T(8,128)} %near.1.refs_2_, f32[20,8,1024]{2,1,0:T(8,128)} %bitcast.3, f32[8,128,128]{2,1,0:T(8,128)} %copy-done, f32[8,128,128]{2,1,0:T(8,128)} %copy-done.1, ...), custom_call_target="tpu_custom_call" | custom-call | flops 8000000000 | bytes 12582912 | tf_op jit(solution)/shard_map/finish/pallas_call | solution.py:177
Async XLA Ops:
  10.2 13.6 %collective-permute-start = (f32[8,128,128]{2,1,0:T(8,128)}, f32[8,128,128]{2,1,0:T(8,128)S(1)}, u32[]{:S(2)}, u32[]{:S(2)}) collective-permute-start(f32[8,128,128]{2,1,0:T(8,128)} %get-tuple-element.10), channel_id=1, source_target_pairs={{0,8},{8,0},{16,24},{24,16},{32,40},{40,32},{48,56},{56,48},{64,72... | collective-permute-start | bytes 1572872 | tf_op jit(solution)/shard_map/ppermute | solution.py:203
  23.8 26.4 %copy-start = (f32[8,128,128]{2,1,0:T(8,128)}, f32[8,128,128]{2,1,0:T(8,128)S(1)}, u32[]{:S(2)}) copy-start(f32[8,128,128]{2,1,0:T(8,128)S(1)} %collective-permute-done.refs_4_) | copy-start | bytes 1572868
  25.1 13.7 %collective-permute-start.1 = (f32[8,128,128]{2,1,0:T(8,128)S(1)}, f32[8,128,128]{2,1,0:T(8,128)S(1)}, u32[]{:S(2)}, u32[]{:S(2)}) collective-permute-start(f32[8,128,128]{2,1,0:T(8,128)S(1)} %add.22), channel_id=1, source_target_pairs={{0,24},{8,16},{16,8},{24,0},{32,56},{40,48},{48,40},{56,32},{64,88... | collective-permute-start | bytes 1572872 | tf_op jit(solution)/shard_map/ppermute | solution.py:203
  38.8 23.9 %copy-start.1 = (f32[8,128,128]{2,1,0:T(8,128)}, f32[8,128,128]{2,1,0:T(8,128)S(1)}, u32[]{:S(2)}) copy-start(f32[8,128,128]{2,1,0:T(8,128)S(1)} %collective-permute-done.1.refs_5_) | copy-start | bytes 1572868
  38.9 11.3 %collective-permute-start.2 = (f32[8,128,128]{2,1,0:T(8,128)S(1)}, f32[8,128,128]{2,1,0:T(8,128)S(1)}, u32[]{:S(2)}, u32[]{:S(2)}) collective-permute-start(f32[8,128,128]{2,1,0:T(8,128)S(1)} %add.23), channel_id=1, source_target_pairs={{0,32},{8,40},{16,48},{24,56},{32,0},{40,8},{48,16},{56,24},{64,96... | collective-permute-start | bytes 1572872 | tf_op jit(solution)/shard_map/ppermute | solution.py:203
  50.1 18.2 %copy-start.2 = (f32[8,128,128]{2,1,0:T(8,128)}, f32[8,128,128]{2,1,0:T(8,128)S(1)}, u32[]{:S(2)}) copy-start(f32[8,128,128]{2,1,0:T(8,128)S(1)} %collective-permute-done.2.refs_6_) | copy-start | bytes 1572868
  50.2 12.4 %collective-permute-start.3 = (f32[8,128,128]{2,1,0:T(8,128)S(1)}, f32[8,128,128]{2,1,0:T(8,128)S(1)}, u32[]{:S(2)}, u32[]{:S(2)}) collective-permute-start(f32[8,128,128]{2,1,0:T(8,128)S(1)} %add.24), channel_id=1, source_target_pairs={{0,96},{8,104},{16,112},{24,120},{32,64},{40,72},{48,80},{56,88},{... | collective-permute-start | bytes 1572872 | tf_op jit(solution)/shard_map/ppermute | solution.py:203
  62.6 14.6 %copy-start.3 = (f32[8,128,128]{2,1,0:T(8,128)}, f32[8,128,128]{2,1,0:T(8,128)S(1)}, u32[]{:S(2)}) copy-start(f32[8,128,128]{2,1,0:T(8,128)S(1)} %collective-permute-done.3.refs_7_) | copy-start | bytes 1572868
  62.7 5.6 %collective-permute-start.4 = (f32[8,128,128]{2,1,0:T(8,128)S(1)}, f32[8,128,128]{2,1,0:T(8,128)S(1)}, u32[]{:S(2)}, u32[]{:S(2)}) collective-permute-start(f32[8,128,128]{2,1,0:T(8,128)S(1)} %add.25), channel_id=1, source_target_pairs={{0,1},{1,0},{2,3},{3,2},{4,5},{5,4},{6,7},{7,6},{8,9},{9,8},{10,11... | collective-permute-start | bytes 1572872 | tf_op jit(solution)/shard_map/ppermute | solution.py:203
  68.3 8.9 %copy-start.4 = (f32[8,128,128]{2,1,0:T(8,128)}, f32[8,128,128]{2,1,0:T(8,128)S(1)}, u32[]{:S(2)}) copy-start(f32[8,128,128]{2,1,0:T(8,128)S(1)} %collective-permute-done.4.refs_8_) | copy-start | bytes 1572868
  68.4 13.2 %collective-permute-start.5 = (f32[8,128,128]{2,1,0:T(8,128)S(1)}, f32[8,128,128]{2,1,0:T(8,128)S(1)}, u32[]{:S(2)}, u32[]{:S(2)}) collective-permute-start(f32[8,128,128]{2,1,0:T(8,128)S(1)} %add.26), channel_id=1, source_target_pairs={{0,2},{1,3},{2,0},{3,1},{4,6},{5,7},{6,4},{7,5},{8,10},{9,11},{10,... | collective-permute-start | bytes 1572872 | tf_op jit(solution)/shard_map/ppermute | solution.py:203
  81.6 14.5 %copy-start.5 = (f32[8,128,128]{2,1,0:T(8,128)}, f32[8,128,128]{2,1,0:T(8,128)S(1)}, u32[]{:S(2)}) copy-start(f32[8,128,128]{2,1,0:T(8,128)S(1)} %collective-permute-done.5.refs_9_) | copy-start | bytes 1572868
  81.7 14.4 %collective-permute-start.6 = (f32[8,128,128]{2,1,0:T(8,128)S(1)}, f32[8,128,128]{2,1,0:T(8,128)S(1)}, u32[]{:S(2)}, u32[]{:S(2)}) collective-permute-start(f32[8,128,128]{2,1,0:T(8,128)S(1)} %add.27), channel_id=1, source_target_pairs={{0,6},{1,7},{2,4},{3,5},{4,2},{5,3},{6,0},{7,1},{8,14},{9,15},{10,... | collective-permute-start | bytes 1572872 | tf_op jit(solution)/shard_map/ppermute | solution.py:203
  96.1 0.8 copy-start.6

commit v2 on v1

v2 whole, which is shorter than its diff:
```python
import functools

import jax
import jax.numpy as jnp
from jax import lax
from jax.experimental import pallas as pl
from jax.experimental.pallas import tpu as pltpu
from jax.sharding import PartitionSpec as P

EPSILON = 1e-06
MIB = 1024 * 1024
NT = (((1,), (1,)), ((), ()))
NN = (((1,), (0,)), ((), ()))
RING = 4
CORES = 2
TILE = 256


def dot(lhs, rhs, dims):
    return lax.dot_general(lhs, rhs, dims, preferred_element_type=jnp.float32)


def params(mib):
    return pltpu.CompilerParams(vmem_limit_bytes=mib * MIB)


def cost(flops, mib):
    return pl.CostEstimate(flops=int(flops), bytes_accessed=int(mib * MIB), transcendentals=0)


def state_kernel(place_ref, key_ref, value_ref, state_ref, *quarter_refs):
    step = pl.program_id(0)

    @pl.when(step == 0)
    def _():
        state_ref[...] = jnp.zeros_like(state_ref)

    keys = jnp.swapaxes(key_ref[...], 0, 1)
    values = jnp.swapaxes(value_ref[...], 0, 1)
    heads = keys.shape[0]
    for head in range(heads):
        state_ref[head] += dot(values[head].T, keys[head], NN)

    @pl.when(step == pl.num_programs(0) - 1)
    def _():
        share = heads // RING
        for apart in range(RING):
            owner = place_ref[0] ^ apart
            quarter_refs[apart][...] = state_ref[pl.ds(owner * share, share)]


def states(place, key, value, rows=512):
    length, heads, width = key.shape
    share = heads // RING
    part = pl.BlockSpec((rows, heads, width), lambda i: (i, 0, 0))
    return pl.pallas_call(
        state_kernel,
        grid=(length // rows,),
        in_specs=[pl.BlockSpec(memory_space=pltpu.SMEM), part, part],
        out_specs=[pl.BlockSpec((heads, width, width), lambda i: (0, 0, 0))]
        + [pl.BlockSpec((share, width, width), lambda i: (0, 0, 0))] * RING,
        out_shape=[jax.ShapeDtypeStruct((heads, width, width), jnp.float32)]
        + [jax.ShapeDtypeStruct((share, width, width), jnp.float32)] * RING,
        compiler_params=params(60),
        cost_estimate=cost(3e8, 5),
        name="states",
    )(place, key, value)


def layout_kernel(query_ref, key_ref, value_ref, tie_ref, query_out, key_out, value_out):
    query_out[...] = jnp.swapaxes(query_ref[...], 0, 1)
    key_out[...] = jnp.swapaxes(key_ref[...], 0, 1)
    values = jnp.swapaxes(value_ref[...], 0, 1)
    for head in range(values.shape[0]):
        value_out[head] = values[head].T


def by_head(query, key, value, tie, rows=512):
    length, heads, width = query.shape
    part = pl.BlockSpec((rows, heads, width), lambda i: (i, 0, 0))
    rowwise = pl.BlockSpec((heads, rows, width), lambda i: (0, i, 0))
    return pl.pallas_call(
        layout_kernel,
        grid=(length // rows,),
        in_specs=[part] * 3 + [pl.BlockSpec(memory_space=pl.ANY)],
        out_specs=[rowwise, rowwise, pl.BlockSpec((heads, width, rows), lambda i: (0, 0, i))],
        out_shape=[jax.ShapeDtypeStruct((heads, length, width), jnp.bfloat16)] * 2
        + [jax.ShapeDtypeStruct((heads, width, length), jnp.bfloat16)],
        compiler_params=params(32),
        cost_estimate=cost(1e6, 12),
        name="by_head",
    )(query, key, value, tie)


def near_kernel(first, query_ref, key_ref, value_ref, weight_ref, tie_ref, near_ref):
    length = query_ref.shape[1]
    head = pl.program_id(0) + first
    groups = TILE // 8
    group_r = lax.broadcasted_iota(jnp.int32, (groups, TILE), 0)
    group_t = lax.broadcasted_iota(jnp.int32, (groups, TILE), 1) >> 3
    apart = group_r ^ group_t
    later = group_t > group_r
    inner_s = lax.broadcasted_iota(jnp.int32, (8, TILE), 0)
    inner_t = lax.broadcasted_iota(jnp.int32, (8, TILE), 1) & 7
    inner = inner_s ^ inner_t
    same = (
        lax.broadcasted_iota(jnp.int32, (groups, 8, TILE), 0)
        == lax.broadcasted_iota(jnp.int32, (groups, 8, TILE), 2) >> 3
    )
    for tile in range(length // TILE):
        cols = slice(tile * TILE, (tile + 1) * TILE)

        def gain(level):
            return weight_ref[level, pl.ds(head, 1), cols]

        query = query_ref[0, cols, :]
        parts = []
        for other in range(tile):
            scores = dot(key_ref[0, other * TILE : (other + 1) * TILE, :], query, NT)
            parts.append((scores * gain(8 + (tile ^ other).bit_length())).astype(jnp.bfloat16))
        outer = gain(4)
        for level in range(5, 9):
            outer = jnp.where(apart >= 1 << (level - 4), gain(level), outer)
        outer = jnp.where(later, outer, 0.0)
        small = gain(0)
        for level in range(1, 4):
            small = jnp.where(inner >= 1 << (level - 1), gain(level), small)
        small = jnp.where(inner_s <= inner_t, small, 0.0)
        mixing = jnp.where(same, small[None], outer[:, None, :]).reshape(TILE, TILE)
        scores = dot(key_ref[0, cols, :], query, NT)
        parts.append((scores * mixing).astype(jnp.bfloat16))
        weighted = jnp.concatenate(parts, 0)
        near_ref[0, :, cols] = dot(value_ref[0, :, : (tile + 1) * TILE], weighted, NN)


def near_part(query, key, value, level_weight, tie, first, count):
    heads, length, width = query.shape
    levels = level_weight.shape[0]
    rows = pl.BlockSpec((1, length, width), lambda h: (h + first, 0, 0))
    flat = pl.BlockSpec((1, width, length), lambda h: (h + first, 0, 0))
    return pl.pallas_call(
        functools.partial(near_kernel, first),
        grid=(count,),
        in_specs=[
            rows,
            rows,
            flat,
            pl.BlockSpec((levels, heads, length), lambda h: (0, 0, 0)),
            pl.BlockSpec(memory_space=pl.ANY),
        ],
        out_specs=pl.BlockSpec((1, width, length), lambda h: (h, 0, 0)),
        out_shape=jax.ShapeDtypeStruct((count, width, length), jnp.float32),
        compiler_params=params(16),
        cost_estimate=cost(count * 5e8, count * 2),
        name="near",
    )(query, key, value, level_weight, tie)


def far_kernel(plan, last, local_bits, place_ref, query_ref, weight_ref, *rest):
    count, bits, pieces = plan
    total_refs, rest = rest[:count], rest[count:]
    piece_refs, rest = rest[: len(pieces)], rest[len(pieces) :]
    if last:
        out_ref, split, total_f = rest
    else:
        out_ref, split = rest
    heads, rows, width = query_ref.shape

    @pl.when(pl.program_id(0) == 0)
    def _():
        for ref, (piece_bits, first_head) in zip(piece_refs, pieces):
            base = first_head(place_ref)
            for at, bit in enumerate(piece_bits):
                for head in range(ref.shape[1]):
                    bucket = ref[at, head]
                    high = bucket.astype(jnp.bfloat16)
                    low = (bucket - high.astype(jnp.float32)).astype(jnp.bfloat16)
                    where = bits.index(bit) * width
                    split[base + head, where : where + width, :width] = high
                    split[base + head, where : where + width, width:] = low

    block = place_ref[3]
    share = heads // count
    for head in range(heads):
        query = query_ref[head]
        products = dot(split[head], jnp.concatenate([query, query], 1), NT)
        total = total_refs[head // share][head % share]
        for at, bit in enumerate(bits):
            gain = weight_ref[local_bits + 1 + bit, head : head + 1, :]
            gain = jnp.where((block >> bit) & 1 == 1, gain, 0.0)
            total = total + products[at * width : (at + 1) * width, :] * gain
        if last:
            mean = jnp.sum(total * total, 0, keepdims=True) * (1.0 / width)
            total = total * lax.rsqrt(mean + EPSILON)
            total_f[pl.ds(head, rows, stride=heads), :] = total.T
        else:
            out_ref[head] = total
    if last:
        out_ref[...] = total_f[...].reshape(rows, heads, width).astype(jnp.bfloat16)


def far_part(place, query, level_weight, totals, bits, pieces, last, rows=256):
    heads, length, width = query.shape
    levels = level_weight.shape[0]
    local_bits = length.bit_length() - 1
    flat = pl.BlockSpec((heads, width, rows), lambda i: (0, 0, i))
    plan = (len(totals), bits, [(piece_bits, first) for _, piece_bits, first in pieces])
    arrays = [array for array, _, _ in pieces]
    scratch = [pltpu.VMEM((heads, len(bits) * width, 2 * width), jnp.bfloat16)]
    if last:
        scratch.append(pltpu.VMEM((rows * heads, width), jnp.float32))
    return pl.pallas_call(
        functools.partial(far_kernel, plan, last, local_bits),
        grid=(length // rows,),
        in_specs=[
            pl.BlockSpec(memory_space=pltpu.SMEM),
            pl.BlockSpec((heads, rows, width), lambda i: (0, i, 0)),
            pl.BlockSpec((levels, heads, rows), lambda i: (0, 0, i)),
        ]
        + [pl.BlockSpec((t.shape[0], width, rows), lambda i: (0, 0, i)) for t in totals]
        + [pl.BlockSpec(a.shape, lambda i: (0, 0, 0, 0)) for a in arrays],
        out_specs=pl.BlockSpec((rows, heads, width), lambda i: (i, 0, 0)) if last else flat,
        out_shape=jax.ShapeDtypeStruct((length, heads, width), jnp.bfloat16)
        if last
        else jax.ShapeDtypeStruct((heads, width, length), jnp.float32),
        scratch_shapes=scratch,
        compiler_params=params(28),
        cost_estimate=cost(len(bits) * 6e8, 10),
        name="finish" if last else "far",
    )(place, query, level_weight, *totals, *arrays)


def along(value, axis, hop):
    return lax.ppermute(value, axis, [(i, hop(i)) for i in range(lax.axis_size(axis))])


def apart_y(value, by):
    return along(value, "short", lambda i: i ^ by)


def apart_z(value, by):
    return along(value, "short", lambda i: i ^ by * RING)


def apart_x(value, by):
    return along(value, "long", lambda i: i ^ by * CORES)


def other_core(value):
    return along(value, "long", lambda i: i ^ 1)


def tied(value, *others):
    return lax.optimization_barrier((value, *others))[0]


def buckets_of_ring(parts):
    return parts[1], parts[2] + parts[3]


def per_device(query, key, value, level_weight):
    level_weight = jnp.transpose(level_weight, (1, 0, 2))
    short_pos = lax.axis_index("short").astype(jnp.int32)
    long_pos = lax.axis_index("long").astype(jnp.int32)
    y, core = short_pos % RING, long_pos % CORES
    block = long_pos * lax.axis_size("short") + short_pos
    place = jnp.stack([y, core, short_pos // RING, block])

    state, *quarters = states(place, key, value)
    quarters = [quarters[0]] + [apart_y(quarters[m], m) for m in (1, 3, 2)]
    quarters = [quarters[0], quarters[1], quarters[3], quarters[2]]
    first = apart_y(state, 1)
    query_h, key_h, value_t = by_head(query, key, value, quarters[0])
    heads = query_h.shape[0]
    share = heads // RING

    def near_of(head, tie):
        return near_part(query_h, key_h, value_t, level_weight, tie, head, share)

    quarters = tied(quarters, query_h)
    ring_y = sum(quarters[1:], quarters[0])

    sums = [ring_y] + [apart_z(ring_y, m) for m in (1, 2, 3)]
    near = [near_of(0, ring_y), near_of(share, ring_y)]
    sums, pair = lax.optimization_barrier((sums, state + first, *near))[:2]
    ring_z = sum(sums[1:], sums[0])
    second = apart_y(pair, 3)
    facing = other_core(ring_z)
    near_buckets = jnp.stack(buckets_of_ring(sums))

    mine = lax.dynamic_slice_in_dim(ring_z, core, 1, 0)
    theirs = lax.dynamic_slice_in_dim(facing, core, 1, 0)
    chip = mine + theirs
    chips = [chip] + [apart_x(chip, m) for m in (1, 2, 3)]
    near.append(near_of(2 * share, chip))
    near_buckets = tied(near_buckets, chip)
    inner = [near_buckets, apart_y(near_buckets, 1), None, apart_y(near_buckets, 3)]
    chips = tied(chips, near[2])
    outer = jnp.stack([jnp.where(core == 0, mine, theirs), *buckets_of_ring(chips)])
    outer = [outer] + [apart_y(outer, m) for m in (1, 2, 3)]
    inner[2] = apart_y(inner[1], 3)
    outer_facing = [other_core(piece) for piece in outer]
    near.append(near_of(3 * share, outer[0]))

    def owner(m):
        return lambda p: (p[0] ^ m) * share

    pieces = [(first[None], (0,), lambda p: 0), (second[None], (1,), lambda p: 0)]
    pieces += [(inner[m], (2, 3), owner(m)) for m in range(RING)]
    total = far_part(place, query_h, level_weight, near, (0, 1, 2, 3), pieces, False)
    pieces = [(outer[m], (4, 5, 6), lambda p, m=m: owner(m)(p) + p[1]) for m in range(RING)]
    pieces += [
        (outer_facing[m], (4, 5, 6), lambda p, m=m: owner(m)(p) + 1 - p[1]) for m in range(RING)
    ]
    return far_part(place, query_h, level_weight, [total], (4, 5, 6), pieces, True)


def solution(mesh):
    return jax.shard_map(
        per_device,
        mesh=mesh,
        in_specs=(
            P(("long", "short"), None, None),
            P(("long", "short"), None, None),
            P(("long", "short"), None, None),
            P(None, None, ("long", "short")),
        ),
        out_specs=P(("long", "short"), None, None),
        check_vma=False,
    )
```

time: 108 us -> 80 us (0.74)
  waiting for transfers between devices: 46.7 us -> 15 us
  Pallas kernels: 40.6 us -> 25.5 us
  local copies, waits for them, and re-layouts: 0.81 us -> 9.86 us
  starting transfers between devices: 18.1 us -> 26 us
  other arithmetic: 1.64 us -> 3.09 us
    ppermute x7 -> x22, waiting for transfers between devices: 46.7 us -> 15 us  [along(): lax.ppermute(value, axis, [(i, hop(i)) for i in range(lax.axis_size(axis))])]
    pallas_call x4 -> x8, Pallas kernels: 40.6 us -> 25.5 us  [the longest x2 10.3 us: far_part(): pl.pallas_call(functools.partial(far_kernel, plan, last, local_bits), gri...]
    unnamed x14 -> x30, local copies, waits for them, and re-layouts: 0.81 us -> 9.86 us
    ppermute x7 -> x22, starting transfers between devices: 18.1 us -> 26 us  [along(): lax.ppermute(value, axis, [(i, hop(i)) for i in range(lax.axis_size(axis))])]
    another operation x0 -> x6, other arithmetic: none -> 2.21 us  [the longest x3 0.91 us: per_device(): jnp.stack([jnp.where(core == 0, mine, theirs), *buckets_of_ring(chips)])]
  transfers between devices with their start and end apart: 7 -> 22, of which waited for: 6 -> 3; matrix products, arithmetic and copies ran while one was open for 0% -> 2% of each run, Pallas kernels for 18% -> 20%
where the time goes in v2:
time: 80 us; the launch traced here: 79.7 us
  starting transfers between devices  26 us (32%)
  Pallas kernels  25.5 us (32%)
  waiting for transfers between devices  15 us (19%)
  local copies, waits for them, and re-layouts  9.86 us (12%)
  other arithmetic  3.09 us (4%)
    ppermute x22, starting transfers between devices, along(): lax.ppermute(value, axis, [(i, hop(i)) for i in range(lax.axis_size(axis))])  26 us
    ppermute x22, waiting for transfers between devices, along(): lax.ppermute(value, axis, [(i, hop(i)) for i in range(lax.axis_size(axis))])  15 us
    pallas_call x2, Pallas kernels, far_part(): pl.pallas_call(functools.partial(far_kernel, plan, last, local_bits), gri...  10.3 us
    unnamed x30, local copies, waits for them, and re-layouts  9.86 us
    pallas_call x4, Pallas kernels, near_part(): pl.pallas_call(functools.partial(near_kernel, first), grid=(count,), in_s...  9.02 us
    pallas_call x1, Pallas kernels, states(): pl.pallas_call(state_kernel, grid=(length // rows,), in_specs=[pl.BlockSp...  3.83 us
    pallas_call x1, Pallas kernels, by_head(): pl.pallas_call(layout_kernel, grid=(length // rows,), in_specs=[part] * 3...  2.3 us
  transfers between devices with their start and end apart: 22, of which 3 were waited for; matrix products, arithmetic and copies ran while one was open for 2% of the time, Pallas kernels for 20%

profile of v2, /device:TPU:1, one launch (start us, length us, event | category | flops | bytes accessed | tf_op | source)
XLA Modules:
  0.0 79.7 jit_solution(9405982219232102182)
XLA Ops:
  0.0 0.6 pad_add_fusion.place_ref
  0.6 3.8 %states.1 = (f32[8,128,128]{2,1,0:T(8,128)}, f32[2,128,128]{2,1,0:T(8,128)}, f32[2,128,128]{2,1,0:T(8,128)}, f32[2,128,128]{2,1,0:T(8,128)}, f32[2,128,128]{2,1,0:T(8,128)}) custom-call(s32[4]{0:T(128)} %pad_add_fusion.place_ref, bf16[1024,8,128]{2,1,0:T(8,128)(2,1)} %key_ref.3, bf16[1024,8,128]{2,1,0:T(8,128)(2,1)} %value_ref.3), custom_call_target="tpu_custom_call" | custom-call | flops 300000000 | bytes 5242880 | tf_op jit(solution)/shard_map/states/pallas_call | solution.py:56
  4.4 2.1 %collective-permute-start = (f32[2,128,128]{2,1,0:T(8,128)}, f32[2,128,128]{2,1,0:T(8,128)S(1)}, u32[]{:S(2)}, u32[]{:S(2)}) collective-permute-start(f32[2,128,128]{2,1,0:T(8,128)} %get-tuple-element.30), channel_id=1, source_target_pairs={{0,8},{8,0},{16,24},{24,16},{32,40},{40,32},{48,56},{56,48},{64,72... | collective-permute-start | bytes 393224 | tf_op jit(solution)/shard_map/ppermute | solution.py:234
  6.5 2.6 %collective-permute-start.1 = (f32[2,128,128]{2,1,0:T(8,128)}, f32[2,128,128]{2,1,0:T(8,128)S(1)}, u32[]{:S(2)}, u32[]{:S(2)}) collective-permute-start(f32[2,128,128]{2,1,0:T(8,128)} %get-tuple-element.31), channel_id=1, source_target_pairs={{0,16},{8,24},{16,0},{24,8},{32,48},{40,56},{48,32},{56,40},{64,80... | collective-permute-start | bytes 393224 | tf_op jit(solution)/shard_map/ppermute | solution.py:234
  9.2 0.0 collective-permute-start.2
  9.2 0.0 collective-permute-start.6
  9.2 1.6 %copy-done.5 = bf16[1024,8,128]{2,1,0:T(8,128)(2,1)S(1)} copy-done((bf16[1024,8,128]{2,1,0:T(8,128)(2,1)S(1)}, bf16[1024,8,128]{2,1,0:T(8,128)(2,1)}, u32[]{:S(2)}) %copy-start.5) | copy-done | bytes 2097176
  10.8 1.6 %copy-done.6 = bf16[1024,8,128]{2,1,0:T(8,128)(2,1)S(1)} copy-done((bf16[1024,8,128]{2,1,0:T(8,128)(2,1)S(1)}, bf16[1024,8,128]{2,1,0:T(8,128)(2,1)}, u32[]{:S(2)}) %copy-start.6) | copy-done | bytes 2097176
  12.4 1.6 %copy-done.11 = bf16[1024,8,128]{2,1,0:T(8,128)(2,1)S(1)} copy-done((bf16[1024,8,128]{2,1,0:T(8,128)(2,1)S(1)}, bf16[1024,8,128]{2,1,0:T(8,128)(2,1)}, u32[]{:S(2)}) %copy-start.11) | copy-done | bytes 2097176
  14.0 0.9 %copy-done.12 = f32[2,128,128]{2,1,0:T(8,128)S(1)} copy-done((f32[2,128,128]{2,1,0:T(8,128)S(1)}, f32[2,128,128]{2,1,0:T(8,128)}, u32[]{:S(2)}) %copy-start.12) | copy-done | bytes 131096
  14.9 2.3 %by_head.1 = (bf16[8,1024,128]{2,1,0:T(8,128)(2,1)S(1)}, bf16[8,1024,128]{2,1,0:T(8,128)(2,1)S(1)}, bf16[8,128,1024]{2,1,0:T(8,128)(2,1)S(1)}) custom-call(bf16[1024,8,128]{2,1,0:T(8,128)(2,1)S(1)} %copy-done.11, bf16[1024,8,128]{2,1,0:T(8,128)(2,1)S(1)} %copy-done.5, bf16[1024,8,128]{2,1,0:T(8,128)(2,1)S(1)} %copy-done.6, f32[2,128,128]{2,1,0:T(8,128)S(1)} %copy-done.12), custom_call_target="tpu_custom_call" | custom-call | flops 1000000 | bytes 12582912 | tf_op jit(solution)/shard_map/by_head/pallas_call | solution.py:82
  17.2 0.0 copy-start
  17.2 0.0 collective-permute-done
  17.2 0.0 collective-permute-done.1
  17.2 0.4 collective-permute-done.2
  17.6 3.8 %collective-permute-start.5 = (f32[2,128,128]{2,1,0:T(8,128)S(1)}, f32[2,128,128]{2,1,0:T(8,128)S(1)}, u32[]{:S(2)}, u32[]{:S(2)}) collective-permute-start(f32[2,128,128]{2,1,0:T(8,128)S(1)} %add_add_fusion.1.tie_ref), channel_id=1, source_target_pairs={{0,96},{8,104},{16,112},{24,120},{32,64},{40,72},{48,80},{56,88},{... | collective-permute-start | bytes 393224 | tf_op jit(solution)/shard_map/ppermute | solution.py:234
  21.5 0.0 collective-permute-start.4
  21.5 0.7 collective-permute-start.3
  22.1 2.2 %near.5.rest_1_ = f32[2,128,1024]{2,1,0:T(8,128)S(1)} custom-call(bf16[8,1024,128]{2,1,0:T(8,128)(2,1)S(1)} %get-tuple-element.27.query_ref, bf16[8,1024,128]{2,1,0:T(8,128)(2,1)S(1)} %get-tuple-element.28.key_ref, bf16[8,128,1024]{2,1,0:T(8,128)(2,1)S(1)} %get-tuple-element.29.value_ref, f32[20,8,1024]{2,1,0:T(8,128)S(1)} %bitcast.15, ...), custom_call_target="tpu_custom_call" | custom-call | flops 1000000000 | bytes 4194304 | tf_op jit(solution)/shard_map/near/pallas_call | solution.py:141
  24.4 2.3 %near.4.rest_0_ = f32[2,128,1024]{2,1,0:T(8,128)S(1)} custom-call(bf16[8,1024,128]{2,1,0:T(8,128)(2,1)S(1)} %get-tuple-element.27.query_ref, bf16[8,1024,128]{2,1,0:T(8,128)(2,1)S(1)} %get-tuple-element.28.key_ref, bf16[8,128,1024]{2,1,0:T(8,128)(2,1)S(1)} %get-tuple-element.29.value_ref, f32[20,8,1024]{2,1,0:T(8,128)S(1)} %bitcast.16, ...), custom_call_target="tpu_custom_call" | custom-call | flops 1000000000 | bytes 4194304 | tf_op jit(solution)/shard_map/near/pallas_call | solution.py:141
  26.7 1.0 %copy-done.9 = f32[2,128,1024]{2,1,0:T(8,128)} copy-done((f32[2,128,1024]{2,1,0:T(8,128)}, f32[2,128,1024]{2,1,0:T(8,128)S(1)}, u32[]{:S(2)}) %copy-start.9) | copy-done | bytes 1048600
  27.7 0.0 collective-permute-done.6
  27.7 0.9 %add.51 = f32[8,128,128]{2,1,0:T(8,128)} add(f32[8,128,128]{2,1,0:T(8,128)S(1)} %copy-done.14, f32[8,128,128]{2,1,0:T(8,128)S(1)} %collective-permute-done.6) | non-fusion elementwise | flops 131072 | bytes 1572864 | tf_op jit(solution)/shard_map/add | solution.py:285
  28.5 0.0 collective-permute-done.5
  28.5 0.0 collective-permute-done.4
  28.5 0.0 collective-permute-done.3
  28.6 0.7 add_bitcast_fusion
  29.3 2.0 %collective-permute-start.7 = (f32[2,128,128]{2,1,0:T(8,128)}, f32[2,128,128]{2,1,0:T(8,128)}, u32[]{:S(2)}, u32[]{:S(2)}) collective-permute-start(f32[2,128,128]{2,1,0:T(8,128)} %get-tuple-element.48), channel_id=1, source_target_pairs={{0,1},{1,0},{2,3},{3,2},{4,5},{5,4},{6,7},{7,6},{8,9},{9,8},{10,11... | collective-permute-start | bytes 393224 | tf_op jit(solution)/shard_map/ppermute | solution.py:234
  31.3 2.4 %collective-permute-start.11 = (f32[8,128,128]{2,1,0:T(8,128)}, f32[8,128,128]{2,1,0:T(8,128)S(1)}, u32[]{:S(2)}, u32[]{:S(2)}) collective-permute-start(f32[8,128,128]{2,1,0:T(8,128)} %add.51), channel_id=1, source_target_pairs={{0,24},{8,16},{16,8},{24,0},{32,56},{40,48},{48,40},{56,32},{64,88... | collective-permute-start | bytes 1572872 | tf_op jit(solution)/shard_map/ppermute | solution.py:234
  33.6 0.0 collective-permute-done.7
  33.7 0.9 %select_bitcast_fusion = (f32[1,1,128,128]{3,2,1,0:T(8,128)S(1)}, f32[1,128,128]{2,1,0:T(8,128)S(1)}) fusion(f32[2,128,128]{2,1,0:T(8,128)} %collective-permute-done.7, s32[]{:T(128)S(6)} %select_n.30, f32[2,128,128]{2,1,0:T(8,128)} %get-tuple-element.48, pred[]{:T(512)S(6)} %eq.6), kind=kLoop, calls=%fused_computation.6 | loop fusion | flops 32768 | bytes 262149 | tf_op jit(solution)/shard_map/stack | solution.py:299
  34.6 2.6 %collective-permute-start.10 = (f32[1,128,128]{2,1,0:T(8,128)S(1)}, f32[1,128,128]{2,1,0:T(8,128)S(1)}, u32[]{:S(2)}, u32[]{:S(2)}) collective-permute-start(f32[1,128,128]{2,1,0:T(8,128)S(1)} %get-tuple-element.50.tie_ref), channel_id=1, source_target_pairs={{0,6},{1,7},{2,4},{3,5},{4,2},{5,3},{6,0},{7,1},{8,14},{9,15},{10,... | collective-permute-start | bytes 196616 | tf_op jit(solution)/shard_map/ppermute | solution.py:234
  37.1 0.5 collective-permute-start.9
  37.6 0.2 collective-permute-start.8
  37.9 1.1 %collective-permute-start.12 = (f32[2,2,128,128]{3,2,1,0:T(8,128)S(1)}, f32[2,2,128,128]{3,2,1,0:T(8,128)S(1)}, u32[]{:S(2)}, u32[]{:S(2)}) collective-permute-start(f32[2,2,128,128]{3,2,1,0:T(8,128)S(1)} %pad_maximum_fusion.rest_6_), channel_id=1, source_target_pairs={{0,8},{8,0},{16,24},{24,16},{32,40},{40,32},{48,56},{56,48},{64,72... | collective-permute-start | bytes 786440 | tf_op jit(solution)/shard_map/ppermute | solution.py:234
  39.0 1.6 %copy-done.1 = bf16[8,1024,128]{2,1,0:T(8,128)(2,1)S(1)} copy-done((bf16[8,1024,128]{2,1,0:T(8,128)(2,1)S(1)}, bf16[8,1024,128]{2,1,0:T(8,128)(2,1)}, u32[]{:S(2)}) %copy-start.1) | copy-done | bytes 2097176
  40.6 1.6 %copy-done.3 = bf16[8,128,1024]{2,1,0:T(8,128)(2,1)S(1)} copy-done((bf16[8,128,1024]{2,1,0:T(8,128)(2,1)S(1)}, bf16[8,128,1024]{2,1,0:T(8,128)(2,1)}, u32[]{:S(2)}) %copy-start.3) | copy-done | bytes 2097176
  42.2 2.3 %near.6.rest_2_ = f32[2,128,1024]{2,1,0:T(8,128)S(1)} custom-call(bf16[8,1024,128]{2,1,0:T(8,128)(2,1)S(1)} %get-tuple-element.27.query_ref, bf16[8,1024,128]{2,1,0:T(8,128)(2,1)S(1)} %copy-done.1, bf16[8,128,1024]{2,1,0:T(8,128)(2,1)S(1)} %copy-done.3, f32[20,8,1024]{2,1,0:T(8,128)S(1)} %bitcast.17, f32[1,128,128]{2,1,0:T(8,128)S(1)} %get-tuple-element.50.tie_ref), custom_call_target="tpu_custom_call" | custom-call | flops 1000000000 | bytes 4194304 | tf_op jit(solution)/shard_map/near/pallas_call | solution.py:141
  44.5 0.0 collective-permute-done.10
  44.5 2.0 %collective-permute-start.14 = (f32[2,2,128,128]{3,2,1,0:T(8,128)S(1)}, f32[2,2,128,128]{3,2,1,0:T(8,128)S(1)}, u32[]{:S(2)}, u32[]{:S(2)}) collective-permute-start(f32[2,2,128,128]{3,2,1,0:T(8,128)S(1)} %pad_maximum_fusion.rest_6_), channel_id=1, source_target_pairs={{0,24},{8,16},{16,8},{24,0},{32,56},{40,48},{48,40},{56,32},{64,88... | collective-permute-start | bytes 786440 | tf_op jit(solution)/shard_map/ppermute | solution.py:234
  46.5 0.0 collective-permute-done.9
  46.5 0.0 collective-permute-done.8
  46.5 0.0 collective-permute-done.12.rest_7_
  46.5 0.9 %collective-permute-start.13 = (f32[2,2,128,128]{3,2,1,0:T(8,128)S(1)}, f32[2,2,128,128]{3,2,1,0:T(8,128)S(1)}, u32[]{:S(2)}, u32[]{:S(2)}) collective-permute-start(f32[2,2,128,128]{3,2,1,0:T(8,128)S(1)} %collective-permute-done.12.rest_7_), channel_id=1, source_target_pairs={{0,24},{8,16},{16,8},{24,0},{32,56},{40,48},{48,40},{56,32},{64,88... | collective-permute-start | bytes 786440 | tf_op jit(solution)/shard_map/ppermute | solution.py:234
  47.4 2.0 %collective-permute-start.17 = (f32[3,1,128,128]{3,2,1,0:T(8,128)S(1)}, f32[3,1,128,128]{3,2,1,0:T(8,128)S(1)}, u32[]{:S(2)}, u32[]{:S(2)}) collective-permute-start(f32[3,1,128,128]{3,2,1,0:T(8,128)S(1)} %pad_maximum_fusion.1.tie_ref.rest_1_), channel_id=1, source_target_pairs={{0,24},{8,16},{16,8},{24,0},{32,56},{40,48},{48,40},{56,32},{64,88... | collective-permute-start | bytes 589832 | tf_op jit(solution)/shard_map/ppermute | solution.py:234
  49.4 0.0 collective-permute-start.16
  49.4 2.8 %collective-permute-done.14.rest_9_ = f32[2,2,128,128]{3,2,1,0:T(8,128)S(1)} collective-permute-done((f32[2,2,128,128]{3,2,1,0:T(8,128)S(1)}, f32[2,2,128,128]{3,2,1,0:T(8,128)S(1)}, u32[]{:S(2)}, u32[]{:S(2)}) %collective-permute-start.14) | collective-permute-done | bytes 262176 | tf_op jit(solution)/shard_map/ppermute | solution.py:234
  52.2 0.0 collective-permute-start.15
  52.2 2.2 %near.7.rest_3_ = f32[2,128,1024]{2,1,0:T(8,128)S(1)} custom-call(bf16[8,1024,128]{2,1,0:T(8,128)(2,1)S(1)} %get-tuple-element.27.query_ref, bf16[8,1024,128]{2,1,0:T(8,128)(2,1)S(1)} %copy-done.1, bf16[8,128,1024]{2,1,0:T(8,128)(2,1)S(1)} %copy-done.3, f32[20,8,1024]{2,1,0:T(8,128)S(1)} %bitcast.18, f32[3,1,128,128]{3,2,1,0:T(8,128)S(1)} %pad_maximum_fusion.1.tie_ref.rest_1_), custom_call_target="tpu_custom_call" | custom-call | flops 1000000000 | bytes 4194304 | tf_op jit(solution)/shard_map/near/pallas_call | solution.py:141
  54.4 11.8 %collective-permute-done.17.rest_4_ = f32[3,1,128,128]{3,2,1,0:T(8,128)S(1)} collective-permute-done((f32[3,1,128,128]{3,2,1,0:T(8,128)S(1)}, f32[3,1,128,128]{3,2,1,0:T(8,128)S(1)}, u32[]{:S(2)}, u32[]{:S(2)}) %collective-permute-start.17) | collective-permute-done | bytes 196640 | tf_op jit(solution)/shard_map/ppermute | solution.py:234
  66.2 2.3 %collective-permute-start.18 = (f32[3,1,128,128]{3,2,1,0:T(8,128)S(1)}, f32[3,1,128,128]{3,2,1,0:T(8,128)S(1)}, u32[]{:S(2)}, u32[]{:S(2)}) collective-permute-start(f32[3,1,128,128]{3,2,1,0:T(8,128)S(1)} %pad_maximum_fusion.1.tie_ref.rest_1_), channel_id=1, source_target_pairs={{0,1},{1,0},{2,3},{3,2},{4,5},{5,4},{6,7},{7,6},{8,9},{9,8},{10,11... | collective-permute-start | bytes 589832 | tf_op jit(solution)/shard_map/ppermute | solution.py:234
  68.5 0.0 collective-permute-done.16.rest_3_
  68.5 0.0 collective-permute-start.21
  68.5 0.0 collective-permute-done.15.rest_2_
  68.5 0.5 collective-permute-start.20
  69.1 0.0 collective-permute-done.11
  69.1 0.3 collective-permute-start.19
  69.3 0.0 collective-permute-done.13.rest_8_
  69.3 4.7 %far.1.rest_0_ = f32[8,128,1024]{2,1,0:T(8,128)S(1)} custom-call(s32[4]{0:T(128)S(1)} %copy-done.13, bf16[8,1024,128]{2,1,0:T(8,128)(2,1)S(1)} %get-tuple-element.27.query_ref, f32[20,8,1024]{2,1,0:T(8,128)S(1)} %bitcast.19, f32[2,128,1024]{2,1,0:T(8,128)S(1)} %copy-done.10, f32[2,128,1024]{2,1,0:T(8,128)S(1)} %copy-done.8, ...), custom_call_target="tpu_custom_call" | custom-call | flops 2400000000 | bytes 10485760 | tf_op jit(solution)/shard_map/far/pallas_call | solution.py:212
  74.1 0.0 collective-permute-done.18.rest_5_
  74.1 0.0 collective-permute-done.21.rest_8_
  74.1 0.0 collective-permute-done.20.rest_7_
  74.1 0.0 collective-permute-done.19.rest_6_
  74.1 5.6 %finish.1 = bf16[1024,8,128]{2,1,0:T(8,128)(2,1)} custom-call(s32[4]{0:T(128)S(1)} %copy-done.13, bf16[8,1024,128]{2,1,0:T(8,128)(2,1)S(1)} %get-tuple-element.27.query_ref, f32[20,8,1024]{2,1,0:T(8,128)S(1)} %bitcast.20, f32[8,128,1024]{2,1,0:T(8,128)S(1)} %far.1.rest_0_, f32[3,1,128,128]{3,2,1,0:T(8,128)S(1)} %pad_maximum_fusion.1.tie_ref.rest_1_, ...), custom_call_target="tpu_custom_call" | custom-call | flops 1800000000 | bytes 10485760 | tf_op jit(solution)/shard_map/finish/pallas_call | solution.py:212
  (26 shorter events, 0.1 us)
Async XLA Ops:
  4.4 12.8 %collective-permute-start = (f32[2,128,128]{2,1,0:T(8,128)}, f32[2,128,128]{2,1,0:T(8,128)S(1)}, u32[]{:S(2)}, u32[]{:S(2)}) collective-permute-start(f32[2,128,128]{2,1,0:T(8,128)} %get-tuple-element.30), channel_id=1, source_target_pairs={{0,8},{8,0},{16,24},{24,16},{32,40},{40,32},{48,56},{56,48},{64,72... | collective-permute-start | bytes 393224 | tf_op jit(solution)/shard_map/ppermute | solution.py:234
  6.5 10.7 %collective-permute-start.1 = (f32[2,128,128]{2,1,0:T(8,128)}, f32[2,128,128]{2,1,0:T(8,128)S(1)}, u32[]{:S(2)}, u32[]{:S(2)}) collective-permute-start(f32[2,128,128]{2,1,0:T(8,128)} %get-tuple-element.31), channel_id=1, source_target_pairs={{0,16},{8,24},{16,0},{24,8},{32,48},{40,56},{48,32},{56,40},{64,80... | collective-permute-start | bytes 393224 | tf_op jit(solution)/shard_map/ppermute | solution.py:234
  9.2 8.4 %collective-permute-start.2 = (f32[2,128,128]{2,1,0:T(8,128)}, f32[2,128,128]{2,1,0:T(8,128)S(1)}, u32[]{:S(2)}, u32[]{:S(2)}) collective-permute-start(f32[2,128,128]{2,1,0:T(8,128)} %get-tuple-element.32), channel_id=1, source_target_pairs={{0,24},{8,16},{16,8},{24,0},{32,56},{40,48},{48,40},{56,32},{64,88... | collective-permute-start | bytes 393224 | tf_op jit(solution)/shard_map/ppermute | solution.py:234
  9.2 18.5 %collective-permute-start.6 = (f32[8,128,128]{2,1,0:T(8,128)}, f32[8,128,128]{2,1,0:T(8,128)S(1)}, u32[]{:S(2)}, u32[]{:S(2)}) collective-permute-start(f32[8,128,128]{2,1,0:T(8,128)} %get-tuple-element.37), channel_id=1, source_target_pairs={{0,8},{8,0},{16,24},{24,16},{32,40},{40,32},{48,56},{56,48},{64,72... | collective-permute-start | bytes 1572872 | tf_op jit(solution)/shard_map/ppermute | solution.py:234
  9.2 1.6 %copy-start.5 = (bf16[1024,8,128]{2,1,0:T(8,128)(2,1)S(1)}, bf16[1024,8,128]{2,1,0:T(8,128)(2,1)}, u32[]{:S(2)}) copy-start(bf16[1024,8,128]{2,1,0:T(8,128)(2,1)} %key_ref.3) | copy-start | bytes 6291460
  10.8 1.6 %copy-start.6 = (bf16[1024,8,128]{2,1,0:T(8,128)(2,1)S(1)}, bf16[1024,8,128]{2,1,0:T(8,128)(2,1)}, u32[]{:S(2)}) copy-start(bf16[1024,8,128]{2,1,0:T(8,128)(2,1)} %value_ref.3) | copy-start | bytes 6291460
  12.4 1.6 %copy-start.11 = (bf16[1024,8,128]{2,1,0:T(8,128)(2,1)S(1)}, bf16[1024,8,128]{2,1,0:T(8,128)(2,1)}, u32[]{:S(2)}) copy-start(bf16[1024,8,128]{2,1,0:T(8,128)(2,1)} %query_ref.1) | copy-start | bytes 6291460
  14.0 0.9 %copy-start.12 = (f32[2,128,128]{2,1,0:T(8,128)S(1)}, f32[2,128,128]{2,1,0:T(8,128)}, u32[]{:S(2)}) copy-start(f32[2,128,128]{2,1,0:T(8,128)} %get-tuple-element.33.tie_ref) | copy-start | bytes 393220
  14.9 7.3 %copy-start.4 = (f32[8,20,1024]{2,0,1:T(8,128)S(1)}, f32[8,20,1024]{2,0,1:T(8,128)}, u32[]{:S(2)}) copy-start(f32[8,20,1024]{2,0,1:T(8,128)} %param.7) | copy-start | bytes 1966084
  17.2 7.2 %copy-start = (bf16[8,1024,128]{2,1,0:T(8,128)(2,1)}, bf16[8,1024,128]{2,1,0:T(8,128)(2,1)S(1)}, u32[]{:S(2)}) copy-start(bf16[8,1024,128]{2,1,0:T(8,128)(2,1)S(1)} %get-tuple-element.28.key_ref) | copy-start | bytes 6291460
  17.2 7.2 %copy-start.2 = (bf16[8,128,1024]{2,1,0:T(8,128)(2,1)}, bf16[8,128,1024]{2,1,0:T(8,128)(2,1)S(1)}, u32[]{:S(2)}) copy-start(bf16[8,128,1024]{2,1,0:T(8,128)(2,1)S(1)} %get-tuple-element.29.value_ref) | copy-start | bytes 6291460
  17.6 10.9 %collective-permute-start.5 = (f32[2,128,128]{2,1,0:T(8,128)S(1)}, f32[2,128,128]{2,1,0:T(8,128)S(1)}, u32[]{:S(2)}, u32[]{:S(2)}) collective-permute-start(f32[2,128,128]{2,1,0:T(8,128)S(1)} %add_add_fusion.1.tie_ref), channel_id=1, source_target_pairs={{0,96},{8,104},{16,112},{24,120},{32,64},{40,72},{48,80},{56,88},{... | collective-permute-start | bytes 393224 | tf_op jit(solution)/shard_map/ppermute | solution.py:234
  21.5 7.1 %collective-permute-start.4 = (f32[2,128,128]{2,1,0:T(8,128)S(1)}, f32[2,128,128]{2,1,0:T(8,128)S(1)}, u32[]{:S(2)}, u32[]{:S(2)}) collective-permute-start(f32[2,128,128]{2,1,0:T(8,128)S(1)} %add_add_fusion.1.tie_ref), channel_id=1, source_target_pairs={{0,64},{8,72},{16,80},{24,88},{32,96},{40,104},{48,112},{56,120},{... | collective-permute-start | bytes 393224 | tf_op jit(solution)/shard_map/ppermute | solution.py:234
  21.5 7.1 %collective-permute-start.3 = (f32[2,128,128]{2,1,0:T(8,128)S(1)}, f32[2,128,128]{2,1,0:T(8,128)S(1)}, u32[]{:S(2)}, u32[]{:S(2)}) collective-permute-start(f32[2,128,128]{2,1,0:T(8,128)S(1)} %add_add_fusion.1.tie_ref), channel_id=1, source_target_pairs={{0,32},{8,40},{16,48},{24,56},{32,0},{40,8},{48,16},{56,24},{64,96... | collective-permute-start | bytes 393224 | tf_op jit(solution)/shard_map/ppermute | solution.py:234
  24.4 2.3 %copy-start.7 = (f32[2,128,1024]{2,1,0:T(8,128)}, f32[2,128,1024]{2,1,0:T(8,128)S(1)}, u32[]{:S(2)}) copy-start(f32[2,128,1024]{2,1,0:T(8,128)S(1)} %near.5.rest_1_) | copy-start | bytes 3145732
  24.4 3.3 %copy-start.14 = (f32[8,128,128]{2,1,0:T(8,128)S(1)}, f32[8,128,128]{2,1,0:T(8,128)}, u32[]{:S(2)}) copy-start(f32[8,128,128]{2,1,0:T(8,128)} %get-tuple-element.37) | copy-start | bytes 1572868
  26.7 1.0 %copy-start.9 = (f32[2,128,1024]{2,1,0:T(8,128)}, f32[2,128,1024]{2,1,0:T(8,128)S(1)}, u32[]{:S(2)}) copy-start(f32[2,128,1024]{2,1,0:T(8,128)S(1)} %near.4.rest_0_) | copy-start | bytes 3145732
  29.3 4.4 %collective-permute-start.7 = (f32[2,128,128]{2,1,0:T(8,128)}, f32[2,128,128]{2,1,0:T(8,128)}, u32[]{:S(2)}, u32[]{:S(2)}) collective-permute-start(f32[2,128,128]{2,1,0:T(8,128)} %get-tuple-element.48), channel_id=1, source_target_pairs={{0,1},{1,0},{2,3},{3,2},{4,5},{5,4},{6,7},{7,6},{8,9},{9,8},{10,11... | collective-permute-start | bytes 393224 | tf_op jit(solution)/shard_map/ppermute | solution.py:234
  31.3 37.8 %collective-permute-start.11 = (f32[8,128,128]{2,1,0:T(8,128)}, f32[8,128,128]{2,1,0:T(8,128)S(1)}, u32[]{:S(2)}, u32[]{:S(2)}) collective-permute-start(f32[8,128,128]{2,1,0:T(8,128)} %add.51), channel_id=1, source_target_pairs={{0,24},{8,16},{16,8},{24,0},{32,56},{40,48},{48,40},{56,32},{64,88... | collective-permute-start | bytes 1572872 | tf_op jit(solution)/shard_map/ppermute | solution.py:234
  34.6 9.9 %collective-permute-start.10 = (f32[1,128,128]{2,1,0:T(8,128)S(1)}, f32[1,128,128]{2,1,0:T(8,128)S(1)}, u32[]{:S(2)}, u32[]{:S(2)}) collective-permute-start(f32[1,128,128]{2,1,0:T(8,128)S(1)} %get-tuple-element.50.tie_ref), channel_id=1, source_target_pairs={{0,6},{1,7},{2,4},{3,5},{4,2},{5,3},{6,0},{7,1},{8,14},{9,15},{10,... | collective-permute-start | bytes 196616 | tf_op jit(solution)/shard_map/ppermute | solution.py:234
  37.1 9.3 %collective-permute-start.9 = (f32[1,128,128]{2,1,0:T(8,128)S(1)}, f32[1,128,128]{2,1,0:T(8,128)S(1)}, u32[]{:S(2)}, u32[]{:S(2)}) collective-permute-start(f32[1,128,128]{2,1,0:T(8,128)S(1)} %get-tuple-element.50.tie_ref), channel_id=1, source_target_pairs={{0,4},{1,5},{2,6},{3,7},{4,0},{5,1},{6,2},{7,3},{8,12},{9,13},{10,... | collective-permute-start | bytes 196616 | tf_op jit(solution)/shard_map/ppermute | solution.py:234
  37.6 8.8 %collective-permute-start.8 = (f32[1,128,128]{2,1,0:T(8,128)S(1)}, f32[1,128,128]{2,1,0:T(8,128)S(1)}, u32[]{:S(2)}, u32[]{:S(2)}) collective-permute-start(f32[1,128,128]{2,1,0:T(8,128)S(1)} %get-tuple-element.50.tie_ref), channel_id=1, source_target_pairs={{0,2},{1,3},{2,0},{3,1},{4,6},{5,7},{6,4},{7,5},{8,10},{9,11},{10,... | collective-permute-start | bytes 196616 | tf_op jit(solution)/shard_map/ppermute | solution.py:234
  37.9 8.6 %collective-permute-start.12 = (f32[2,2,128,128]{3,2,1,0:T(8,128)S(1)}, f32[2,2,128,128]{3,2,1,0:T(8,128)S(1)}, u32[]{:S(2)}, u32[]{:S(2)}) collective-permute-start(f32[2,2,128,128]{3,2,1,0:T(8,128)S(1)} %pad_maximum_fusion.rest_6_), channel_id=1, source_target_pairs={{0,8},{8,0},{16,24},{24,16},{32,40},{40,32},{48,56},{56,48},{64,72... | collective-permute-start | bytes 786440 | tf_op jit(solution)/shard_map/ppermute | solution.py:234
  39.0 1.6 %copy-start.1 = (bf16[8,1024,128]{2,1,0:T(8,128)(2,1)S(1)}, bf16[8,1024,128]{2,1,0:T(8,128)(2,1)}, u32[]{:S(2)}) copy-start(bf16[8,1024,128]{2,1,0:T(8,128)(2,1)} %copy-done) | copy-start | bytes 6291460
  40.6 1.6 %copy-start.3 = (bf16[8,128,1024]{2,1,0:T(8,128)(2,1)S(1)}, bf16[8,128,1024]{2,1,0:T(8,128)(2,1)}, u32[]{:S(2)}) copy-start(bf16[8,128,1024]{2,1,0:T(8,128)(2,1)} %copy-done.2) | copy-start | bytes 6291460
  44.5 7.7 %collective-permute-start.14 = (f32[2,2,128,128]{3,2,1,0:T(8,128)S(1)}, f32[2,2,128,128]{3,2,1,0:T(8,128)S(1)}, u32[]{:S(2)}, u32[]{:S(2)}) collective-permute-start(f32[2,2,128,128]{3,2,1,0:T(8,128)S(1)} %pad_maximum_fusion.rest_6_), channel_id=1, source_target_pairs={{0,24},{8,16},{16,8},{24,0},{32,56},{40,48},{48,40},{56,32},{64,88... | collective-permute-start | bytes 786440 | tf_op jit(solution)/shard_map/ppermute | solution.py:234
  46.5 22.8 %collective-permute-start.13 = (f32[2,2,128,128]{3,2,1,0:T(8,128)S(1)}, f32[2,2,128,128]{3,2,1,0:T(8,128)S(1)}, u32[]{:S(2)}, u32[]{:S(2)}) collective-permute-start(f32[2,2,128,128]{3,2,1,0:T(8,128)S(1)} %collective-permute-done.12.rest_7_), channel_id=1, source_target_pairs={{0,24},{8,16},{16,8},{24,0},{32,56},{40,48},{48,40},{56,32},{64,88... | collective-permute-start | bytes 786440 | tf_op jit(solution)/shard_map/ppermute | solution.py:234
  47.4 22.0 %copy-start.8 = (f32[2,128,1024]{2,1,0:T(8,128)S(1)}, f32[2,128,1024]{2,1,0:T(8,128)}, u32[]{:S(2)}) copy-start(f32[2,128,1024]{2,1,0:T(8,128)} %copy-done.7) | copy-start | bytes 3145732
  47.4 22.0 %copy-start.10 = (f32[2,128,1024]{2,1,0:T(8,128)S(1)}, f32[2,128,1024]{2,1,0:T(8,128)}, u32[]{:S(2)}) copy-start(f32[2,128,1024]{2,1,0:T(8,128)} %copy-done.9) | copy-start | bytes 3145732
  47.4 22.0 %copy-start.13 = (s32[4]{0:T(128)S(1)}, s32[4]{0:T(128)}, u32[]{:S(2)}) copy-start(s32[4]{0:T(128)} %pad_add_fusion.place_ref) | copy-start | bytes 52
  47.4 18.8 %collective-permute-start.17 = (f32[3,1,128,128]{3,2,1,0:T(8,128)S(1)}, f32[3,1,128,128]{3,2,1,0:T(8,128)S(1)}, u32[]{:S(2)}, u32[]{:S(2)}) collective-permute-start(f32[3,1,128,128]{3,2,1,0:T(8,128)S(1)} %pad_maximum_fusion.1.tie_ref.rest_1_), channel_id=1, source_target_pairs={{0,24},{8,16},{16,8},{24,0},{32,56},{40,48},{48,40},{56,32},{64,88... | collective-permute-start | bytes 589832 | tf_op jit(solution)/shard_map/ppermute | solution.py:234
  49.4 19.2 %collective-permute-start.16 = (f32[3,1,128,128]{3,2,1,0:T(8,128)S(1)}, f32[3,1,128,128]{3,2,1,0:T(8,128)S(1)}, u32[]{:S(2)}, u32[]{:S(2)}) collective-permute-start(f32[3,1,128,128]{3,2,1,0:T(8,128)S(1)} %pad_maximum_fusion.1.tie_ref.rest_1_), channel_id=1, source_target_pairs={{0,16},{8,24},{16,0},{24,8},{32,48},{40,56},{48,32},{56,40},{64,80... | collective-permute-start | bytes 589832 | tf_op jit(solution)/shard_map/ppermute | solution.py:234
  52.2 16.4 %collective-permute-start.15 = (f32[3,1,128,128]{3,2,1,0:T(8,128)S(1)}, f32[3,1,128,128]{3,2,1,0:T(8,128)S(1)}, u32[]{:S(2)}, u32[]{:S(2)}) collective-permute-start(f32[3,1,128,128]{3,2,1,0:T(8,128)S(1)} %pad_maximum_fusion.1.tie_ref.rest_1_), channel_id=1, source_target_pairs={{0,8},{8,0},{16,24},{24,16},{32,40},{40,32},{48,56},{56,48},{64,72... | collective-permute-start | bytes 589832 | tf_op jit(solution)/shard_map/ppermute | solution.py:234
  66.2 7.9 %collective-permute-start.18 = (f32[3,1,128,128]{3,2,1,0:T(8,128)S(1)}, f32[3,1,128,128]{3,2,1,0:T(8,128)S(1)}, u32[]{:S(2)}, u32[]{:S(2)}) collective-permute-start(f32[3,1,128,128]{3,2,1,0:T(8,128)S(1)} %pad_maximum_fusion.1.tie_ref.rest_1_), channel_id=1, source_target_pairs={{0,1},{1,0},{2,3},{3,2},{4,5},{5,4},{6,7},{7,6},{8,9},{9,8},{10,11... | collective-permute-start | bytes 589832 | tf_op jit(solution)/shard_map/ppermute | solution.py:234
  68.5 5.6 %collective-permute-start.21 = (f32[3,1,128,128]{3,2,1,0:T(8,128)S(1)}, f32[3,1,128,128]{3,2,1,0:T(8,128)S(1)}, u32[]{:S(2)}, u32[]{:S(2)}) collective-permute-start(f32[3,1,128,128]{3,2,1,0:T(8,128)S(1)} %collective-permute-done.17.rest_4_), channel_id=1, source_target_pairs={{0,1},{1,0},{2,3},{3,2},{4,5},{5,4},{6,7},{7,6},{8,9},{9,8},{10,11... | collective-permute-start | bytes 589832 | tf_op jit(solution)/shard_map/ppermute | solution.py:234
  68.5 5.6 %collective-permute-start.20 = (f32[3,1,128,128]{3,2,1,0:T(8,128)S(1)}, f32[3,1,128,128]{3,2,1,0:T(8,128)S(1)}, u32[]{:S(2)}, u32[]{:S(2)}) collective-permute-start(f32[3,1,128,128]{3,2,1,0:T(8,128)S(1)} %collective-permute-done.16.rest_3_), channel_id=1, source_target_pairs={{0,1},{1,0},{2,3},{3,2},{4,5},{5,4},{6,7},{7,6},{8,9},{9,8},{10,11... | collective-permute-start | bytes 589832 | tf_op jit(solution)/shard_map/ppermute | solution.py:234
  69.1 5.1 %collective-permute-start.19 = (f32[3,1,128,128]{3,2,1,0:T(8,128)S(1)}, f32[3,1,128,128]{3,2,1,0:T(8,128)S(1)}, u32[]{:S(2)}, u32[]{:S(2)}) collective-permute-start(f32[3,1,128,128]{3,2,1,0:T(8,128)S(1)} %collective-permute-done.15.rest_2_), channel_id=1, source_target_pairs={{0,1},{1,0},{2,3},{3,2},{4,5},{5,4},{6,7},{7,6},{8,9},{9,8},{10,11... | collective-permute-start | bytes 589832 | tf_op jit(solution)/shard_map/ppermute | solution.py:234

commit v3 on v2

--- a/solution.py
+++ b/solution.py
@@ -14,6 +14,7 @@
 RING = 4
 CORES = 2
 TILE = 256
+EARLY_HEADS = 4
 
 
 def dot(lhs, rhs, dims):
@@ -28,7 +29,14 @@
     return pl.CostEstimate(flops=int(flops), bytes_accessed=int(mib * MIB), transcendentals=0)
 
 
-def state_kernel(place_ref, key_ref, value_ref, state_ref, *quarter_refs):
+def place():
+    short_pos = lax.axis_index("short").astype(jnp.int32)
+    long_pos = lax.axis_index("long").astype(jnp.int32)
+    block = long_pos * lax.axis_size("short") + short_pos
+    return short_pos & (RING - 1), long_pos & (CORES - 1), block
+
+
+def state_kernel(key_ref, value_ref, state_ref, *quarter_refs):
     step = pl.program_id(0)
 
     @pl.when(step == 0)
@@ -45,18 +53,18 @@
     def _():
         share = heads // RING
         for apart in range(RING):
-            owner = place_ref[0] ^ apart
+            owner = place()[0] ^ apart
             quarter_refs[apart][...] = state_ref[pl.ds(owner * share, share)]
 
 
-def states(place, key, value, rows=512):
+def states(key, value, rows=512):
     length, heads, width = key.shape
     share = heads // RING
     part = pl.BlockSpec((rows, heads, width), lambda i: (i, 0, 0))
     return pl.pallas_call(
         state_kernel,
         grid=(length // rows,),
-        in_specs=[pl.BlockSpec(memory_space=pltpu.SMEM), part, part],
+        in_specs=[part, part],
         out_specs=[pl.BlockSpec((heads, width, width), lambda i: (0, 0, 0))]
         + [pl.BlockSpec((share, width, width), lambda i: (0, 0, 0))] * RING,
         out_shape=[jax.ShapeDtypeStruct((heads, width, width), jnp.float32)]
@@ -64,10 +72,10 @@
         compiler_params=params(60),
         cost_estimate=cost(3e8, 5),
         name="states",
-    )(place, key, value)
-
-
-def layout_kernel(query_ref, key_ref, value_ref, tie_ref, query_out, key_out, value_out):
+    )(key, value)
+
+
+def layout_kernel(query_ref, key_ref, value_ref, query_out, key_out, value_out):
     query_out[...] = jnp.swapaxes(query_ref[...], 0, 1)
     key_out[...] = jnp.swapaxes(key_ref[...], 0, 1)
     values = jnp.swapaxes(value_ref[...], 0, 1)
@@ -75,21 +83,21 @@
         value_out[head] = values[head].T
 
 
-def by_head(query, key, value, tie, rows=512):
+def by_head(query, key, value, rows=512):
     length, heads, width = query.shape
     part = pl.BlockSpec((rows, heads, width), lambda i: (i, 0, 0))
     rowwise = pl.BlockSpec((heads, rows, width), lambda i: (0, i, 0))
     return pl.pallas_call(
         layout_kernel,
         grid=(length // rows,),
-        in_specs=[part] * 3 + [pl.BlockSpec(memory_space=pl.ANY)],
+        in_specs=[part] * 3,
         out_specs=[rowwise, rowwise, pl.BlockSpec((heads, width, rows), lambda i: (0, 0, i))],
         out_shape=[jax.ShapeDtypeStruct((heads, length, width), jnp.bfloat16)] * 2
         + [jax.ShapeDtypeStruct((heads, width, length), jnp.bfloat16)],
-        compiler_params=params(32),
-        cost_estimate=cost(1e6, 12),
+        compiler_params=params(24),
+        cost_estimate=cost(1e6, 0.01),
         name="by_head",
-    )(query, key, value, tie)
+    )(query, key, value)
 
 
 def near_kernel(first, query_ref, key_ref, value_ref, weight_ref, tie_ref, near_ref):
@@ -133,7 +141,7 @@
         near_ref[0, :, cols] = dot(value_ref[0, :, : (tile + 1) * TILE], weighted, NN)
 
 
-def near_part(query, key, value, level_weight, tie, first, count):
+def near_part(query, key, value, level_weight, tie, first, count, mib):
     heads, length, width = query.shape
     levels = level_weight.shape[0]
     rows = pl.BlockSpec((1, length, width), lambda h: (h + first, 0, 0))
@@ -150,13 +158,13 @@
         ],
         out_specs=pl.BlockSpec((1, width, length), lambda h: (h, 0, 0)),
         out_shape=jax.ShapeDtypeStruct((count, width, length), jnp.float32),
-        compiler_params=params(16),
-        cost_estimate=cost(count * 5e8, count * 2),
+        compiler_params=params(mib),
+        cost_estimate=cost(1e6, 0.01),
         name="near",
     )(query, key, value, level_weight, tie)
 
 
-def far_kernel(plan, last, local_bits, place_ref, query_ref, weight_ref, *rest):
+def far_kernel(plan, last, local_bits, query_ref, weight_ref, *rest):
     count, bits, pieces = plan
     total_refs, rest = rest[:count], rest[count:]
     piece_refs, rest = rest[: len(pieces)], rest[len(pieces) :]
@@ -169,7 +177,7 @@
     @pl.when(pl.program_id(0) == 0)
     def _():
         for ref, (piece_bits, first_head) in zip(piece_refs, pieces):
-            base = first_head(place_ref)
+            base = first_head(place())
             for at, bit in enumerate(piece_bits):
                 for head in range(ref.shape[1]):
                     bucket = ref[at, head]
@@ -179,12 +187,13 @@
                     split[base + head, where : where + width, :width] = high
                     split[base + head, where : where + width, width:] = low
 
-    block = place_ref[3]
-    share = heads // count
+    block = place()[2]
+    held = [(ref, at) for ref in total_refs for at in range(ref.shape[0])]
     for head in range(heads):
         query = query_ref[head]
         products = dot(split[head], jnp.concatenate([query, query], 1), NT)
-        total = total_refs[head // share][head % share]
+        ref, at = held[head]
+        total = ref[at]
         for at, bit in enumerate(bits):
             gain = weight_ref[local_bits + 1 + bit, head : head + 1, :]
             gain = jnp.where((block >> bit) & 1 == 1, gain, 0.0)
@@ -199,7 +208,7 @@
         out_ref[...] = total_f[...].reshape(rows, heads, width).astype(jnp.bfloat16)
 
 
-def far_part(place, query, level_weight, totals, bits, pieces, last, rows=256):
+def far_part(query, level_weight, totals, bits, pieces, last, rows=512):
     heads, length, width = query.shape
     levels = level_weight.shape[0]
     local_bits = length.bit_length() - 1
@@ -213,7 +222,6 @@
         functools.partial(far_kernel, plan, last, local_bits),
         grid=(length // rows,),
         in_specs=[
-            pl.BlockSpec(memory_space=pltpu.SMEM),
             pl.BlockSpec((heads, rows, width), lambda i: (0, i, 0)),
             pl.BlockSpec((levels, heads, rows), lambda i: (0, 0, i)),
         ]
@@ -224,10 +232,10 @@
         if last
         else jax.ShapeDtypeStruct((heads, width, length), jnp.float32),
         scratch_shapes=scratch,
-        compiler_params=params(28),
-        cost_estimate=cost(len(bits) * 6e8, 10),
+        compiler_params=params(20 if last else 24),
+        cost_estimate=cost(1e6, 0.01),
         name="finish" if last else "far",
-    )(place, query, level_weight, *totals, *arrays)
+    )(query, level_weight, *totals, *arrays)
 
 
 def along(value, axis, hop):
@@ -260,59 +268,57 @@
 
 def per_device(query, key, value, level_weight):
     level_weight = jnp.transpose(level_weight, (1, 0, 2))
-    short_pos = lax.axis_index("short").astype(jnp.int32)
-    long_pos = lax.axis_index("long").astype(jnp.int32)
-    y, core = short_pos % RING, long_pos % CORES
-    block = long_pos * lax.axis_size("short") + short_pos
-    place = jnp.stack([y, core, short_pos // RING, block])
-
-    state, *quarters = states(place, key, value)
-    quarters = [quarters[0]] + [apart_y(quarters[m], m) for m in (1, 3, 2)]
-    quarters = [quarters[0], quarters[1], quarters[3], quarters[2]]
+    core = place()[1]
+    state, *quarters = states(key, value)
+    quarters = [quarters[0]] + [apart_y(quarters[m], m) for m in (1, 2, 3)]
+    query_h, key_h, value_t = by_head(tied(query, state), key, value)
     first = apart_y(state, 1)
-    query_h, key_h, value_t = by_head(query, key, value, quarters[0])
     heads = query_h.shape[0]
     share = heads // RING
 
-    def near_of(head, tie):
-        return near_part(query_h, key_h, value_t, level_weight, tie, head, share)
-
     quarters = tied(quarters, query_h)
     ring_y = sum(quarters[1:], quarters[0])
 
+    def near_of(head, count, tie, mib):
+        return near_part(query_h, key_h, value_t, level_weight, tie, head, count, mib)
+
     sums = [ring_y] + [apart_z(ring_y, m) for m in (1, 2, 3)]
-    near = [near_of(0, ring_y), near_of(share, ring_y)]
-    sums, pair = lax.optimization_barrier((sums, state + first, *near))[:2]
+    near = [near_of(0, EARLY_HEADS, ring_y, 12)]
+    sums = tied(sums, near[0])
     ring_z = sum(sums[1:], sums[0])
+    facing = other_core(ring_z)
+    pair = state + tied(first, ring_z)
     second = apart_y(pair, 3)
-    facing = other_core(ring_z)
+    facing = tied(facing, pair)
     near_buckets = jnp.stack(buckets_of_ring(sums))
+    inner = [near_buckets, apart_y(near_buckets, 1), None, None]
 
     mine = lax.dynamic_slice_in_dim(ring_z, core, 1, 0)
     theirs = lax.dynamic_slice_in_dim(facing, core, 1, 0)
     chip = mine + theirs
-    chips = [chip] + [apart_x(chip, m) for m in (1, 2, 3)]
-    near.append(near_of(2 * share, chip))
-    near_buckets = tied(near_buckets, chip)
-    inner = [near_buckets, apart_y(near_buckets, 1), None, apart_y(near_buckets, 3)]
-    chips = tied(chips, near[2])
-    outer = jnp.stack([jnp.where(core == 0, mine, theirs), *buckets_of_ring(chips)])
+    chip_first = apart_x(chip, 1)
+    inner[3] = apart_y(tied(near_buckets, chip), 3)
+    chip_second = apart_x(chip + chip_first, 3)
+    chip_second = tied(chip_second, inner[1], inner[3])
+    outer = jnp.stack([jnp.where(core == 0, mine, theirs), chip_first, chip_second])
+    outer_facing = [other_core(outer)]
     outer = [outer] + [apart_y(outer, m) for m in (1, 2, 3)]
-    inner[2] = apart_y(inner[1], 3)
-    outer_facing = [other_core(piece) for piece in outer]
-    near.append(near_of(3 * share, outer[0]))
+    inner[2] = apart_y(tied(inner[3], outer_facing[0]), 1)
+    near.append(near_of(EARLY_HEADS, heads - EARLY_HEADS, outer_facing[0], 12))
 
     def owner(m):
         return lambda p: (p[0] ^ m) * share
 
     pieces = [(first[None], (0,), lambda p: 0), (second[None], (1,), lambda p: 0)]
     pieces += [(inner[m], (2, 3), owner(m)) for m in range(RING)]
-    total = far_part(place, query_h, level_weight, near, (0, 1, 2, 3), pieces, False)
+    total = far_part(query_h, level_weight, near, (0, 1, 2, 3), pieces, False)
+    outer = [outer[0]] + tied(outer[1:], total)
+    outer_facing += [other_core(piece) for piece in outer[1:]]
     pieces = [(outer[m], (4, 5, 6), lambda p, m=m: owner(m)(p) + p[1]) for m in range(RING)]
     pieces += [
         (outer_facing[m], (4, 5, 6), lambda p, m=m: owner(m)(p) + 1 - p[1]) for m in range(RING)
     ]
-    return far_part(place, query_h, level_weight, [total], (4, 5, 6), pieces, True)
+    return far_part(query_h, level_weight, [total], (4, 5, 6), pieces, True)
 
 
 def solution(mesh):

time: 80 us -> 73.2 us (0.915)
  waiting for transfers between devices: 15 us -> 11.3 us
  local copies, waits for them, and re-layouts: 9.86 us -> 7.76 us
  Pallas kernels: 25.5 us -> 23.5 us
  starting transfers between devices: 26 us -> 27.3 us
    ppermute x22 -> x21, waiting for transfers between devices: 15 us -> 11.3 us  [along(): lax.ppermute(value, axis, [(i, hop(i)) for i in range(lax.axis_size(axis))])]
    unnamed x30 -> x22, local copies, waits for them, and re-layouts: 9.86 us -> 7.76 us
    pallas_call x2, Pallas kernels: 10.3 us -> 8.4 us  [far_part(): pl.pallas_call(functools.partial(far_kernel, plan, last, local_bits), gri...]
    ppermute x22 -> x21, starting transfers between devices: 26 us -> 27.3 us  [along(): lax.ppermute(value, axis, [(i, hop(i)) for i in range(lax.axis_size(axis))])]
    pallas_call x4 -> x2, Pallas kernels: 9.02 us -> 8.99 us  [near_part(): pl.pallas_call(functools.partial(near_kernel, first), grid=(count,), in_s...]
  transfers between devices with their start and end apart: 22 -> 21, of which waited for: 3 -> 9; matrix products, arithmetic and copies ran while one was open for 2% -> 4% of each run, Pallas kernels for 20% -> 21%
where the time goes in v3:
time: 73.2 us; the launch traced here: 72.9 us
  starting transfers between devices  27.3 us (37%)
  Pallas kernels  23.5 us (32%)
  waiting for transfers between devices  11.3 us (15%)
  local copies, waits for them, and re-layouts  7.76 us (11%)
  other arithmetic  2.86 us (4%)
    ppermute x21, starting transfers between devices, along(): lax.ppermute(value, axis, [(i, hop(i)) for i in range(lax.axis_size(axis))])  27.3 us
    ppermute x21, waiting for transfers between devices, along(): lax.ppermute(value, axis, [(i, hop(i)) for i in range(lax.axis_size(axis))])  11.3 us
    pallas_call x2, Pallas kernels, near_part(): pl.pallas_call(functools.partial(near_kernel, first), grid=(count,), in_s...  8.99 us
    pallas_call x2, Pallas kernels, far_part(): pl.pallas_call(functools.partial(far_kernel, plan, last, local_bits), gri...  8.4 us
    unnamed x22, local copies, waits for them, and re-layouts  7.76 us
    pallas_call x1, Pallas kernels, states(): pl.pallas_call(state_kernel, grid=(length // rows,), in_specs=[part, part...  3.79 us
    pallas_call x1, Pallas kernels, by_head(): pl.pallas_call(layout_kernel, grid=(length // rows,), in_specs=[part] * 3...  2.3 us
  transfers between devices with their start and end apart: 21, of which 9 were waited for; matrix products, arithmetic and copies ran while one was open for 4% of the time, Pallas kernels for 21%

profile of v3, /device:TPU:1, one launch (start us, length us, event | category | flops | bytes accessed | tf_op | source)
XLA Modules:
  0.0 72.9 jit_solution(13565299587478057488)
XLA Ops:
  0.0 3.8 %states.1 = (f32[8,128,128]{2,1,0:T(8,128)}, f32[2,128,128]{2,1,0:T(8,128)}, f32[2,128,128]{2,1,0:T(8,128)}, f32[2,128,128]{2,1,0:T(8,128)}, f32[2,128,128]{2,1,0:T(8,128)}) custom-call(bf16[1024,8,128]{2,1,0:T(8,128)(2,1)} %key_ref.3, bf16[1024,8,128]{2,1,0:T(8,128)(2,1)} %value_ref.3), custom_call_target="tpu_custom_call" | custom-call | flops 300000000 | bytes 5242880 | tf_op jit(solution)/shard_map/states/pallas_call | solution.py:64
  3.8 2.1 %collective-permute-start = (f32[2,128,128]{2,1,0:T(8,128)}, f32[2,128,128]{2,1,0:T(8,128)S(1)}, u32[]{:S(2)}, u32[]{:S(2)}) collective-permute-start(f32[2,128,128]{2,1,0:T(8,128)} %get-tuple-element.36), channel_id=1, source_target_pairs={{0,8},{8,0},{16,24},{24,16},{32,40},{40,32},{48,56},{56,48},{64,72... | collective-permute-start | bytes 393224 | tf_op jit(solution)/shard_map/ppermute | solution.py:242
  5.9 2.6 %collective-permute-start.1 = (f32[2,128,128]{2,1,0:T(8,128)}, f32[2,128,128]{2,1,0:T(8,128)S(1)}, u32[]{:S(2)}, u32[]{:S(2)}) collective-permute-start(f32[2,128,128]{2,1,0:T(8,128)} %get-tuple-element.37), channel_id=1, source_target_pairs={{0,16},{8,24},{16,0},{24,8},{32,48},{40,56},{48,32},{56,40},{64,80... | collective-permute-start | bytes 393224 | tf_op jit(solution)/shard_map/ppermute | solution.py:242
  8.5 0.0 collective-permute-start.2
  8.5 0.0 collective-permute-start.7
  8.6 1.7 %copy-done.1 = bf16[1024,8,128]{2,1,0:T(8,128)(2,1)S(1)} copy-done((bf16[1024,8,128]{2,1,0:T(8,128)(2,1)S(1)}, bf16[1024,8,128]{2,1,0:T(8,128)(2,1)}, u32[]{:S(2)}) %copy-start.1) | copy-done | bytes 2097176
  10.2 1.6 %copy-done.2 = bf16[1024,8,128]{2,1,0:T(8,128)(2,1)S(1)} copy-done((bf16[1024,8,128]{2,1,0:T(8,128)(2,1)S(1)}, bf16[1024,8,128]{2,1,0:T(8,128)(2,1)}, u32[]{:S(2)}) %copy-start.2) | copy-done | bytes 2097176
  11.8 1.6 %copy-done.9 = bf16[1024,8,128]{2,1,0:T(8,128)(2,1)S(1)} copy-done((bf16[1024,8,128]{2,1,0:T(8,128)(2,1)S(1)}, bf16[1024,8,128]{2,1,0:T(8,128)(2,1)}, u32[]{:S(2)}) %copy-start.9) | copy-done | bytes 2097176
  13.4 2.3 %by_head.1 = (bf16[8,1024,128]{2,1,0:T(8,128)(2,1)S(1)}, bf16[8,1024,128]{2,1,0:T(8,128)(2,1)S(1)}, bf16[8,128,1024]{2,1,0:T(8,128)(2,1)S(1)}) custom-call(bf16[1024,8,128]{2,1,0:T(8,128)(2,1)S(1)} %copy-done.9, bf16[1024,8,128]{2,1,0:T(8,128)(2,1)S(1)} %copy-done.1, bf16[1024,8,128]{2,1,0:T(8,128)(2,1)S(1)} %copy-done.2), custom_call_target="tpu_custom_call" | custom-call | flops 1000000 | bytes 10485 | tf_op jit(solution)/shard_map/by_head/pallas_call | solution.py:90
  15.7 0.0 copy-start.5
  15.7 0.0 copy-start.7
  15.7 0.0 collective-permute-done
  15.7 0.0 collective-permute-done.1
  15.7 1.2 %collective-permute-done.2 = f32[2,128,128]{2,1,0:T(8,128)S(1)} collective-permute-done((f32[2,128,128]{2,1,0:T(8,128)}, f32[2,128,128]{2,1,0:T(8,128)S(1)}, u32[]{:S(2)}, u32[]{:S(2)}) %collective-permute-start.2) | collective-permute-done | bytes 131104 | tf_op jit(solution)/shard_map/ppermute | solution.py:242
  17.0 0.0 copy-done.10
  17.0 1.7 %collective-permute-start.3 = (f32[2,128,128]{2,1,0:T(8,128)S(1)}, f32[2,128,128]{2,1,0:T(8,128)S(1)}, u32[]{:S(2)}, u32[]{:S(2)}) collective-permute-start(f32[2,128,128]{2,1,0:T(8,128)S(1)} %add_add_fusion.1.tie_ref), channel_id=1, source_target_pairs={{0,32},{8,40},{16,48},{24,56},{32,0},{40,8},{48,16},{56,24},{64,96... | collective-permute-start | bytes 393224 | tf_op jit(solution)/shard_map/ppermute | solution.py:242
  18.7 3.3 %collective-permute-start.4 = (f32[2,128,128]{2,1,0:T(8,128)S(1)}, f32[2,128,128]{2,1,0:T(8,128)S(1)}, u32[]{:S(2)}, u32[]{:S(2)}) collective-permute-start(f32[2,128,128]{2,1,0:T(8,128)S(1)} %add_add_fusion.1.tie_ref), channel_id=1, source_target_pairs={{0,64},{8,72},{16,80},{24,88},{32,96},{40,104},{48,112},{56,120},{... | collective-permute-start | bytes 393224 | tf_op jit(solution)/shard_map/ppermute | solution.py:242
  22.0 0.0 collective-permute-start.5
  22.0 0.0 copy-done
  22.0 4.5 %near.2.rest_0_ = f32[4,128,1024]{2,1,0:T(8,128)S(1)} custom-call(bf16[8,1024,128]{2,1,0:T(8,128)(2,1)S(1)} %get-tuple-element.32.query_ref, bf16[8,1024,128]{2,1,0:T(8,128)(2,1)S(1)} %get-tuple-element.33.key_ref, bf16[8,128,1024]{2,1,0:T(8,128)(2,1)S(1)} %get-tuple-element.34.value_ref, f32[20,8,1024]{2,1,0:T(8,128)S(1)} %bitcast.10, ...), custom_call_target="tpu_custom_call" | custom-call | flops 1000000 | bytes 10485 | tf_op jit(solution)/shard_map/near/pallas_call | solution.py:149
  26.5 0.0 copy-done.5
  26.5 0.0 copy-done.7
  26.5 0.0 copy-start.3
  26.6 1.3 %copy-done.3 = f32[4,128,1024]{2,1,0:T(8,128)} copy-done((f32[4,128,1024]{2,1,0:T(8,128)}, f32[4,128,1024]{2,1,0:T(8,128)S(1)}, u32[]{:S(2)}) %copy-start.3) | copy-done | bytes 2097176
  27.9 0.0 collective-permute-done.3
  27.9 0.0 collective-permute-done.4
  27.9 1.8 %collective-permute-done.5 = f32[2,128,128]{2,1,0:T(8,128)S(1)} collective-permute-done((f32[2,128,128]{2,1,0:T(8,128)S(1)}, f32[2,128,128]{2,1,0:T(8,128)S(1)}, u32[]{:S(2)}, u32[]{:S(2)}) %collective-permute-start.5) | collective-permute-done | bytes 131104 | tf_op jit(solution)/shard_map/ppermute | solution.py:242
  29.7 0.7 add_bitcast_fusion
  30.3 1.5 %collective-permute-start.6 = (f32[2,128,128]{2,1,0:T(8,128)}, f32[2,128,128]{2,1,0:T(8,128)}, u32[]{:S(2)}, u32[]{:S(2)}) collective-permute-start(f32[2,128,128]{2,1,0:T(8,128)} %get-tuple-element.58), channel_id=1, source_target_pairs={{0,1},{1,0},{2,3},{3,2},{4,5},{5,4},{6,7},{7,6},{8,9},{9,8},{10,11... | collective-permute-start | bytes 393224 | tf_op jit(solution)/shard_map/ppermute | solution.py:242
  31.8 0.1 collective-permute-start.10
  31.9 0.0 collective-permute-done.7
  32.0 1.2 %add.41 = f32[8,128,128]{2,1,0:T(8,128)S(1)} add(f32[8,128,128]{2,1,0:T(8,128)} %get-tuple-element.30, f32[8,128,128]{2,1,0:T(8,128)S(1)} %collective-permute-done.7) | non-fusion elementwise | flops 131072 | bytes 1572864 | tf_op jit(solution)/shard_map/add | solution.py:290
  33.2 0.0 collective-permute-done.6
  33.2 0.9 %select_bitcast_fusion = (f32[1,1,128,128]{3,2,1,0:T(8,128)S(1)}, f32[1,128,128]{2,1,0:T(8,128)S(1)}) fusion(f32[2,128,128]{2,1,0:T(8,128)} %collective-permute-done.6, s32[]{:T(128)S(6)} %select_n.13, f32[2,128,128]{2,1,0:T(8,128)} %get-tuple-element.58, pred[]{:T(512)S(6)} %eq.3), kind=kLoop, calls=%fused_computation.5 | loop fusion | flops 32768 | bytes 262149 | tf_op jit(solution)/shard_map/stack | solution.py:303
  34.1 2.5 %collective-permute-start.11 = (f32[2,2,128,128]{3,2,1,0:T(8,128)S(1)}, f32[2,2,128,128]{3,2,1,0:T(8,128)S(1)}, u32[]{:S(2)}, u32[]{:S(2)}) collective-permute-start(f32[2,2,128,128]{3,2,1,0:T(8,128)S(1)} %pad_maximum_fusion.rest_4_), channel_id=1, source_target_pairs={{0,24},{8,16},{16,8},{24,0},{32,56},{40,48},{48,40},{56,32},{64,88... | collective-permute-start | bytes 786440 | tf_op jit(solution)/shard_map/ppermute | solution.py:242
  36.6 1.2 %collective-permute-start.8 = (f32[1,128,128]{2,1,0:T(8,128)S(1)}, f32[1,128,128]{2,1,0:T(8,128)S(1)}, u32[]{:S(2)}, u32[]{:S(2)}) collective-permute-start(f32[1,128,128]{2,1,0:T(8,128)S(1)} %get-tuple-element.56), channel_id=1, source_target_pairs={{0,2},{1,3},{2,0},{3,1},{4,6},{5,7},{6,4},{7,5},{8,10},{9,11},{10,... | collective-permute-start | bytes 196616 | tf_op jit(solution)/shard_map/ppermute | solution.py:242
  37.8 2.2 %collective-permute-done.8 = f32[1,128,128]{2,1,0:T(8,128)S(1)} collective-permute-done((f32[1,128,128]{2,1,0:T(8,128)S(1)}, f32[1,128,128]{2,1,0:T(8,128)S(1)}, u32[]{:S(2)}, u32[]{:S(2)}) %collective-permute-start.8) | collective-permute-done | bytes 65568 | tf_op jit(solution)/shard_map/ppermute | solution.py:242
  40.0 2.6 %collective-permute-start.9 = (f32[1,128,128]{2,1,0:T(8,128)S(1)}, f32[1,128,128]{2,1,0:T(8,128)S(1)}, u32[]{:S(2)}, u32[]{:S(2)}) collective-permute-start(f32[1,128,128]{2,1,0:T(8,128)S(1)} %add.43), channel_id=1, source_target_pairs={{0,6},{1,7},{2,4},{3,5},{4,2},{5,3},{6,0},{7,1},{8,14},{9,15},{10,... | collective-permute-start | bytes 196616 | tf_op jit(solution)/shard_map/ppermute | solution.py:242
  42.6 0.3 collective-permute-start.13
  42.8 0.0 collective-permute-done.10.rest_5_
  42.8 1.6 %collective-permute-done.9 = f32[1,128,128]{2,1,0:T(8,128)S(1)} collective-permute-done((f32[1,128,128]{2,1,0:T(8,128)S(1)}, f32[1,128,128]{2,1,0:T(8,128)S(1)}, u32[]{:S(2)}, u32[]{:S(2)}) %collective-permute-start.9) | collective-permute-done | bytes 65568 | tf_op jit(solution)/shard_map/ppermute | solution.py:242
  44.4 0.0 collective-permute-done.11.rest_7_
  44.4 0.0 copy-start.4
  44.4 2.6 %collective-permute-start.12 = (f32[3,1,128,128]{3,2,1,0:T(8,128)S(1)}, f32[3,1,128,128]{3,2,1,0:T(8,128)S(1)}, u32[]{:S(2)}, u32[]{:S(2)}) collective-permute-start(f32[3,1,128,128]{3,2,1,0:T(8,128)S(1)} %pad_maximum_fusion.1.rest_1_), channel_id=1, source_target_pairs={{0,1},{1,0},{2,3},{3,2},{4,5},{5,4},{6,7},{7,6},{8,9},{9,8},{10,11... | collective-permute-start | bytes 589832 | tf_op jit(solution)/shard_map/ppermute | solution.py:242
  47.1 1.1 %collective-permute-done.12.tie_ref.rest_5_ = f32[3,1,128,128]{3,2,1,0:T(8,128)S(1)} collective-permute-done((f32[3,1,128,128]{3,2,1,0:T(8,128)S(1)}, f32[3,1,128,128]{3,2,1,0:T(8,128)S(1)}, u32[]{:S(2)}, u32[]{:S(2)}) %collective-permute-start.12) | collective-permute-done | bytes 196640 | tf_op jit(solution)/shard_map/ppermute | solution.py:242
  48.2 0.0 collective-permute-start.14
  48.2 1.5 %collective-permute-start.15 = (f32[3,1,128,128]{3,2,1,0:T(8,128)S(1)}, f32[3,1,128,128]{3,2,1,0:T(8,128)S(1)}, u32[]{:S(2)}, u32[]{:S(2)}) collective-permute-start(f32[3,1,128,128]{3,2,1,0:T(8,128)S(1)} %pad_maximum_fusion.1.rest_1_), channel_id=1, source_target_pairs={{0,8},{8,0},{16,24},{24,16},{32,40},{40,32},{48,56},{56,48},{64,72... | collective-permute-start | bytes 589832 | tf_op jit(solution)/shard_map/ppermute | solution.py:242
  49.6 0.7 collective-permute-start.16
  50.3 1.7 %collective-permute-start.17 = (f32[3,1,128,128]{3,2,1,0:T(8,128)S(1)}, f32[3,1,128,128]{3,2,1,0:T(8,128)S(1)}, u32[]{:S(2)}, u32[]{:S(2)}) collective-permute-start(f32[3,1,128,128]{3,2,1,0:T(8,128)S(1)} %pad_maximum_fusion.1.rest_1_), channel_id=1, source_target_pairs={{0,24},{8,16},{16,8},{24,0},{32,56},{40,48},{48,40},{56,32},{64,88... | collective-permute-start | bytes 589832 | tf_op jit(solution)/shard_map/ppermute | solution.py:242
  52.1 1.6 %copy-done.8 = bf16[8,128,1024]{2,1,0:T(8,128)(2,1)S(1)} copy-done((bf16[8,128,1024]{2,1,0:T(8,128)(2,1)S(1)}, bf16[8,128,1024]{2,1,0:T(8,128)(2,1)}, u32[]{:S(2)}) %copy-start.8) | copy-done | bytes 2097176
  53.6 4.5 %near.3.rest_1_ = f32[4,128,1024]{2,1,0:T(8,128)S(1)} custom-call(bf16[8,1024,128]{2,1,0:T(8,128)(2,1)S(1)} %get-tuple-element.32.query_ref, bf16[8,1024,128]{2,1,0:T(8,128)(2,1)S(1)} %copy-done.6, bf16[8,128,1024]{2,1,0:T(8,128)(2,1)S(1)} %copy-done.8, f32[20,8,1024]{2,1,0:T(8,128)S(1)} %bitcast.11, ...), custom_call_target="tpu_custom_call" | custom-call | flops 1000000 | bytes 10485 | tf_op jit(solution)/shard_map/near/pallas_call | solution.py:149
  58.2 0.0 collective-permute-done.13
  58.2 0.0 collective-permute-done.14.rest_6_
  58.2 3.7 %far.1.rest_0_ = f32[8,128,1024]{2,1,0:T(8,128)S(1)} custom-call(bf16[8,1024,128]{2,1,0:T(8,128)(2,1)S(1)} %get-tuple-element.32.query_ref, f32[20,8,1024]{2,1,0:T(8,128)S(1)} %bitcast.12, f32[4,128,1024]{2,1,0:T(8,128)S(1)} %copy-done.4, f32[4,128,1024]{2,1,0:T(8,128)S(1)} %near.3.rest_1_, f32[1,8,128,128]{3,2,1,0:T(8,128)S(1)} %bitcast.14, ...), custom_call_target="tpu_custom_call" | custom-call | flops 1000000 | bytes 10485 | tf_op jit(solution)/shard_map/far/pallas_call | solution.py:221
  61.9 0.0 collective-permute-done.15.rest_2_
  61.9 2.2 %collective-permute-done.16.rest_3_ = f32[3,1,128,128]{3,2,1,0:T(8,128)S(1)} collective-permute-done((f32[3,1,128,128]{3,2,1,0:T(8,128)S(1)}, f32[3,1,128,128]{3,2,1,0:T(8,128)S(1)}, u32[]{:S(2)}, u32[]{:S(2)}) %collective-permute-start.16) | collective-permute-done | bytes 196640 | tf_op jit(solution)/shard_map/ppermute | solution.py:242
  64.2 0.0 collective-permute-done.17.rest_4_
  64.2 2.4 %collective-permute-start.18 = (f32[3,1,128,128]{3,2,1,0:T(8,128)S(1)}, f32[3,1,128,128]{3,2,1,0:T(8,128)S(1)}, u32[]{:S(2)}, u32[]{:S(2)}) collective-permute-start(f32[3,1,128,128]{3,2,1,0:T(8,128)S(1)} %collective-permute-done.15.rest_2_), channel_id=1, source_target_pairs={{0,1},{1,0},{2,3},{3,2},{4,5},{5,4},{6,7},{7,6},{8,9},{9,8},{10,11... | collective-permute-start | bytes 589832 | tf_op jit(solution)/shard_map/ppermute | solution.py:242
  66.5 0.0 collective-permute-start.19
  66.5 0.5 collective-permute-start.20
  67.0 0.6 collective-permute-done.18.rest_6_
  67.6 0.4 collective-permute-done.19.rest_7_
  68.0 0.3 collective-permute-done.20.rest_8_
  68.3 4.7 %finish.1 = bf16[1024,8,128]{2,1,0:T(8,128)(2,1)} custom-call(bf16[8,1024,128]{2,1,0:T(8,128)(2,1)S(1)} %get-tuple-element.32.query_ref, f32[20,8,1024]{2,1,0:T(8,128)S(1)} %bitcast.13, f32[8,128,1024]{2,1,0:T(8,128)S(1)} %far.1.rest_0_, f32[3,1,128,128]{3,2,1,0:T(8,128)S(1)} %pad_maximum_fusion.1.rest_1_, ...), custom_call_target="tpu_custom_call" | custom-call | flops 1000000 | bytes 10485 | tf_op jit(solution)/shard_map/finish/pallas_call | solution.py:221
  (13 shorter events, 0.1 us)
Async XLA Ops:
  3.8 11.9 %collective-permute-start = (f32[2,128,128]{2,1,0:T(8,128)}, f32[2,128,128]{2,1,0:T(8,128)S(1)}, u32[]{:S(2)}, u32[]{:S(2)}) collective-permute-start(f32[2,128,128]{2,1,0:T(8,128)} %get-tuple-element.36), channel_id=1, source_target_pairs={{0,8},{8,0},{16,24},{24,16},{32,40},{40,32},{48,56},{56,48},{64,72... | collective-permute-start | bytes 393224 | tf_op jit(solution)/shard_map/ppermute | solution.py:242
  5.9 9.8 %collective-permute-start.1 = (f32[2,128,128]{2,1,0:T(8,128)}, f32[2,128,128]{2,1,0:T(8,128)S(1)}, u32[]{:S(2)}, u32[]{:S(2)}) collective-permute-start(f32[2,128,128]{2,1,0:T(8,128)} %get-tuple-element.37), channel_id=1, source_target_pairs={{0,16},{8,24},{16,0},{24,8},{32,48},{40,56},{48,32},{56,40},{64,80... | collective-permute-start | bytes 393224 | tf_op jit(solution)/shard_map/ppermute | solution.py:242
  8.5 8.4 %collective-permute-start.2 = (f32[2,128,128]{2,1,0:T(8,128)}, f32[2,128,128]{2,1,0:T(8,128)S(1)}, u32[]{:S(2)}, u32[]{:S(2)}) collective-permute-start(f32[2,128,128]{2,1,0:T(8,128)} %get-tuple-element.38), channel_id=1, source_target_pairs={{0,24},{8,16},{16,8},{24,0},{32,56},{40,48},{48,40},{56,32},{64,88... | collective-permute-start | bytes 393224 | tf_op jit(solution)/shard_map/ppermute | solution.py:242
  8.5 13.5 %copy-start = (f32[8,20,1024]{2,0,1:T(8,128)S(1)}, f32[8,20,1024]{2,0,1:T(8,128)}, u32[]{:S(2)}) copy-start(f32[8,20,1024]{2,0,1:T(8,128)} %param.7) | copy-start | bytes 1966084
  8.5 23.4 %collective-permute-start.7 = (f32[8,128,128]{2,1,0:T(8,128)}, f32[8,128,128]{2,1,0:T(8,128)S(1)}, u32[]{:S(2)}, u32[]{:S(2)}) collective-permute-start(f32[8,128,128]{2,1,0:T(8,128)} %get-tuple-element.30), channel_id=1, source_target_pairs={{0,8},{8,0},{16,24},{24,16},{32,40},{40,32},{48,56},{56,48},{64,72... | collective-permute-start | bytes 1572872 | tf_op jit(solution)/shard_map/ppermute | solution.py:242
  8.6 1.7 %copy-start.1 = (bf16[1024,8,128]{2,1,0:T(8,128)(2,1)S(1)}, bf16[1024,8,128]{2,1,0:T(8,128)(2,1)}, u32[]{:S(2)}) copy-start(bf16[1024,8,128]{2,1,0:T(8,128)(2,1)} %key_ref.3) | copy-start | bytes 6291460
  10.2 1.6 %copy-start.2 = (bf16[1024,8,128]{2,1,0:T(8,128)(2,1)S(1)}, bf16[1024,8,128]{2,1,0:T(8,128)(2,1)}, u32[]{:S(2)}) copy-start(bf16[1024,8,128]{2,1,0:T(8,128)(2,1)} %value_ref.3) | copy-start | bytes 6291460
  11.8 1.6 %copy-start.9 = (bf16[1024,8,128]{2,1,0:T(8,128)(2,1)S(1)}, bf16[1024,8,128]{2,1,0:T(8,128)(2,1)}, u32[]{:S(2)}) copy-start(bf16[1024,8,128]{2,1,0:T(8,128)(2,1)} %query_ref) | copy-start | bytes 6291460
  13.4 3.6 %copy-start.10 = (f32[2,128,128]{2,1,0:T(8,128)S(1)}, f32[2,128,128]{2,1,0:T(8,128)}, u32[]{:S(2)}) copy-start(f32[2,128,128]{2,1,0:T(8,128)} %get-tuple-element.39) | copy-start | bytes 393220
  15.7 10.8 %copy-start.5 = (bf16[8,1024,128]{2,1,0:T(8,128)(2,1)}, bf16[8,1024,128]{2,1,0:T(8,128)(2,1)S(1)}, u32[]{:S(2)}) copy-start(bf16[8,1024,128]{2,1,0:T(8,128)(2,1)S(1)} %get-tuple-element.33.key_ref) | copy-start | bytes 6291460
  15.7 10.8 %copy-start.7 = (bf16[8,128,1024]{2,1,0:T(8,128)(2,1)}, bf16[8,128,1024]{2,1,0:T(8,128)(2,1)S(1)}, u32[]{:S(2)}) copy-start(bf16[8,128,1024]{2,1,0:T(8,128)(2,1)S(1)} %get-tuple-element.34.value_ref) | copy-start | bytes 6291460
  17.0 10.9 %collective-permute-start.3 = (f32[2,128,128]{2,1,0:T(8,128)S(1)}, f32[2,128,128]{2,1,0:T(8,128)S(1)}, u32[]{:S(2)}, u32[]{:S(2)}) collective-permute-start(f32[2,128,128]{2,1,0:T(8,128)S(1)} %add_add_fusion.1.tie_ref), channel_id=1, source_target_pairs={{0,32},{8,40},{16,48},{24,56},{32,0},{40,8},{48,16},{56,24},{64,96... | collective-permute-start | bytes 393224 | tf_op jit(solution)/shard_map/ppermute | solution.py:242
  18.7 9.2 %collective-permute-start.4 = (f32[2,128,128]{2,1,0:T(8,128)S(1)}, f32[2,128,128]{2,1,0:T(8,128)S(1)}, u32[]{:S(2)}, u32[]{:S(2)}) collective-permute-start(f32[2,128,128]{2,1,0:T(8,128)S(1)} %add_add_fusion.1.tie_ref), channel_id=1, source_target_pairs={{0,64},{8,72},{16,80},{24,88},{32,96},{40,104},{48,112},{56,120},{... | collective-permute-start | bytes 393224 | tf_op jit(solution)/shard_map/ppermute | solution.py:242
  22.0 7.6 %collective-permute-start.5 = (f32[2,128,128]{2,1,0:T(8,128)S(1)}, f32[2,128,128]{2,1,0:T(8,128)S(1)}, u32[]{:S(2)}, u32[]{:S(2)}) collective-permute-start(f32[2,128,128]{2,1,0:T(8,128)S(1)} %add_add_fusion.1.tie_ref), channel_id=1, source_target_pairs={{0,96},{8,104},{16,112},{24,120},{32,64},{40,72},{48,80},{56,88},{... | collective-permute-start | bytes 393224 | tf_op jit(solution)/shard_map/ppermute | solution.py:242
  26.5 1.3 %copy-start.3 = (f32[4,128,1024]{2,1,0:T(8,128)}, f32[4,128,1024]{2,1,0:T(8,128)S(1)}, u32[]{:S(2)}) copy-start(f32[4,128,1024]{2,1,0:T(8,128)S(1)} %near.2.rest_0_) | copy-start | bytes 6291460
  30.3 2.8 %collective-permute-start.6 = (f32[2,128,128]{2,1,0:T(8,128)}, f32[2,128,128]{2,1,0:T(8,128)}, u32[]{:S(2)}, u32[]{:S(2)}) collective-permute-start(f32[2,128,128]{2,1,0:T(8,128)} %get-tuple-element.58), channel_id=1, source_target_pairs={{0,1},{1,0},{2,3},{3,2},{4,5},{5,4},{6,7},{7,6},{8,9},{9,8},{10,11... | collective-permute-start | bytes 393224 | tf_op jit(solution)/shard_map/ppermute | solution.py:242
  31.8 20.2 %copy-start.6 = (bf16[8,1024,128]{2,1,0:T(8,128)(2,1)S(1)}, bf16[8,1024,128]{2,1,0:T(8,128)(2,1)}, u32[]{:S(2)}) copy-start(bf16[8,1024,128]{2,1,0:T(8,128)(2,1)} %copy-done.5) | copy-start | bytes 6291460
  31.8 11.0 %collective-permute-start.10 = (f32[2,2,128,128]{3,2,1,0:T(8,128)S(1)}, f32[2,2,128,128]{3,2,1,0:T(8,128)S(1)}, u32[]{:S(2)}, u32[]{:S(2)}) collective-permute-start(f32[2,2,128,128]{3,2,1,0:T(8,128)S(1)} %pad_maximum_fusion.rest_4_), channel_id=1, source_target_pairs={{0,8},{8,0},{16,24},{24,16},{32,40},{40,32},{48,56},{56,48},{64,72... | collective-permute-start | bytes 786440 | tf_op jit(solution)/shard_map/ppermute | solution.py:242
  34.1 10.3 %collective-permute-start.11 = (f32[2,2,128,128]{3,2,1,0:T(8,128)S(1)}, f32[2,2,128,128]{3,2,1,0:T(8,128)S(1)}, u32[]{:S(2)}, u32[]{:S(2)}) collective-permute-start(f32[2,2,128,128]{3,2,1,0:T(8,128)S(1)} %pad_maximum_fusion.rest_4_), channel_id=1, source_target_pairs={{0,24},{8,16},{16,8},{24,0},{32,56},{40,48},{48,40},{56,32},{64,88... | collective-permute-start | bytes 786440 | tf_op jit(solution)/shard_map/ppermute | solution.py:242
  36.6 3.4 %collective-permute-start.8 = (f32[1,128,128]{2,1,0:T(8,128)S(1)}, f32[1,128,128]{2,1,0:T(8,128)S(1)}, u32[]{:S(2)}, u32[]{:S(2)}) collective-permute-start(f32[1,128,128]{2,1,0:T(8,128)S(1)} %get-tuple-element.56), channel_id=1, source_target_pairs={{0,2},{1,3},{2,0},{3,1},{4,6},{5,7},{6,4},{7,5},{8,10},{9,11},{10,... | collective-permute-start | bytes 196616 | tf_op jit(solution)/shard_map/ppermute | solution.py:242
  40.0 4.4 %collective-permute-start.9 = (f32[1,128,128]{2,1,0:T(8,128)S(1)}, f32[1,128,128]{2,1,0:T(8,128)S(1)}, u32[]{:S(2)}, u32[]{:S(2)}) collective-permute-start(f32[1,128,128]{2,1,0:T(8,128)S(1)} %add.43), channel_id=1, source_target_pairs={{0,6},{1,7},{2,4},{3,5},{4,2},{5,3},{6,0},{7,1},{8,14},{9,15},{10,... | collective-permute-start | bytes 196616 | tf_op jit(solution)/shard_map/ppermute | solution.py:242
  42.6 15.6 %collective-permute-start.13 = (f32[8,128,128]{2,1,0:T(8,128)S(1)}, f32[8,128,128]{2,1,0:T(8,128)S(1)}, u32[]{:S(2)}, u32[]{:S(2)}) collective-permute-start(f32[8,128,128]{2,1,0:T(8,128)S(1)} %add.41), channel_id=1, source_target_pairs={{0,24},{8,16},{16,8},{24,0},{32,56},{40,48},{48,40},{56,32},{64,88... | collective-permute-start | bytes 1572872 | tf_op jit(solution)/shard_map/ppermute | solution.py:242
  44.4 13.7 %copy-start.4 = (f32[4,128,1024]{2,1,0:T(8,128)S(1)}, f32[4,128,1024]{2,1,0:T(8,128)}, u32[]{:S(2)}) copy-start(f32[4,128,1024]{2,1,0:T(8,128)} %copy-done.3) | copy-start | bytes 6291460
  44.4 3.7 %collective-permute-start.12 = (f32[3,1,128,128]{3,2,1,0:T(8,128)S(1)}, f32[3,1,128,128]{3,2,1,0:T(8,128)S(1)}, u32[]{:S(2)}, u32[]{:S(2)}) collective-permute-start(f32[3,1,128,128]{3,2,1,0:T(8,128)S(1)} %pad_maximum_fusion.1.rest_1_), channel_id=1, source_target_pairs={{0,1},{1,0},{2,3},{3,2},{4,5},{5,4},{6,7},{7,6},{8,9},{9,8},{10,11... | collective-permute-start | bytes 589832 | tf_op jit(solution)/shard_map/ppermute | solution.py:242
  48.2 10.0 %collective-permute-start.14 = (f32[2,2,128,128]{3,2,1,0:T(8,128)S(1)}, f32[2,2,128,128]{3,2,1,0:T(8,128)S(1)}, u32[]{:S(2)}, u32[]{:S(2)}) collective-permute-start(f32[2,2,128,128]{3,2,1,0:T(8,128)S(1)} %collective-permute-done.11.rest_7_), channel_id=1, source_target_pairs={{0,8},{8,0},{16,24},{24,16},{32,40},{40,32},{48,56},{56,48},{64,72... | collective-permute-start | bytes 786440 | tf_op jit(solution)/shard_map/ppermute | solution.py:242
  48.2 13.8 %collective-permute-start.15 = (f32[3,1,128,128]{3,2,1,0:T(8,128)S(1)}, f32[3,1,128,128]{3,2,1,0:T(8,128)S(1)}, u32[]{:S(2)}, u32[]{:S(2)}) collective-permute-start(f32[3,1,128,128]{3,2,1,0:T(8,128)S(1)} %pad_maximum_fusion.1.rest_1_), channel_id=1, source_target_pairs={{0,8},{8,0},{16,24},{24,16},{32,40},{40,32},{48,56},{56,48},{64,72... | collective-permute-start | bytes 589832 | tf_op jit(solution)/shard_map/ppermute | solution.py:242
  49.6 14.5 %collective-permute-start.16 = (f32[3,1,128,128]{3,2,1,0:T(8,128)S(1)}, f32[3,1,128,128]{3,2,1,0:T(8,128)S(1)}, u32[]{:S(2)}, u32[]{:S(2)}) collective-permute-start(f32[3,1,128,128]{3,2,1,0:T(8,128)S(1)} %pad_maximum_fusion.1.rest_1_), channel_id=1, source_target_pairs={{0,16},{8,24},{16,0},{24,8},{32,48},{40,56},{48,32},{56,40},{64,80... | collective-permute-start | bytes 589832 | tf_op jit(solution)/shard_map/ppermute | solution.py:242
  50.3 13.8 %collective-permute-start.17 = (f32[3,1,128,128]{3,2,1,0:T(8,128)S(1)}, f32[3,1,128,128]{3,2,1,0:T(8,128)S(1)}, u32[]{:S(2)}, u32[]{:S(2)}) collective-permute-start(f32[3,1,128,128]{3,2,1,0:T(8,128)S(1)} %pad_maximum_fusion.1.rest_1_), channel_id=1, source_target_pairs={{0,24},{8,16},{16,8},{24,0},{32,56},{40,48},{48,40},{56,32},{64,88... | collective-permute-start | bytes 589832 | tf_op jit(solution)/shard_map/ppermute | solution.py:242
  52.1 1.6 %copy-start.8 = (bf16[8,128,1024]{2,1,0:T(8,128)(2,1)S(1)}, bf16[8,128,1024]{2,1,0:T(8,128)(2,1)}, u32[]{:S(2)}) copy-start(bf16[8,128,1024]{2,1,0:T(8,128)(2,1)} %copy-done.7) | copy-start | bytes 6291460
  64.2 3.4 %collective-permute-start.18 = (f32[3,1,128,128]{3,2,1,0:T(8,128)S(1)}, f32[3,1,128,128]{3,2,1,0:T(8,128)S(1)}, u32[]{:S(2)}, u32[]{:S(2)}) collective-permute-start(f32[3,1,128,128]{3,2,1,0:T(8,128)S(1)} %collective-permute-done.15.rest_2_), channel_id=1, source_target_pairs={{0,1},{1,0},{2,3},{3,2},{4,5},{5,4},{6,7},{7,6},{8,9},{9,8},{10,11... | collective-permute-start | bytes 589832 | tf_op jit(solution)/shard_map/ppermute | solution.py:242
  66.5 1.4 %collective-permute-start.19 = (f32[3,1,128,128]{3,2,1,0:T(8,128)S(1)}, f32[3,1,128,128]{3,2,1,0:T(8,128)S(1)}, u32[]{:S(2)}, u32[]{:S(2)}) collective-permute-start(f32[3,1,128,128]{3,2,1,0:T(8,128)S(1)} %collective-permute-done.16.rest_3_), channel_id=1, source_target_pairs={{0,1},{1,0},{2,3},{3,2},{4,5},{5,4},{6,7},{7,6},{8,9},{9,8},{10,11... | collective-permute-start | bytes 589832 | tf_op jit(solution)/shard_map/ppermute | solution.py:242
  66.5 1.7 %collective-permute-start.20 = (f32[3,1,128,128]{3,2,1,0:T(8,128)S(1)}, f32[3,1,128,128]{3,2,1,0:T(8,128)S(1)}, u32[]{:S(2)}, u32[]{:S(2)}) collective-permute-start(f32[3,1,128,128]{3,2,1,0:T(8,128)S(1)} %collective-permute-done.17.rest_4_), channel_id=1, source_target_pairs={{0,1},{1,0},{2,3},{3,2},{4,5},{5,4},{6,7},{7,6},{8,9},{9,8},{10,11... | collective-permute-start | bytes 589832 | tf_op jit(solution)/shard_map/ppermute | solution.py:242

commit v4 on v3

--- a/solution.py
+++ b/solution.py
@@ -14,7 +14,8 @@
 RING = 4
 CORES = 2
 TILE = 256
-EARLY_HEADS = 4
+EARLY_HEADS = 3
+ROWS = 512
 
 
 def dot(lhs, rhs, dims):
@@ -169,70 +170,70 @@
     total_refs, rest = rest[:count], rest[count:]
     piece_refs, rest = rest[: len(pieces)], rest[len(pieces) :]
     if last:
-        out_ref, split, total_f = rest
+        out_ref, split, result, sent = rest
     else:
         out_ref, split = rest
-    heads, rows, width = query_ref.shape
-
-    @pl.when(pl.program_id(0) == 0)
-    def _():
-        for ref, (piece_bits, first_head) in zip(piece_refs, pieces):
-            base = first_head(place())
-            for at, bit in enumerate(piece_bits):
-                for head in range(ref.shape[1]):
-                    bucket = ref[at, head]
-                    high = bucket.astype(jnp.bfloat16)
-                    low = (bucket - high.astype(jnp.float32)).astype(jnp.bfloat16)
-                    where = bits.index(bit) * width
-                    split[base + head, where : where + width, :width] = high
-                    split[base + head, where : where + width, width:] = low
+    heads, length, width = query_ref.shape
+    for ref, (piece_bits, first_head) in zip(piece_refs, pieces):
+        base = first_head(place())
+        for at, bit in enumerate(piece_bits):
+            for head in range(ref.shape[1]):
+                bucket = ref[at, head]
+                high = bucket.astype(jnp.bfloat16)
+                low = (bucket - high.astype(jnp.float32)).astype(jnp.bfloat16)
+                where = bits.index(bit) * width
+                split[base + head, where : where + width, :width] = high
+                split[base + head, where : where + width, width:] = low
 
     block = place()[2]
     held = [(ref, at) for ref in total_refs for at in range(ref.shape[0])]
-    for head in range(heads):
-        query = query_ref[head]
-        products = dot(split[head], jnp.concatenate([query, query], 1), NT)
-        ref, at = held[head]
-        total = ref[at]
-        for at, bit in enumerate(bits):
-            gain = weight_ref[local_bits + 1 + bit, head : head + 1, :]
-            gain = jnp.where((block >> bit) & 1 == 1, gain, 0.0)
-            total = total + products[at * width : (at + 1) * width, :] * gain
+    copies = []
+    for start in range(0, length, ROWS):
+        cols = slice(start, start + ROWS)
+        done = []
+        for head in range(heads):
+            query = query_ref[head, cols, :]
+            products = dot(split[head], jnp.concatenate([query, query], 1), NT)
+            ref, at = held[head]
+            total = ref[at, :, cols]
+            for at, bit in enumerate(bits):
+                gain = weight_ref[local_bits + 1 + bit, head : head + 1, cols]
+                gain = jnp.where((block >> bit) & 1 == 1, gain, 0.0)
+                total = total + products[at * width : (at + 1) * width, :] * gain
+            if last:
+                mean = jnp.sum(total * total, 0, keepdims=True) * (1.0 / width)
+                done.append((total * lax.rsqrt(mean + EPSILON)).astype(jnp.bfloat16).T)
+            else:
+                out_ref[head, :, cols] = total
         if last:
-            mean = jnp.sum(total * total, 0, keepdims=True) * (1.0 / width)
-            total = total * lax.rsqrt(mean + EPSILON)
-            total_f[pl.ds(head, rows, stride=heads), :] = total.T
-        else:
-            out_ref[head] = total
-    if last:
-        out_ref[...] = total_f[...].reshape(rows, heads, width).astype(jnp.bfloat16)
-
-
-def far_part(query, level_weight, totals, bits, pieces, last, rows=512):
+            result[cols] = jnp.swapaxes(jnp.stack(done), 0, 1)
+            copies.append(
+                pltpu.make_async_copy(result.at[cols], out_ref.at[cols], sent.at[len(copies)])
+            )
+            copies[-1].start()
+    for copy in copies:
+        copy.wait()
+
+
+def far_part(query, level_weight, totals, bits, pieces, last):
     heads, length, width = query.shape
-    levels = level_weight.shape[0]
     local_bits = length.bit_length() - 1
-    flat = pl.BlockSpec((heads, width, rows), lambda i: (0, 0, i))
     plan = (len(totals), bits, [(piece_bits, first) for _, piece_bits, first in pieces])
     arrays = [array for array, _, _ in pieces]
     scratch = [pltpu.VMEM((heads, len(bits) * width, 2 * width), jnp.bfloat16)]
     if last:
-        scratch.append(pltpu.VMEM((rows * heads, width), jnp.float32))
+        scratch.append(pltpu.VMEM((length, heads, width), jnp.bfloat16))
+        scratch.append(pltpu.SemaphoreType.DMA((length // ROWS,)))
+    held = pl.BlockSpec(memory_space=pltpu.VMEM)
     return pl.pallas_call(
         functools.partial(far_kernel, plan, last, local_bits),
-        grid=(length // rows,),
-        in_specs=[
-            pl.BlockSpec((heads, rows, width), lambda i: (0, i, 0)),
-            pl.BlockSpec((levels, heads, rows), lambda i: (0, 0, i)),
-        ]
-        + [pl.BlockSpec((t.shape[0], width, rows), lambda i: (0, 0, i)) for t in totals]
-        + [pl.BlockSpec(a.shape, lambda i: (0, 0, 0, 0)) for a in arrays],
-        out_specs=pl.BlockSpec((rows, heads, width), lambda i: (i, 0, 0)) if last else flat,
+        in_specs=[held] * (2 + len(totals) + len(arrays)),
+        out_specs=pl.BlockSpec(memory_space=pl.ANY) if last else held,
         out_shape=jax.ShapeDtypeStruct((length, heads, width), jnp.bfloat16)
         if last
         else jax.ShapeDtypeStruct((heads, width, length), jnp.float32),
         scratch_shapes=scratch,
-        compiler_params=params(20 if last else 24),
+        compiler_params=params(24),
         cost_estimate=cost(1e6, 0.01),
         name="finish" if last else "far",
     )(query, level_weight, *totals, *arrays)
@@ -301,10 +302,9 @@
     chip_second = apart_x(chip + chip_first, 3)
     chip_second = tied(chip_second, inner[1], inner[3])
     outer = jnp.stack([jnp.where(core == 0, mine, theirs), chip_first, chip_second])
-    outer_facing = [other_core(outer)]
     outer = [outer] + [apart_y(outer, m) for m in (1, 2, 3)]
-    inner[2] = apart_y(tied(inner[3], outer_facing[0]), 1)
-    near.append(near_of(EARLY_HEADS, heads - EARLY_HEADS, outer_facing[0], 12))
+    inner[2] = apart_y(inner[3], 1)
+    near.append(near_of(EARLY_HEADS, heads - EARLY_HEADS, outer[0], 12))
 
     def owner(m):
         return lambda p: (p[0] ^ m) * share
@@ -312,8 +312,8 @@
     pieces = [(first[None], (0,), lambda p: 0), (second[None], (1,), lambda p: 0)]
     pieces += [(inner[m], (2, 3), owner(m)) for m in range(RING)]
     total = far_part(query_h, level_weight, near, (0, 1, 2, 3), pieces, False)
-    outer = [outer[0]] + tied(outer[1:], total)
-    outer_facing += [other_core(piece) for piece in outer[1:]]
+    outer = tied(outer, total)
+    outer_facing = [other_core(piece) for piece in outer]
     pieces = [(outer[m], (4, 5, 6), lambda p, m=m: owner(m)(p) + p[1]) for m in range(RING)]
     pieces += [
         (outer_facing[m], (4, 5, 6), lambda p, m=m: owner(m)(p) + 1 - p[1]) for m in range(RING)

time: 73.2 us -> 70.6 us (0.964)
  starting transfers between devices: 27.3 us -> 25.2 us
  Pallas kernels: 23.5 us -> 21.6 us
  waiting for transfers between devices: 11.3 us -> 12.7 us
    ppermute x21, starting transfers between devices: 27.3 us -> 25.2 us  [along(): lax.ppermute(value, axis, [(i, hop(i)) for i in range(lax.axis_size(axis))])]
    pallas_call x2, Pallas kernels: 8.4 us -> 6.47 us  [far_part(): pl.pallas_call(functools.partial(far_kernel, plan, last, local_bits), in_...]
    ppermute x21, waiting for transfers between devices: 11.3 us -> 12.7 us  [along(): lax.ppermute(value, axis, [(i, hop(i)) for i in range(lax.axis_size(axis))])]
  transfers between devices with their start and end apart: 21 -> 21, of which waited for: 9 -> 11; matrix products, arithmetic and copies ran while one was open for 4% -> 4% of each run, Pallas kernels for 21% -> 20%
where the time goes in v4:
time: 70.6 us; the launch traced here: 70.3 us
  starting transfers between devices  25.2 us (36%)
  Pallas kernels  21.6 us (31%)
  waiting for transfers between devices  12.7 us (18%)
  local copies, waits for them, and re-layouts  7.59 us (11%)
  other arithmetic  2.86 us (4%)
    ppermute x21, starting transfers between devices, along(): lax.ppermute(value, axis, [(i, hop(i)) for i in range(lax.axis_size(axis))])  25.2 us
    ppermute x21, waiting for transfers between devices, along(): lax.ppermute(value, axis, [(i, hop(i)) for i in range(lax.axis_size(axis))])  12.7 us
    pallas_call x2, Pallas kernels, near_part(): pl.pallas_call(functools.partial(near_kernel, first), grid=(count,), in_s...  8.99 us
    unnamed x22, local copies, waits for them, and re-layouts  7.59 us
    pallas_call x2, Pallas kernels, far_part(): pl.pallas_call(functools.partial(far_kernel, plan, last, local_bits), in_...  6.47 us
    pallas_call x1, Pallas kernels, states(): pl.pallas_call(state_kernel, grid=(length // rows,), in_specs=[part, part...  3.83 us
    pallas_call x1, Pallas kernels, by_head(): pl.pallas_call(layout_kernel, grid=(length // rows,), in_specs=[part] * 3...  2.3 us
  transfers between devices with their start and end apart: 21, of which 11 were waited for; matrix products, arithmetic and copies ran while one was open for 4% of the time, Pallas kernels for 20%

profile of v4, /device:TPU:1, one launch (start us, length us, event | category | flops | bytes accessed | tf_op | source)
XLA Modules:
  0.0 70.3 jit_solution(16652660464045733197)
XLA Ops:
  0.0 3.8 %states.1 = (f32[8,128,128]{2,1,0:T(8,128)}, f32[2,128,128]{2,1,0:T(8,128)}, f32[2,128,128]{2,1,0:T(8,128)}, f32[2,128,128]{2,1,0:T(8,128)}, f32[2,128,128]{2,1,0:T(8,128)}) custom-call(bf16[1024,8,128]{2,1,0:T(8,128)(2,1)} %key_ref.3, bf16[1024,8,128]{2,1,0:T(8,128)(2,1)} %value_ref.3), custom_call_target="tpu_custom_call" | custom-call | flops 300000000 | bytes 5242880 | tf_op jit(solution)/shard_map/states/pallas_call | solution.py:65
  3.8 2.1 %collective-permute-start = (f32[2,128,128]{2,1,0:T(8,128)}, f32[2,128,128]{2,1,0:T(8,128)S(1)}, u32[]{:S(2)}, u32[]{:S(2)}) collective-permute-start(f32[2,128,128]{2,1,0:T(8,128)} %get-tuple-element.36), channel_id=1, source_target_pairs={{0,8},{8,0},{16,24},{24,16},{32,40},{40,32},{48,56},{56,48},{64,72... | collective-permute-start | bytes 393224 | tf_op jit(solution)/shard_map/ppermute | solution.py:243
  6.0 2.6 %collective-permute-start.1 = (f32[2,128,128]{2,1,0:T(8,128)}, f32[2,128,128]{2,1,0:T(8,128)S(1)}, u32[]{:S(2)}, u32[]{:S(2)}) collective-permute-start(f32[2,128,128]{2,1,0:T(8,128)} %get-tuple-element.37), channel_id=1, source_target_pairs={{0,16},{8,24},{16,0},{24,8},{32,48},{40,56},{48,32},{56,40},{64,80... | collective-permute-start | bytes 393224 | tf_op jit(solution)/shard_map/ppermute | solution.py:243
  8.6 0.0 collective-permute-start.2
  8.6 0.0 collective-permute-start.7
  8.6 1.6 %copy-done.1 = bf16[1024,8,128]{2,1,0:T(8,128)(2,1)S(1)} copy-done((bf16[1024,8,128]{2,1,0:T(8,128)(2,1)S(1)}, bf16[1024,8,128]{2,1,0:T(8,128)(2,1)}, u32[]{:S(2)}) %copy-start.1) | copy-done | bytes 2097176
  10.3 1.6 %copy-done.2 = bf16[1024,8,128]{2,1,0:T(8,128)(2,1)S(1)} copy-done((bf16[1024,8,128]{2,1,0:T(8,128)(2,1)S(1)}, bf16[1024,8,128]{2,1,0:T(8,128)(2,1)}, u32[]{:S(2)}) %copy-start.2) | copy-done | bytes 2097176
  11.9 1.6 %copy-done.9 = bf16[1024,8,128]{2,1,0:T(8,128)(2,1)S(1)} copy-done((bf16[1024,8,128]{2,1,0:T(8,128)(2,1)S(1)}, bf16[1024,8,128]{2,1,0:T(8,128)(2,1)}, u32[]{:S(2)}) %copy-start.9) | copy-done | bytes 2097176
  13.5 2.3 %by_head.1 = (bf16[8,1024,128]{2,1,0:T(8,128)(2,1)S(1)}, bf16[8,1024,128]{2,1,0:T(8,128)(2,1)S(1)}, bf16[8,128,1024]{2,1,0:T(8,128)(2,1)S(1)}) custom-call(bf16[1024,8,128]{2,1,0:T(8,128)(2,1)S(1)} %copy-done.9, bf16[1024,8,128]{2,1,0:T(8,128)(2,1)S(1)} %copy-done.1, bf16[1024,8,128]{2,1,0:T(8,128)(2,1)S(1)} %copy-done.2), custom_call_target="tpu_custom_call" | custom-call | flops 1000000 | bytes 10485 | tf_op jit(solution)/shard_map/by_head/pallas_call | solution.py:91
  15.8 0.0 copy-start.3
  15.8 0.0 copy-start.5
  15.8 0.0 collective-permute-done
  15.8 0.0 collective-permute-done.1
  15.8 1.2 %collective-permute-done.2 = f32[2,128,128]{2,1,0:T(8,128)S(1)} collective-permute-done((f32[2,128,128]{2,1,0:T(8,128)}, f32[2,128,128]{2,1,0:T(8,128)S(1)}, u32[]{:S(2)}, u32[]{:S(2)}) %collective-permute-start.2) | collective-permute-done | bytes 131104 | tf_op jit(solution)/shard_map/ppermute | solution.py:243
  17.0 0.0 copy-done.10
  17.0 1.7 %collective-permute-start.3 = (f32[2,128,128]{2,1,0:T(8,128)S(1)}, f32[2,128,128]{2,1,0:T(8,128)S(1)}, u32[]{:S(2)}, u32[]{:S(2)}) collective-permute-start(f32[2,128,128]{2,1,0:T(8,128)S(1)} %add_add_fusion.1.tie_ref), channel_id=1, source_target_pairs={{0,32},{8,40},{16,48},{24,56},{32,0},{40,8},{48,16},{56,24},{64,96... | collective-permute-start | bytes 393224 | tf_op jit(solution)/shard_map/ppermute | solution.py:243
  18.8 3.3 %collective-permute-start.4 = (f32[2,128,128]{2,1,0:T(8,128)S(1)}, f32[2,128,128]{2,1,0:T(8,128)S(1)}, u32[]{:S(2)}, u32[]{:S(2)}) collective-permute-start(f32[2,128,128]{2,1,0:T(8,128)S(1)} %add_add_fusion.1.tie_ref), channel_id=1, source_target_pairs={{0,64},{8,72},{16,80},{24,88},{32,96},{40,104},{48,112},{56,120},{... | collective-permute-start | bytes 393224 | tf_op jit(solution)/shard_map/ppermute | solution.py:243
  22.1 0.0 collective-permute-start.5
  22.1 0.0 copy-done
  22.1 3.4 %near.2.rest_0_ = f32[3,128,1024]{2,1,0:T(8,128)S(1)} custom-call(bf16[8,1024,128]{2,1,0:T(8,128)(2,1)S(1)} %get-tuple-element.32.query_ref, bf16[8,1024,128]{2,1,0:T(8,128)(2,1)S(1)} %get-tuple-element.33.key_ref, bf16[8,128,1024]{2,1,0:T(8,128)(2,1)S(1)} %get-tuple-element.34.value_ref, f32[20,8,1024]{2,1,0:T(8,128)S(1)} %bitcast.10, ...), custom_call_target="tpu_custom_call" | custom-call | flops 1000000 | bytes 10485 | tf_op jit(solution)/shard_map/near/pallas_call | solution.py:150
  25.5 0.0 copy-done.3
  25.5 0.0 copy-done.5
  25.5 0.0 copy-start.7
  25.5 1.1 %copy-done.7 = f32[3,128,1024]{2,1,0:T(8,128)} copy-done((f32[3,128,1024]{2,1,0:T(8,128)}, f32[3,128,1024]{2,1,0:T(8,128)S(1)}, u32[]{:S(2)}) %copy-start.7) | copy-done | bytes 1572888
  26.6 0.0 collective-permute-done.3
  26.6 0.3 collective-permute-done.4
  26.9 2.8 %collective-permute-done.5 = f32[2,128,128]{2,1,0:T(8,128)S(1)} collective-permute-done((f32[2,128,128]{2,1,0:T(8,128)S(1)}, f32[2,128,128]{2,1,0:T(8,128)S(1)}, u32[]{:S(2)}, u32[]{:S(2)}) %collective-permute-start.5) | collective-permute-done | bytes 131104 | tf_op jit(solution)/shard_map/ppermute | solution.py:243
  29.7 0.7 add_bitcast_fusion
  30.4 1.5 %collective-permute-start.6 = (f32[2,128,128]{2,1,0:T(8,128)}, f32[2,128,128]{2,1,0:T(8,128)}, u32[]{:S(2)}, u32[]{:S(2)}) collective-permute-start(f32[2,128,128]{2,1,0:T(8,128)} %get-tuple-element.58), channel_id=1, source_target_pairs={{0,1},{1,0},{2,3},{3,2},{4,5},{5,4},{6,7},{7,6},{8,9},{9,8},{10,11... | collective-permute-start | bytes 393224 | tf_op jit(solution)/shard_map/ppermute | solution.py:243
  31.9 0.1 collective-permute-start.10
  32.0 0.0 collective-permute-done.7
  32.0 1.2 %add.41 = f32[8,128,128]{2,1,0:T(8,128)S(1)} add(f32[8,128,128]{2,1,0:T(8,128)} %get-tuple-element.30, f32[8,128,128]{2,1,0:T(8,128)S(1)} %collective-permute-done.7) | non-fusion elementwise | flops 131072 | bytes 1572864 | tf_op jit(solution)/shard_map/add | solution.py:291
  33.2 0.0 collective-permute-done.6
  33.2 0.9 %select_bitcast_fusion = (f32[1,1,128,128]{3,2,1,0:T(8,128)S(1)}, f32[1,128,128]{2,1,0:T(8,128)S(1)}) fusion(f32[2,128,128]{2,1,0:T(8,128)} %collective-permute-done.6, s32[]{:T(128)S(6)} %select_n.13, f32[2,128,128]{2,1,0:T(8,128)} %get-tuple-element.58, pred[]{:T(512)S(6)} %eq.3), kind=kLoop, calls=%fused_computation.5 | loop fusion | flops 32768 | bytes 262149 | tf_op jit(solution)/shard_map/stack | solution.py:304
  34.1 2.5 %collective-permute-start.11 = (f32[2,2,128,128]{3,2,1,0:T(8,128)S(1)}, f32[2,2,128,128]{3,2,1,0:T(8,128)S(1)}, u32[]{:S(2)}, u32[]{:S(2)}) collective-permute-start(f32[2,2,128,128]{3,2,1,0:T(8,128)S(1)} %pad_maximum_fusion.rest_4_), channel_id=1, source_target_pairs={{0,24},{8,16},{16,8},{24,0},{32,56},{40,48},{48,40},{56,32},{64,88... | collective-permute-start | bytes 786440 | tf_op jit(solution)/shard_map/ppermute | solution.py:243
  36.6 0.3 collective-permute-start.12
  36.9 1.2 %collective-permute-start.8 = (f32[1,128,128]{2,1,0:T(8,128)S(1)}, f32[1,128,128]{2,1,0:T(8,128)S(1)}, u32[]{:S(2)}, u32[]{:S(2)}) collective-permute-start(f32[1,128,128]{2,1,0:T(8,128)S(1)} %get-tuple-element.56), channel_id=1, source_target_pairs={{0,2},{1,3},{2,0},{3,1},{4,6},{5,7},{6,4},{7,5},{8,10},{9,11},{10,... | collective-permute-start | bytes 196616 | tf_op jit(solution)/shard_map/ppermute | solution.py:243
  38.1 2.2 %collective-permute-done.8 = f32[1,128,128]{2,1,0:T(8,128)S(1)} collective-permute-done((f32[1,128,128]{2,1,0:T(8,128)S(1)}, f32[1,128,128]{2,1,0:T(8,128)S(1)}, u32[]{:S(2)}, u32[]{:S(2)}) %collective-permute-start.8) | collective-permute-done | bytes 65568 | tf_op jit(solution)/shard_map/ppermute | solution.py:243
  40.3 2.6 %collective-permute-start.9 = (f32[1,128,128]{2,1,0:T(8,128)S(1)}, f32[1,128,128]{2,1,0:T(8,128)S(1)}, u32[]{:S(2)}, u32[]{:S(2)}) collective-permute-start(f32[1,128,128]{2,1,0:T(8,128)S(1)} %add.43), channel_id=1, source_target_pairs={{0,6},{1,7},{2,4},{3,5},{4,2},{5,3},{6,0},{7,1},{8,14},{9,15},{10,... | collective-permute-start | bytes 196616 | tf_op jit(solution)/shard_map/ppermute | solution.py:243
  42.9 0.0 collective-permute-done.10.rest_5_
  42.9 2.1 %collective-permute-done.9 = f32[1,128,128]{2,1,0:T(8,128)S(1)} collective-permute-done((f32[1,128,128]{2,1,0:T(8,128)S(1)}, f32[1,128,128]{2,1,0:T(8,128)S(1)}, u32[]{:S(2)}, u32[]{:S(2)}) %collective-permute-start.9) | collective-permute-done | bytes 65568 | tf_op jit(solution)/shard_map/ppermute | solution.py:243
  45.0 0.0 collective-permute-done.11.rest_7_
  45.0 0.0 collective-permute-start.13
  45.0 1.5 %collective-permute-start.14 = (f32[3,1,128,128]{3,2,1,0:T(8,128)S(1)}, f32[3,1,128,128]{3,2,1,0:T(8,128)S(1)}, u32[]{:S(2)}, u32[]{:S(2)}) collective-permute-start(f32[3,1,128,128]{3,2,1,0:T(8,128)S(1)} %pad_maximum_fusion.1.tie_ref.rest_1_), channel_id=1, source_target_pairs={{0,8},{8,0},{16,24},{24,16},{32,40},{40,32},{48,56},{56,48},{64,72... | collective-permute-start | bytes 589832 | tf_op jit(solution)/shard_map/ppermute | solution.py:243
  46.6 2.2 %collective-permute-start.15 = (f32[3,1,128,128]{3,2,1,0:T(8,128)S(1)}, f32[3,1,128,128]{3,2,1,0:T(8,128)S(1)}, u32[]{:S(2)}, u32[]{:S(2)}) collective-permute-start(f32[3,1,128,128]{3,2,1,0:T(8,128)S(1)} %pad_maximum_fusion.1.tie_ref.rest_1_), channel_id=1, source_target_pairs={{0,16},{8,24},{16,0},{24,8},{32,48},{40,56},{48,32},{56,40},{64,80... | collective-permute-start | bytes 589832 | tf_op jit(solution)/shard_map/ppermute | solution.py:243
  48.8 0.3 collective-permute-start.16
  49.1 1.6 %copy-done.6 = bf16[8,128,1024]{2,1,0:T(8,128)(2,1)S(1)} copy-done((bf16[8,128,1024]{2,1,0:T(8,128)(2,1)S(1)}, bf16[8,128,1024]{2,1,0:T(8,128)(2,1)}, u32[]{:S(2)}) %copy-start.6) | copy-done | bytes 2097176
  50.7 5.6 %near.3.rest_1_ = f32[5,128,1024]{2,1,0:T(8,128)S(1)} custom-call(bf16[8,1024,128]{2,1,0:T(8,128)(2,1)S(1)} %get-tuple-element.32.query_ref, bf16[8,1024,128]{2,1,0:T(8,128)(2,1)S(1)} %copy-done.4, bf16[8,128,1024]{2,1,0:T(8,128)(2,1)S(1)} %copy-done.6, f32[20,8,1024]{2,1,0:T(8,128)S(1)} %bitcast.11, f32[3,1,128,128]{3,2,1,0:T(8,128)S(1)} %pad_maximum_fusion.1.tie_ref.rest_1_), custom_call_target="tpu_custom_call" | custom-call | flops 1000000 | bytes 10485 | tf_op jit(solution)/shard_map/near/pallas_call | solution.py:150
  56.3 0.0 collective-permute-done.13.rest_6_
  56.3 0.0 collective-permute-done.12
  56.3 0.0 copy-done.8
  56.3 2.7 %far.1.rest_0_ = f32[8,128,1024]{2,1,0:T(8,128)S(1)} custom-call(bf16[8,1024,128]{2,1,0:T(8,128)(2,1)S(1)} %get-tuple-element.32.query_ref, f32[20,8,1024]{2,1,0:T(8,128)S(1)} %bitcast.12, f32[3,128,1024]{2,1,0:T(8,128)S(1)} %copy-done.8, f32[5,128,1024]{2,1,0:T(8,128)S(1)} %near.3.rest_1_, f32[1,8,128,128]{3,2,1,0:T(8,128)S(1)} %bitcast.14, ...), custom_call_target="tpu_custom_call" | custom-call | flops 1000000 | bytes 10485 | tf_op jit(solution)/shard_map/far/pallas_call | solution.py:228
  59.0 0.0 collective-permute-done.14.rest_2_
  59.0 1.5 %collective-permute-done.15.rest_3_ = f32[3,1,128,128]{3,2,1,0:T(8,128)S(1)} collective-permute-done((f32[3,1,128,128]{3,2,1,0:T(8,128)S(1)}, f32[3,1,128,128]{3,2,1,0:T(8,128)S(1)}, u32[]{:S(2)}, u32[]{:S(2)}) %collective-permute-start.15) | collective-permute-done | bytes 196640 | tf_op jit(solution)/shard_map/ppermute | solution.py:243
  60.5 1.0 %collective-permute-done.16.rest_4_ = f32[3,1,128,128]{3,2,1,0:T(8,128)S(1)} collective-permute-done((f32[3,1,128,128]{3,2,1,0:T(8,128)S(1)}, f32[3,1,128,128]{3,2,1,0:T(8,128)S(1)}, u32[]{:S(2)}, u32[]{:S(2)}) %collective-permute-start.16) | collective-permute-done | bytes 196640 | tf_op jit(solution)/shard_map/ppermute | solution.py:243
  61.6 2.7 %collective-permute-start.17 = (f32[3,1,128,128]{3,2,1,0:T(8,128)S(1)}, f32[3,1,128,128]{3,2,1,0:T(8,128)S(1)}, u32[]{:S(2)}, u32[]{:S(2)}) collective-permute-start(f32[3,1,128,128]{3,2,1,0:T(8,128)S(1)} %pad_maximum_fusion.1.tie_ref.rest_1_), channel_id=1, source_target_pairs={{0,1},{1,0},{2,3},{3,2},{4,5},{5,4},{6,7},{7,6},{8,9},{9,8},{10,11... | collective-permute-start | bytes 589832 | tf_op jit(solution)/shard_map/ppermute | solution.py:243
  64.3 0.0 collective-permute-start.18
  64.3 0.5 collective-permute-start.19
  64.8 0.0 collective-permute-start.20
  64.8 0.6 collective-permute-done.17.rest_5_
  65.4 0.4 collective-permute-done.18.rest_6_
  65.8 0.3 collective-permute-done.19.rest_7_
  66.0 0.3 collective-permute-done.20.rest_8_
  66.3 3.8 %finish.1 = bf16[1024,8,128]{2,1,0:T(8,128)(2,1)} custom-call(bf16[8,1024,128]{2,1,0:T(8,128)(2,1)S(1)} %get-tuple-element.32.query_ref, f32[20,8,1024]{2,1,0:T(8,128)S(1)} %bitcast.13, f32[8,128,1024]{2,1,0:T(8,128)S(1)} %far.1.rest_0_, f32[3,1,128,128]{3,2,1,0:T(8,128)S(1)} %pad_maximum_fusion.1.tie_ref.rest_1_, ...), custom_call_target="tpu_custom_call" | custom-call | flops 1000000 | bytes 10485 | tf_op jit(solution)/shard_map/finish/pallas_call | solution.py:228
  (13 shorter events, 0.1 us)
Async XLA Ops:
  3.8 11.9 %collective-permute-start = (f32[2,128,128]{2,1,0:T(8,128)}, f32[2,128,128]{2,1,0:T(8,128)S(1)}, u32[]{:S(2)}, u32[]{:S(2)}) collective-permute-start(f32[2,128,128]{2,1,0:T(8,128)} %get-tuple-element.36), channel_id=1, source_target_pairs={{0,8},{8,0},{16,24},{24,16},{32,40},{40,32},{48,56},{56,48},{64,72... | collective-permute-start | bytes 393224 | tf_op jit(solution)/shard_map/ppermute | solution.py:243
  6.0 9.8 %collective-permute-start.1 = (f32[2,128,128]{2,1,0:T(8,128)}, f32[2,128,128]{2,1,0:T(8,128)S(1)}, u32[]{:S(2)}, u32[]{:S(2)}) collective-permute-start(f32[2,128,128]{2,1,0:T(8,128)} %get-tuple-element.37), channel_id=1, source_target_pairs={{0,16},{8,24},{16,0},{24,8},{32,48},{40,56},{48,32},{56,40},{64,80... | collective-permute-start | bytes 393224 | tf_op jit(solution)/shard_map/ppermute | solution.py:243
  8.6 8.4 %collective-permute-start.2 = (f32[2,128,128]{2,1,0:T(8,128)}, f32[2,128,128]{2,1,0:T(8,128)S(1)}, u32[]{:S(2)}, u32[]{:S(2)}) collective-permute-start(f32[2,128,128]{2,1,0:T(8,128)} %get-tuple-element.38), channel_id=1, source_target_pairs={{0,24},{8,16},{16,8},{24,0},{32,56},{40,48},{48,40},{56,32},{64,88... | collective-permute-start | bytes 393224 | tf_op jit(solution)/shard_map/ppermute | solution.py:243
  8.6 13.5 %copy-start = (f32[8,20,1024]{2,0,1:T(8,128)S(1)}, f32[8,20,1024]{2,0,1:T(8,128)}, u32[]{:S(2)}) copy-start(f32[8,20,1024]{2,0,1:T(8,128)} %param.7) | copy-start | bytes 1966084
  8.6 23.4 %collective-permute-start.7 = (f32[8,128,128]{2,1,0:T(8,128)}, f32[8,128,128]{2,1,0:T(8,128)S(1)}, u32[]{:S(2)}, u32[]{:S(2)}) collective-permute-start(f32[8,128,128]{2,1,0:T(8,128)} %get-tuple-element.30), channel_id=1, source_target_pairs={{0,8},{8,0},{16,24},{24,16},{32,40},{40,32},{48,56},{56,48},{64,72... | collective-permute-start | bytes 1572872 | tf_op jit(solution)/shard_map/ppermute | solution.py:243
  8.6 1.7 %copy-start.1 = (bf16[1024,8,128]{2,1,0:T(8,128)(2,1)S(1)}, bf16[1024,8,128]{2,1,0:T(8,128)(2,1)}, u32[]{:S(2)}) copy-start(bf16[1024,8,128]{2,1,0:T(8,128)(2,1)} %key_ref.3) | copy-start | bytes 6291460
  10.3 1.6 %copy-start.2 = (bf16[1024,8,128]{2,1,0:T(8,128)(2,1)S(1)}, bf16[1024,8,128]{2,1,0:T(8,128)(2,1)}, u32[]{:S(2)}) copy-start(bf16[1024,8,128]{2,1,0:T(8,128)(2,1)} %value_ref.3) | copy-start | bytes 6291460
  11.9 1.6 %copy-start.9 = (bf16[1024,8,128]{2,1,0:T(8,128)(2,1)S(1)}, bf16[1024,8,128]{2,1,0:T(8,128)(2,1)}, u32[]{:S(2)}) copy-start(bf16[1024,8,128]{2,1,0:T(8,128)(2,1)} %query_ref) | copy-start | bytes 6291460
  13.5 3.6 %copy-start.10 = (f32[2,128,128]{2,1,0:T(8,128)S(1)}, f32[2,128,128]{2,1,0:T(8,128)}, u32[]{:S(2)}) copy-start(f32[2,128,128]{2,1,0:T(8,128)} %get-tuple-element.39) | copy-start | bytes 393220
  15.8 9.7 %copy-start.3 = (bf16[8,1024,128]{2,1,0:T(8,128)(2,1)}, bf16[8,1024,128]{2,1,0:T(8,128)(2,1)S(1)}, u32[]{:S(2)}) copy-start(bf16[8,1024,128]{2,1,0:T(8,128)(2,1)S(1)} %get-tuple-element.33.key_ref) | copy-start | bytes 6291460
  15.8 9.7 %copy-start.5 = (bf16[8,128,1024]{2,1,0:T(8,128)(2,1)}, bf16[8,128,1024]{2,1,0:T(8,128)(2,1)S(1)}, u32[]{:S(2)}) copy-start(bf16[8,128,1024]{2,1,0:T(8,128)(2,1)S(1)} %get-tuple-element.34.value_ref) | copy-start | bytes 6291460
  17.0 9.6 %collective-permute-start.3 = (f32[2,128,128]{2,1,0:T(8,128)S(1)}, f32[2,128,128]{2,1,0:T(8,128)S(1)}, u32[]{:S(2)}, u32[]{:S(2)}) collective-permute-start(f32[2,128,128]{2,1,0:T(8,128)S(1)} %add_add_fusion.1.tie_ref), channel_id=1, source_target_pairs={{0,32},{8,40},{16,48},{24,56},{32,0},{40,8},{48,16},{56,24},{64,96... | collective-permute-start | bytes 393224 | tf_op jit(solution)/shard_map/ppermute | solution.py:243
  18.8 8.1 %collective-permute-start.4 = (f32[2,128,128]{2,1,0:T(8,128)S(1)}, f32[2,128,128]{2,1,0:T(8,128)S(1)}, u32[]{:S(2)}, u32[]{:S(2)}) collective-permute-start(f32[2,128,128]{2,1,0:T(8,128)S(1)} %add_add_fusion.1.tie_ref), channel_id=1, source_target_pairs={{0,64},{8,72},{16,80},{24,88},{32,96},{40,104},{48,112},{56,120},{... | collective-permute-start | bytes 393224 | tf_op jit(solution)/shard_map/ppermute | solution.py:243
  22.1 7.6 %collective-permute-start.5 = (f32[2,128,128]{2,1,0:T(8,128)S(1)}, f32[2,128,128]{2,1,0:T(8,128)S(1)}, u32[]{:S(2)}, u32[]{:S(2)}) collective-permute-start(f32[2,128,128]{2,1,0:T(8,128)S(1)} %add_add_fusion.1.tie_ref), channel_id=1, source_target_pairs={{0,96},{8,104},{16,112},{24,120},{32,64},{40,72},{48,80},{56,88},{... | collective-permute-start | bytes 393224 | tf_op jit(solution)/shard_map/ppermute | solution.py:243
  25.5 1.1 %copy-start.7 = (f32[3,128,1024]{2,1,0:T(8,128)}, f32[3,128,1024]{2,1,0:T(8,128)S(1)}, u32[]{:S(2)}) copy-start(f32[3,128,1024]{2,1,0:T(8,128)S(1)} %near.2.rest_0_) | copy-start | bytes 4718596
  30.4 2.8 %collective-permute-start.6 = (f32[2,128,128]{2,1,0:T(8,128)}, f32[2,128,128]{2,1,0:T(8,128)}, u32[]{:S(2)}, u32[]{:S(2)}) collective-permute-start(f32[2,128,128]{2,1,0:T(8,128)} %get-tuple-element.58), channel_id=1, source_target_pairs={{0,1},{1,0},{2,3},{3,2},{4,5},{5,4},{6,7},{7,6},{8,9},{9,8},{10,11... | collective-permute-start | bytes 393224 | tf_op jit(solution)/shard_map/ppermute | solution.py:243
  31.9 17.2 %copy-start.4 = (bf16[8,1024,128]{2,1,0:T(8,128)(2,1)S(1)}, bf16[8,1024,128]{2,1,0:T(8,128)(2,1)}, u32[]{:S(2)}) copy-start(bf16[8,1024,128]{2,1,0:T(8,128)(2,1)} %copy-done.3) | copy-start | bytes 6291460
  31.9 11.0 %collective-permute-start.10 = (f32[2,2,128,128]{3,2,1,0:T(8,128)S(1)}, f32[2,2,128,128]{3,2,1,0:T(8,128)S(1)}, u32[]{:S(2)}, u32[]{:S(2)}) collective-permute-start(f32[2,2,128,128]{3,2,1,0:T(8,128)S(1)} %pad_maximum_fusion.rest_4_), channel_id=1, source_target_pairs={{0,8},{8,0},{16,24},{24,16},{32,40},{40,32},{48,56},{56,48},{64,72... | collective-permute-start | bytes 786440 | tf_op jit(solution)/shard_map/ppermute | solution.py:243
  34.1 10.9 %collective-permute-start.11 = (f32[2,2,128,128]{3,2,1,0:T(8,128)S(1)}, f32[2,2,128,128]{3,2,1,0:T(8,128)S(1)}, u32[]{:S(2)}, u32[]{:S(2)}) collective-permute-start(f32[2,2,128,128]{3,2,1,0:T(8,128)S(1)} %pad_maximum_fusion.rest_4_), channel_id=1, source_target_pairs={{0,24},{8,16},{16,8},{24,0},{32,56},{40,48},{48,40},{56,32},{64,88... | collective-permute-start | bytes 786440 | tf_op jit(solution)/shard_map/ppermute | solution.py:243
  36.6 19.7 %collective-permute-start.12 = (f32[8,128,128]{2,1,0:T(8,128)S(1)}, f32[8,128,128]{2,1,0:T(8,128)S(1)}, u32[]{:S(2)}, u32[]{:S(2)}) collective-permute-start(f32[8,128,128]{2,1,0:T(8,128)S(1)} %add.41), channel_id=1, source_target_pairs={{0,24},{8,16},{16,8},{24,0},{32,56},{40,48},{48,40},{56,32},{64,88... | collective-permute-start | bytes 1572872 | tf_op jit(solution)/shard_map/ppermute | solution.py:243
  36.9 3.4 %collective-permute-start.8 = (f32[1,128,128]{2,1,0:T(8,128)S(1)}, f32[1,128,128]{2,1,0:T(8,128)S(1)}, u32[]{:S(2)}, u32[]{:S(2)}) collective-permute-start(f32[1,128,128]{2,1,0:T(8,128)S(1)} %get-tuple-element.56), channel_id=1, source_target_pairs={{0,2},{1,3},{2,0},{3,1},{4,6},{5,7},{6,4},{7,5},{8,10},{9,11},{10,... | collective-permute-start | bytes 196616 | tf_op jit(solution)/shard_map/ppermute | solution.py:243
  40.3 4.7 %collective-permute-start.9 = (f32[1,128,128]{2,1,0:T(8,128)S(1)}, f32[1,128,128]{2,1,0:T(8,128)S(1)}, u32[]{:S(2)}, u32[]{:S(2)}) collective-permute-start(f32[1,128,128]{2,1,0:T(8,128)S(1)} %add.43), channel_id=1, source_target_pairs={{0,6},{1,7},{2,4},{3,5},{4,2},{5,3},{6,0},{7,1},{8,14},{9,15},{10,... | collective-permute-start | bytes 196616 | tf_op jit(solution)/shard_map/ppermute | solution.py:243
  45.0 11.3 %collective-permute-start.13 = (f32[2,2,128,128]{3,2,1,0:T(8,128)S(1)}, f32[2,2,128,128]{3,2,1,0:T(8,128)S(1)}, u32[]{:S(2)}, u32[]{:S(2)}) collective-permute-start(f32[2,2,128,128]{3,2,1,0:T(8,128)S(1)} %collective-permute-done.11.rest_7_), channel_id=1, source_target_pairs={{0,8},{8,0},{16,24},{24,16},{32,40},{40,32},{48,56},{56,48},{64,72... | collective-permute-start | bytes 786440 | tf_op jit(solution)/shard_map/ppermute | solution.py:243
  45.0 14.0 %collective-permute-start.14 = (f32[3,1,128,128]{3,2,1,0:T(8,128)S(1)}, f32[3,1,128,128]{3,2,1,0:T(8,128)S(1)}, u32[]{:S(2)}, u32[]{:S(2)}) collective-permute-start(f32[3,1,128,128]{3,2,1,0:T(8,128)S(1)} %pad_maximum_fusion.1.tie_ref.rest_1_), channel_id=1, source_target_pairs={{0,8},{8,0},{16,24},{24,16},{32,40},{40,32},{48,56},{56,48},{64,72... | collective-permute-start | bytes 589832 | tf_op jit(solution)/shard_map/ppermute | solution.py:243
  46.6 13.9 %collective-permute-start.15 = (f32[3,1,128,128]{3,2,1,0:T(8,128)S(1)}, f32[3,1,128,128]{3,2,1,0:T(8,128)S(1)}, u32[]{:S(2)}, u32[]{:S(2)}) collective-permute-start(f32[3,1,128,128]{3,2,1,0:T(8,128)S(1)} %pad_maximum_fusion.1.tie_ref.rest_1_), channel_id=1, source_target_pairs={{0,16},{8,24},{16,0},{24,8},{32,48},{40,56},{48,32},{56,40},{64,80... | collective-permute-start | bytes 589832 | tf_op jit(solution)/shard_map/ppermute | solution.py:243
  48.8 12.8 %collective-permute-start.16 = (f32[3,1,128,128]{3,2,1,0:T(8,128)S(1)}, f32[3,1,128,128]{3,2,1,0:T(8,128)S(1)}, u32[]{:S(2)}, u32[]{:S(2)}) collective-permute-start(f32[3,1,128,128]{3,2,1,0:T(8,128)S(1)} %pad_maximum_fusion.1.tie_ref.rest_1_), channel_id=1, source_target_pairs={{0,24},{8,16},{16,8},{24,0},{32,56},{40,48},{48,40},{56,32},{64,88... | collective-permute-start | bytes 589832 | tf_op jit(solution)/shard_map/ppermute | solution.py:243
  49.1 1.6 %copy-start.6 = (bf16[8,128,1024]{2,1,0:T(8,128)(2,1)S(1)}, bf16[8,128,1024]{2,1,0:T(8,128)(2,1)}, u32[]{:S(2)}) copy-start(bf16[8,128,1024]{2,1,0:T(8,128)(2,1)} %copy-done.5) | copy-start | bytes 6291460
  50.7 5.7 %copy-start.8 = (f32[3,128,1024]{2,1,0:T(8,128)S(1)}, f32[3,128,1024]{2,1,0:T(8,128)}, u32[]{:S(2)}) copy-start(f32[3,128,1024]{2,1,0:T(8,128)} %copy-done.7) | copy-start | bytes 4718596
  61.6 3.8 %collective-permute-start.17 = (f32[3,1,128,128]{3,2,1,0:T(8,128)S(1)}, f32[3,1,128,128]{3,2,1,0:T(8,128)S(1)}, u32[]{:S(2)}, u32[]{:S(2)}) collective-permute-start(f32[3,1,128,128]{3,2,1,0:T(8,128)S(1)} %pad_maximum_fusion.1.tie_ref.rest_1_), channel_id=1, source_target_pairs={{0,1},{1,0},{2,3},{3,2},{4,5},{5,4},{6,7},{7,6},{8,9},{9,8},{10,11... | collective-permute-start | bytes 589832 | tf_op jit(solution)/shard_map/ppermute | solution.py:243
  64.3 1.4 %collective-permute-start.18 = (f32[3,1,128,128]{3,2,1,0:T(8,128)S(1)}, f32[3,1,128,128]{3,2,1,0:T(8,128)S(1)}, u32[]{:S(2)}, u32[]{:S(2)}) collective-permute-start(f32[3,1,128,128]{3,2,1,0:T(8,128)S(1)} %collective-permute-done.14.rest_2_), channel_id=1, source_target_pairs={{0,1},{1,0},{2,3},{3,2},{4,5},{5,4},{6,7},{7,6},{8,9},{9,8},{10,11... | collective-permute-start | bytes 589832 | tf_op jit(solution)/shard_map/ppermute | solution.py:243
  64.3 1.7 %collective-permute-start.19 = (f32[3,1,128,128]{3,2,1,0:T(8,128)S(1)}, f32[3,1,128,128]{3,2,1,0:T(8,128)S(1)}, u32[]{:S(2)}, u32[]{:S(2)}) collective-permute-start(f32[3,1,128,128]{3,2,1,0:T(8,128)S(1)} %collective-permute-done.15.rest_3_), channel_id=1, source_target_pairs={{0,1},{1,0},{2,3},{3,2},{4,5},{5,4},{6,7},{7,6},{8,9},{9,8},{10,11... | collective-permute-start | bytes 589832 | tf_op jit(solution)/shard_map/ppermute | solution.py:243
  64.8 1.5 %collective-permute-start.20 = (f32[3,1,128,128]{3,2,1,0:T(8,128)S(1)}, f32[3,1,128,128]{3,2,1,0:T(8,128)S(1)}, u32[]{:S(2)}, u32[]{:S(2)}) collective-permute-start(f32[3,1,128,128]{3,2,1,0:T(8,128)S(1)} %collective-permute-done.16.rest_4_), channel_id=1, source_target_pairs={{0,1},{1,0},{2,3},{3,2},{4,5},{5,4},{6,7},{7,6},{8,9},{9,8},{10,11... | collective-permute-start | bytes 589832 | tf_op jit(solution)/shard_map/ppermute | solution.py:243

commit v5 on v4

--- a/solution.py
+++ b/solution.py
@@ -14,7 +14,7 @@
 RING = 4
 CORES = 2
 TILE = 256
-EARLY_HEADS = 3
+EARLY_HEADS = 4
 ROWS = 512
 
 
@@ -188,8 +188,9 @@
     block = place()[2]
     held = [(ref, at) for ref in total_refs for at in range(ref.shape[0])]
     copies = []
-    for start in range(0, length, ROWS):
-        cols = slice(start, start + ROWS)
+    rows = ROWS // 2 if last else ROWS
+    for start in range(0, length, rows):
+        cols = slice(start, start + rows)
         done = []
         for head in range(heads):
             query = query_ref[head, cols, :]
@@ -223,7 +224,7 @@
     scratch = [pltpu.VMEM((heads, len(bits) * width, 2 * width), jnp.bfloat16)]
     if last:
         scratch.append(pltpu.VMEM((length, heads, width), jnp.bfloat16))
-        scratch.append(pltpu.SemaphoreType.DMA((length // ROWS,)))
+        scratch.append(pltpu.SemaphoreType.DMA((2 * length // ROWS,)))
     held = pl.BlockSpec(memory_space=pltpu.VMEM)
     return pl.pallas_call(
         functools.partial(far_kernel, plan, last, local_bits),
@@ -288,9 +289,8 @@
     sums = tied(sums, near[0])
     ring_z = sum(sums[1:], sums[0])
     facing = other_core(ring_z)
-    pair = state + tied(first, ring_z)
-    second = apart_y(pair, 3)
-    facing = tied(facing, pair)
+    first = tied(first, ring_z)
+    facing = tied(facing, first)
     near_buckets = jnp.stack(buckets_of_ring(sums))
     inner = [near_buckets, apart_y(near_buckets, 1), None, None]
 
@@ -298,7 +298,10 @@
     theirs = lax.dynamic_slice_in_dim(facing, core, 1, 0)
     chip = mine + theirs
     chip_first = apart_x(chip, 1)
+    pair = state + tied(first, chip)
+    second = apart_y(pair, 3)
     inner[3] = apart_y(tied(near_buckets, chip), 3)
+    chip_first = tied(chip_first, pair)
     chip_second = apart_x(chip + chip_first, 3)
     chip_second = tied(chip_second, inner[1], inner[3])
     outer = jnp.stack([jnp.where(core == 0, mine, theirs), chip_first, chip_second])

time: 70.6 us -> 70.6 us (level)
  starting transfers between devices: 25.2 us -> 26.3 us
  waiting for transfers between devices: 12.7 us -> 11.6 us
    ppermute x21, starting transfers between devices: 25.2 us -> 26.3 us  [along(): lax.ppermute(value, axis, [(i, hop(i)) for i in range(lax.axis_size(axis))])]
    ppermute x21, waiting for transfers between devices: 12.7 us -> 11.6 us  [along(): lax.ppermute(value, axis, [(i, hop(i)) for i in range(lax.axis_size(axis))])]
  transfers between devices with their start and end apart: 21 -> 21, of which waited for: 11 -> 10; matrix products, arithmetic and copies ran while one was open for 4% -> 4% of each run, Pallas kernels for 20% -> 20%
where the time goes in v5:
time: 70.6 us; the launch traced here: 70.3 us
  starting transfers between devices  26.3 us (37%)
  Pallas kernels  21.5 us (30%)
  waiting for transfers between devices  11.6 us (16%)
  local copies, waits for them, and re-layouts  7.76 us (11%)
  other arithmetic  2.71 us (4%)
    ppermute x21, starting transfers between devices, along(): lax.ppermute(value, axis, [(i, hop(i)) for i in range(lax.axis_size(axis))])  26.3 us
    ppermute x21, waiting for transfers between devices, along(): lax.ppermute(value, axis, [(i, hop(i)) for i in range(lax.axis_size(axis))])  11.6 us
    pallas_call x2, Pallas kernels, near_part(): pl.pallas_call(functools.partial(near_kernel, first), grid=(count,), in_s...  8.99 us
    unnamed x22, local copies, waits for them, and re-layouts  7.76 us
    pallas_call x2, Pallas kernels, far_part(): pl.pallas_call(functools.partial(far_kernel, plan, last, local_bits), in_...  6.45 us
    pallas_call x1, Pallas kernels, states(): pl.pallas_call(state_kernel, grid=(length // rows,), in_specs=[part, part...  3.79 us
    pallas_call x1, Pallas kernels, by_head(): pl.pallas_call(layout_kernel, grid=(length // rows,), in_specs=[part] * 3...  2.3 us
  transfers between devices with their start and end apart: 21, of which 10 were waited for; matrix products, arithmetic and copies ran while one was open for 4% of the time, Pallas kernels for 20%

profile of v5, /device:TPU:1, one launch (start us, length us, event | category | flops | bytes accessed | tf_op | source)
XLA Modules:
  0.0 70.3 jit_solution(8999978169891806455)
XLA Ops:
  0.0 3.8 %states.1 = (f32[8,128,128]{2,1,0:T(8,128)}, f32[2,128,128]{2,1,0:T(8,128)}, f32[2,128,128]{2,1,0:T(8,128)}, f32[2,128,128]{2,1,0:T(8,128)}, f32[2,128,128]{2,1,0:T(8,128)}) custom-call(bf16[1024,8,128]{2,1,0:T(8,128)(2,1)} %key_ref.3, bf16[1024,8,128]{2,1,0:T(8,128)(2,1)} %value_ref.3), custom_call_target="tpu_custom_call" | custom-call | flops 300000000 | bytes 5242880 | tf_op jit(solution)/shard_map/states/pallas_call | solution.py:65
  3.8 2.1 %collective-permute-start = (f32[2,128,128]{2,1,0:T(8,128)}, f32[2,128,128]{2,1,0:T(8,128)S(1)}, u32[]{:S(2)}, u32[]{:S(2)}) collective-permute-start(f32[2,128,128]{2,1,0:T(8,128)} %get-tuple-element.38), channel_id=1, source_target_pairs={{0,8},{8,0},{16,24},{24,16},{32,40},{40,32},{48,56},{56,48},{64,72... | collective-permute-start | bytes 393224 | tf_op jit(solution)/shard_map/ppermute | solution.py:244
  5.9 2.6 %collective-permute-start.1 = (f32[2,128,128]{2,1,0:T(8,128)}, f32[2,128,128]{2,1,0:T(8,128)S(1)}, u32[]{:S(2)}, u32[]{:S(2)}) collective-permute-start(f32[2,128,128]{2,1,0:T(8,128)} %get-tuple-element.39), channel_id=1, source_target_pairs={{0,16},{8,24},{16,0},{24,8},{32,48},{40,56},{48,32},{56,40},{64,80... | collective-permute-start | bytes 393224 | tf_op jit(solution)/shard_map/ppermute | solution.py:244
  8.5 0.0 collective-permute-start.2
  8.5 0.0 collective-permute-start.7
  8.6 1.6 %copy-done.1 = bf16[1024,8,128]{2,1,0:T(8,128)(2,1)S(1)} copy-done((bf16[1024,8,128]{2,1,0:T(8,128)(2,1)S(1)}, bf16[1024,8,128]{2,1,0:T(8,128)(2,1)}, u32[]{:S(2)}) %copy-start.1) | copy-done | bytes 2097176
  10.2 1.6 %copy-done.2 = bf16[1024,8,128]{2,1,0:T(8,128)(2,1)S(1)} copy-done((bf16[1024,8,128]{2,1,0:T(8,128)(2,1)S(1)}, bf16[1024,8,128]{2,1,0:T(8,128)(2,1)}, u32[]{:S(2)}) %copy-start.2) | copy-done | bytes 2097176
  11.8 1.6 %copy-done.9 = bf16[1024,8,128]{2,1,0:T(8,128)(2,1)S(1)} copy-done((bf16[1024,8,128]{2,1,0:T(8,128)(2,1)S(1)}, bf16[1024,8,128]{2,1,0:T(8,128)(2,1)}, u32[]{:S(2)}) %copy-start.9) | copy-done | bytes 2097176
  13.4 2.3 %by_head.1 = (bf16[8,1024,128]{2,1,0:T(8,128)(2,1)S(1)}, bf16[8,1024,128]{2,1,0:T(8,128)(2,1)S(1)}, bf16[8,128,1024]{2,1,0:T(8,128)(2,1)S(1)}) custom-call(bf16[1024,8,128]{2,1,0:T(8,128)(2,1)S(1)} %copy-done.9, bf16[1024,8,128]{2,1,0:T(8,128)(2,1)S(1)} %copy-done.1, bf16[1024,8,128]{2,1,0:T(8,128)(2,1)S(1)} %copy-done.2), custom_call_target="tpu_custom_call" | custom-call | flops 1000000 | bytes 10485 | tf_op jit(solution)/shard_map/by_head/pallas_call | solution.py:91
  15.7 0.0 copy-start.5
  15.7 0.0 copy-start.7
  15.7 0.0 collective-permute-done
  15.7 0.0 collective-permute-done.1
  15.8 1.2 %collective-permute-done.2 = f32[2,128,128]{2,1,0:T(8,128)S(1)} collective-permute-done((f32[2,128,128]{2,1,0:T(8,128)}, f32[2,128,128]{2,1,0:T(8,128)S(1)}, u32[]{:S(2)}, u32[]{:S(2)}) %collective-permute-start.2) | collective-permute-done | bytes 131104 | tf_op jit(solution)/shard_map/ppermute | solution.py:244
  17.0 0.0 copy-done.10
  17.0 1.7 %collective-permute-start.3 = (f32[2,128,128]{2,1,0:T(8,128)S(1)}, f32[2,128,128]{2,1,0:T(8,128)S(1)}, u32[]{:S(2)}, u32[]{:S(2)}) collective-permute-start(f32[2,128,128]{2,1,0:T(8,128)S(1)} %add_add_fusion.1.tie_ref), channel_id=1, source_target_pairs={{0,32},{8,40},{16,48},{24,56},{32,0},{40,8},{48,16},{56,24},{64,96... | collective-permute-start | bytes 393224 | tf_op jit(solution)/shard_map/ppermute | solution.py:244
  18.7 3.3 %collective-permute-start.4 = (f32[2,128,128]{2,1,0:T(8,128)S(1)}, f32[2,128,128]{2,1,0:T(8,128)S(1)}, u32[]{:S(2)}, u32[]{:S(2)}) collective-permute-start(f32[2,128,128]{2,1,0:T(8,128)S(1)} %add_add_fusion.1.tie_ref), channel_id=1, source_target_pairs={{0,64},{8,72},{16,80},{24,88},{32,96},{40,104},{48,112},{56,120},{... | collective-permute-start | bytes 393224 | tf_op jit(solution)/shard_map/ppermute | solution.py:244
  22.0 0.0 collective-permute-start.5
  22.0 0.0 copy-done
  22.0 4.5 %near.2.rest_0_ = f32[4,128,1024]{2,1,0:T(8,128)S(1)} custom-call(bf16[8,1024,128]{2,1,0:T(8,128)(2,1)S(1)} %get-tuple-element.34.query_ref, bf16[8,1024,128]{2,1,0:T(8,128)(2,1)S(1)} %get-tuple-element.35.key_ref, bf16[8,128,1024]{2,1,0:T(8,128)(2,1)S(1)} %get-tuple-element.36.value_ref, f32[20,8,1024]{2,1,0:T(8,128)S(1)} %bitcast.10, ...), custom_call_target="tpu_custom_call" | custom-call | flops 1000000 | bytes 10485 | tf_op jit(solution)/shard_map/near/pallas_call | solution.py:150
  26.5 0.0 copy-done.5
  26.5 0.0 copy-done.7
  26.5 0.0 copy-start.3
  26.6 1.3 %copy-done.3 = f32[4,128,1024]{2,1,0:T(8,128)} copy-done((f32[4,128,1024]{2,1,0:T(8,128)}, f32[4,128,1024]{2,1,0:T(8,128)S(1)}, u32[]{:S(2)}) %copy-start.3) | copy-done | bytes 2097176
  27.9 0.0 collective-permute-done.3
  27.9 0.0 collective-permute-done.4
  27.9 1.8 %collective-permute-done.5 = f32[2,128,128]{2,1,0:T(8,128)S(1)} collective-permute-done((f32[2,128,128]{2,1,0:T(8,128)S(1)}, f32[2,128,128]{2,1,0:T(8,128)S(1)}, u32[]{:S(2)}, u32[]{:S(2)}) %collective-permute-start.5) | collective-permute-done | bytes 131104 | tf_op jit(solution)/shard_map/ppermute | solution.py:244
  29.7 0.7 add_bitcast_fusion
  30.3 1.5 %collective-permute-start.6 = (f32[2,128,128]{2,1,0:T(8,128)}, f32[2,128,128]{2,1,0:T(8,128)}, u32[]{:S(2)}, u32[]{:S(2)}) collective-permute-start(f32[2,128,128]{2,1,0:T(8,128)} %get-tuple-element.62), channel_id=1, source_target_pairs={{0,1},{1,0},{2,3},{3,2},{4,5},{5,4},{6,7},{7,6},{8,9},{9,8},{10,11... | collective-permute-start | bytes 393224 | tf_op jit(solution)/shard_map/ppermute | solution.py:244
  31.9 0.1 collective-permute-start.10
  31.9 0.0 collective-permute-done.7
  32.0 1.2 %collective-permute-done.6 = f32[2,128,128]{2,1,0:T(8,128)} collective-permute-done((f32[2,128,128]{2,1,0:T(8,128)}, f32[2,128,128]{2,1,0:T(8,128)}, u32[]{:S(2)}, u32[]{:S(2)}) %collective-permute-start.6) | collective-permute-done | bytes 131104 | tf_op jit(solution)/shard_map/ppermute | solution.py:244
  33.2 0.9 %select_bitcast_fusion = (f32[1,1,128,128]{3,2,1,0:T(8,128)S(1)}, f32[1,128,128]{2,1,0:T(8,128)S(1)}) fusion(f32[2,128,128]{2,1,0:T(8,128)} %collective-permute-done.6, s32[]{:T(128)S(6)} %select_n.13, f32[2,128,128]{2,1,0:T(8,128)} %get-tuple-element.62, pred[]{:T(512)S(6)} %eq.3), kind=kLoop, calls=%fused_computation.5 | loop fusion | flops 32768 | bytes 262149 | tf_op jit(solution)/shard_map/stack | solution.py:307
  34.0 1.4 %collective-permute-start.11 = (f32[2,2,128,128]{3,2,1,0:T(8,128)S(1)}, f32[2,2,128,128]{3,2,1,0:T(8,128)S(1)}, u32[]{:S(2)}, u32[]{:S(2)}) collective-permute-start(f32[2,2,128,128]{3,2,1,0:T(8,128)S(1)} %pad_maximum_fusion.rest_4_), channel_id=1, source_target_pairs={{0,24},{8,16},{16,8},{24,0},{32,56},{40,48},{48,40},{56,32},{64,88... | collective-permute-start | bytes 786440 | tf_op jit(solution)/shard_map/ppermute | solution.py:244
  35.5 1.1 %add.42 = f32[8,128,128]{2,1,0:T(8,128)S(1)} add(f32[8,128,128]{2,1,0:T(8,128)} %get-tuple-element.32, f32[8,128,128]{2,1,0:T(8,128)S(1)} %collective-permute-done.7) | non-fusion elementwise | flops 131072 | bytes 1572864 | tf_op jit(solution)/shard_map/add | solution.py:301
  36.6 1.4 %collective-permute-start.12 = (f32[8,128,128]{2,1,0:T(8,128)S(1)}, f32[8,128,128]{2,1,0:T(8,128)S(1)}, u32[]{:S(2)}, u32[]{:S(2)}) collective-permute-start(f32[8,128,128]{2,1,0:T(8,128)S(1)} %add.42), channel_id=1, source_target_pairs={{0,24},{8,16},{16,8},{24,0},{32,56},{40,48},{48,40},{56,32},{64,88... | collective-permute-start | bytes 1572872 | tf_op jit(solution)/shard_map/ppermute | solution.py:244
  38.0 1.2 %collective-permute-start.8 = (f32[1,128,128]{2,1,0:T(8,128)S(1)}, f32[1,128,128]{2,1,0:T(8,128)S(1)}, u32[]{:S(2)}, u32[]{:S(2)}) collective-permute-start(f32[1,128,128]{2,1,0:T(8,128)S(1)} %get-tuple-element.60), channel_id=1, source_target_pairs={{0,2},{1,3},{2,0},{3,1},{4,6},{5,7},{6,4},{7,5},{8,10},{9,11},{10,... | collective-permute-start | bytes 196616 | tf_op jit(solution)/shard_map/ppermute | solution.py:244
  39.2 2.2 %collective-permute-done.8 = f32[1,128,128]{2,1,0:T(8,128)S(1)} collective-permute-done((f32[1,128,128]{2,1,0:T(8,128)S(1)}, f32[1,128,128]{2,1,0:T(8,128)S(1)}, u32[]{:S(2)}, u32[]{:S(2)}) %collective-permute-start.8) | collective-permute-done | bytes 65568 | tf_op jit(solution)/shard_map/ppermute | solution.py:244
  41.4 2.6 %collective-permute-start.9 = (f32[1,128,128]{2,1,0:T(8,128)S(1)}, f32[1,128,128]{2,1,0:T(8,128)S(1)}, u32[]{:S(2)}, u32[]{:S(2)}) collective-permute-start(f32[1,128,128]{2,1,0:T(8,128)S(1)} %add.43), channel_id=1, source_target_pairs={{0,6},{1,7},{2,4},{3,5},{4,2},{5,3},{6,0},{7,1},{8,14},{9,15},{10,... | collective-permute-start | bytes 196616 | tf_op jit(solution)/shard_map/ppermute | solution.py:244
  44.0 0.0 collective-permute-done.10.rest_5_
  44.0 2.1 %collective-permute-done.9 = f32[1,128,128]{2,1,0:T(8,128)S(1)} collective-permute-done((f32[1,128,128]{2,1,0:T(8,128)S(1)}, f32[1,128,128]{2,1,0:T(8,128)S(1)}, u32[]{:S(2)}, u32[]{:S(2)}) %collective-permute-start.9) | collective-permute-done | bytes 65568 | tf_op jit(solution)/shard_map/ppermute | solution.py:244
  46.1 0.0 collective-permute-done.11.rest_7_
  46.1 0.0 collective-permute-start.13
  46.1 0.0 copy-start.4
  46.1 1.5 %collective-permute-start.14 = (f32[3,1,128,128]{3,2,1,0:T(8,128)S(1)}, f32[3,1,128,128]{3,2,1,0:T(8,128)S(1)}, u32[]{:S(2)}, u32[]{:S(2)}) collective-permute-start(f32[3,1,128,128]{3,2,1,0:T(8,128)S(1)} %pad_maximum_fusion.1.tie_ref.rest_1_), channel_id=1, source_target_pairs={{0,8},{8,0},{16,24},{24,16},{32,40},{40,32},{48,56},{56,48},{64,72... | collective-permute-start | bytes 589832 | tf_op jit(solution)/shard_map/ppermute | solution.py:244
  47.7 1.2 %collective-permute-start.15 = (f32[3,1,128,128]{3,2,1,0:T(8,128)S(1)}, f32[3,1,128,128]{3,2,1,0:T(8,128)S(1)}, u32[]{:S(2)}, u32[]{:S(2)}) collective-permute-start(f32[3,1,128,128]{3,2,1,0:T(8,128)S(1)} %pad_maximum_fusion.1.tie_ref.rest_1_), channel_id=1, source_target_pairs={{0,16},{8,24},{16,0},{24,8},{32,48},{40,56},{48,32},{56,40},{64,80... | collective-permute-start | bytes 589832 | tf_op jit(solution)/shard_map/ppermute | solution.py:244
  48.8 1.3 %collective-permute-start.16 = (f32[3,1,128,128]{3,2,1,0:T(8,128)S(1)}, f32[3,1,128,128]{3,2,1,0:T(8,128)S(1)}, u32[]{:S(2)}, u32[]{:S(2)}) collective-permute-start(f32[3,1,128,128]{3,2,1,0:T(8,128)S(1)} %pad_maximum_fusion.1.tie_ref.rest_1_), channel_id=1, source_target_pairs={{0,24},{8,16},{16,8},{24,0},{32,56},{40,48},{48,40},{56,32},{64,88... | collective-permute-start | bytes 589832 | tf_op jit(solution)/shard_map/ppermute | solution.py:244
  50.2 1.6 %copy-done.8 = bf16[8,128,1024]{2,1,0:T(8,128)(2,1)S(1)} copy-done((bf16[8,128,1024]{2,1,0:T(8,128)(2,1)S(1)}, bf16[8,128,1024]{2,1,0:T(8,128)(2,1)}, u32[]{:S(2)}) %copy-start.8) | copy-done | bytes 2097176
  51.8 4.5 %near.3.rest_1_ = f32[4,128,1024]{2,1,0:T(8,128)S(1)} custom-call(bf16[8,1024,128]{2,1,0:T(8,128)(2,1)S(1)} %get-tuple-element.34.query_ref, bf16[8,1024,128]{2,1,0:T(8,128)(2,1)S(1)} %copy-done.6, bf16[8,128,1024]{2,1,0:T(8,128)(2,1)S(1)} %copy-done.8, f32[20,8,1024]{2,1,0:T(8,128)S(1)} %bitcast.11, f32[3,1,128,128]{3,2,1,0:T(8,128)S(1)} %pad_maximum_fusion.1.tie_ref.rest_1_), custom_call_target="tpu_custom_call" | custom-call | flops 1000000 | bytes 10485 | tf_op jit(solution)/shard_map/near/pallas_call | solution.py:150
  56.3 0.0 collective-permute-done.13.rest_6_
  56.3 0.0 collective-permute-done.12
  56.3 2.7 %far.1.rest_0_ = f32[8,128,1024]{2,1,0:T(8,128)S(1)} custom-call(bf16[8,1024,128]{2,1,0:T(8,128)(2,1)S(1)} %get-tuple-element.34.query_ref, f32[20,8,1024]{2,1,0:T(8,128)S(1)} %bitcast.12, f32[4,128,1024]{2,1,0:T(8,128)S(1)} %copy-done.4, f32[4,128,1024]{2,1,0:T(8,128)S(1)} %near.3.rest_1_, f32[1,8,128,128]{3,2,1,0:T(8,128)S(1)} %bitcast.14, ...), custom_call_target="tpu_custom_call" | custom-call | flops 1000000 | bytes 10485 | tf_op jit(solution)/shard_map/far/pallas_call | solution.py:229
  59.0 0.0 collective-permute-done.14.rest_2_
  59.0 1.5 %collective-permute-done.15.rest_3_ = f32[3,1,128,128]{3,2,1,0:T(8,128)S(1)} collective-permute-done((f32[3,1,128,128]{3,2,1,0:T(8,128)S(1)}, f32[3,1,128,128]{3,2,1,0:T(8,128)S(1)}, u32[]{:S(2)}, u32[]{:S(2)}) %collective-permute-start.15) | collective-permute-done | bytes 196640 | tf_op jit(solution)/shard_map/ppermute | solution.py:244
  60.5 0.0 collective-permute-done.16.rest_4_
  60.5 3.8 %collective-permute-start.17 = (f32[3,1,128,128]{3,2,1,0:T(8,128)S(1)}, f32[3,1,128,128]{3,2,1,0:T(8,128)S(1)}, u32[]{:S(2)}, u32[]{:S(2)}) collective-permute-start(f32[3,1,128,128]{3,2,1,0:T(8,128)S(1)} %pad_maximum_fusion.1.tie_ref.rest_1_), channel_id=1, source_target_pairs={{0,1},{1,0},{2,3},{3,2},{4,5},{5,4},{6,7},{7,6},{8,9},{9,8},{10,11... | collective-permute-start | bytes 589832 | tf_op jit(solution)/shard_map/ppermute | solution.py:244
  64.3 0.0 collective-permute-start.18
  64.3 0.5 collective-permute-start.19
  64.8 0.0 collective-permute-start.20
  64.8 0.6 collective-permute-done.17.rest_5_
  65.4 0.4 collective-permute-done.18.rest_6_
  65.8 0.3 collective-permute-done.19.rest_7_
  66.0 0.3 collective-permute-done.20.rest_8_
  66.3 3.8 %finish.1 = bf16[1024,8,128]{2,1,0:T(8,128)(2,1)} custom-call(bf16[8,1024,128]{2,1,0:T(8,128)(2,1)S(1)} %get-tuple-element.34.query_ref, f32[20,8,1024]{2,1,0:T(8,128)S(1)} %bitcast.13, f32[8,128,1024]{2,1,0:T(8,128)S(1)} %far.1.rest_0_, f32[3,1,128,128]{3,2,1,0:T(8,128)S(1)} %pad_maximum_fusion.1.tie_ref.rest_1_, ...), custom_call_target="tpu_custom_call" | custom-call | flops 1000000 | bytes 10485 | tf_op jit(solution)/shard_map/finish/pallas_call | solution.py:229
  (13 shorter events, 0.1 us)
Async XLA Ops:
  3.8 11.9 %collective-permute-start = (f32[2,128,128]{2,1,0:T(8,128)}, f32[2,128,128]{2,1,0:T(8,128)S(1)}, u32[]{:S(2)}, u32[]{:S(2)}) collective-permute-start(f32[2,128,128]{2,1,0:T(8,128)} %get-tuple-element.38), channel_id=1, source_target_pairs={{0,8},{8,0},{16,24},{24,16},{32,40},{40,32},{48,56},{56,48},{64,72... | collective-permute-start | bytes 393224 | tf_op jit(solution)/shard_map/ppermute | solution.py:244
  5.9 9.8 %collective-permute-start.1 = (f32[2,128,128]{2,1,0:T(8,128)}, f32[2,128,128]{2,1,0:T(8,128)S(1)}, u32[]{:S(2)}, u32[]{:S(2)}) collective-permute-start(f32[2,128,128]{2,1,0:T(8,128)} %get-tuple-element.39), channel_id=1, source_target_pairs={{0,16},{8,24},{16,0},{24,8},{32,48},{40,56},{48,32},{56,40},{64,80... | collective-permute-start | bytes 393224 | tf_op jit(solution)/shard_map/ppermute | solution.py:244
  8.5 8.4 %collective-permute-start.2 = (f32[2,128,128]{2,1,0:T(8,128)}, f32[2,128,128]{2,1,0:T(8,128)S(1)}, u32[]{:S(2)}, u32[]{:S(2)}) collective-permute-start(f32[2,128,128]{2,1,0:T(8,128)} %get-tuple-element.40), channel_id=1, source_target_pairs={{0,24},{8,16},{16,8},{24,0},{32,56},{40,48},{48,40},{56,32},{64,88... | collective-permute-start | bytes 393224 | tf_op jit(solution)/shard_map/ppermute | solution.py:244
  8.5 13.5 %copy-start = (f32[8,20,1024]{2,0,1:T(8,128)S(1)}, f32[8,20,1024]{2,0,1:T(8,128)}, u32[]{:S(2)}) copy-start(f32[8,20,1024]{2,0,1:T(8,128)} %param.7) | copy-start | bytes 1966084
  8.5 23.4 %collective-permute-start.7 = (f32[8,128,128]{2,1,0:T(8,128)}, f32[8,128,128]{2,1,0:T(8,128)S(1)}, u32[]{:S(2)}, u32[]{:S(2)}) collective-permute-start(f32[8,128,128]{2,1,0:T(8,128)} %get-tuple-element.32), channel_id=1, source_target_pairs={{0,8},{8,0},{16,24},{24,16},{32,40},{40,32},{48,56},{56,48},{64,72... | collective-permute-start | bytes 1572872 | tf_op jit(solution)/shard_map/ppermute | solution.py:244
  8.6 1.7 %copy-start.1 = (bf16[1024,8,128]{2,1,0:T(8,128)(2,1)S(1)}, bf16[1024,8,128]{2,1,0:T(8,128)(2,1)}, u32[]{:S(2)}) copy-start(bf16[1024,8,128]{2,1,0:T(8,128)(2,1)} %key_ref.3) | copy-start | bytes 6291460
  10.2 1.6 %copy-start.2 = (bf16[1024,8,128]{2,1,0:T(8,128)(2,1)S(1)}, bf16[1024,8,128]{2,1,0:T(8,128)(2,1)}, u32[]{:S(2)}) copy-start(bf16[1024,8,128]{2,1,0:T(8,128)(2,1)} %value_ref.3) | copy-start | bytes 6291460
  11.8 1.6 %copy-start.9 = (bf16[1024,8,128]{2,1,0:T(8,128)(2,1)S(1)}, bf16[1024,8,128]{2,1,0:T(8,128)(2,1)}, u32[]{:S(2)}) copy-start(bf16[1024,8,128]{2,1,0:T(8,128)(2,1)} %query_ref) | copy-start | bytes 6291460
  13.4 3.6 %copy-start.10 = (f32[2,128,128]{2,1,0:T(8,128)S(1)}, f32[2,128,128]{2,1,0:T(8,128)}, u32[]{:S(2)}) copy-start(f32[2,128,128]{2,1,0:T(8,128)} %get-tuple-element.41) | copy-start | bytes 393220
  15.7 10.8 %copy-start.5 = (bf16[8,1024,128]{2,1,0:T(8,128)(2,1)}, bf16[8,1024,128]{2,1,0:T(8,128)(2,1)S(1)}, u32[]{:S(2)}) copy-start(bf16[8,1024,128]{2,1,0:T(8,128)(2,1)S(1)} %get-tuple-element.35.key_ref) | copy-start | bytes 6291460
  15.7 10.8 %copy-start.7 = (bf16[8,128,1024]{2,1,0:T(8,128)(2,1)}, bf16[8,128,1024]{2,1,0:T(8,128)(2,1)S(1)}, u32[]{:S(2)}) copy-start(bf16[8,128,1024]{2,1,0:T(8,128)(2,1)S(1)} %get-tuple-element.36.value_ref) | copy-start | bytes 6291460
  17.0 10.9 %collective-permute-start.3 = (f32[2,128,128]{2,1,0:T(8,128)S(1)}, f32[2,128,128]{2,1,0:T(8,128)S(1)}, u32[]{:S(2)}, u32[]{:S(2)}) collective-permute-start(f32[2,128,128]{2,1,0:T(8,128)S(1)} %add_add_fusion.1.tie_ref), channel_id=1, source_target_pairs={{0,32},{8,40},{16,48},{24,56},{32,0},{40,8},{48,16},{56,24},{64,96... | collective-permute-start | bytes 393224 | tf_op jit(solution)/shard_map/ppermute | solution.py:244
  18.7 9.2 %collective-permute-start.4 = (f32[2,128,128]{2,1,0:T(8,128)S(1)}, f32[2,128,128]{2,1,0:T(8,128)S(1)}, u32[]{:S(2)}, u32[]{:S(2)}) collective-permute-start(f32[2,128,128]{2,1,0:T(8,128)S(1)} %add_add_fusion.1.tie_ref), channel_id=1, source_target_pairs={{0,64},{8,72},{16,80},{24,88},{32,96},{40,104},{48,112},{56,120},{... | collective-permute-start | bytes 393224 | tf_op jit(solution)/shard_map/ppermute | solution.py:244
  22.0 7.6 %collective-permute-start.5 = (f32[2,128,128]{2,1,0:T(8,128)S(1)}, f32[2,128,128]{2,1,0:T(8,128)S(1)}, u32[]{:S(2)}, u32[]{:S(2)}) collective-permute-start(f32[2,128,128]{2,1,0:T(8,128)S(1)} %add_add_fusion.1.tie_ref), channel_id=1, source_target_pairs={{0,96},{8,104},{16,112},{24,120},{32,64},{40,72},{48,80},{56,88},{... | collective-permute-start | bytes 393224 | tf_op jit(solution)/shard_map/ppermute | solution.py:244
  26.5 1.3 %copy-start.3 = (f32[4,128,1024]{2,1,0:T(8,128)}, f32[4,128,1024]{2,1,0:T(8,128)S(1)}, u32[]{:S(2)}) copy-start(f32[4,128,1024]{2,1,0:T(8,128)S(1)} %near.2.rest_0_) | copy-start | bytes 6291460
  30.3 2.8 %collective-permute-start.6 = (f32[2,128,128]{2,1,0:T(8,128)}, f32[2,128,128]{2,1,0:T(8,128)}, u32[]{:S(2)}, u32[]{:S(2)}) collective-permute-start(f32[2,128,128]{2,1,0:T(8,128)} %get-tuple-element.62), channel_id=1, source_target_pairs={{0,1},{1,0},{2,3},{3,2},{4,5},{5,4},{6,7},{7,6},{8,9},{9,8},{10,11... | collective-permute-start | bytes 393224 | tf_op jit(solution)/shard_map/ppermute | solution.py:244
  31.8 18.3 %copy-start.6 = (bf16[8,1024,128]{2,1,0:T(8,128)(2,1)S(1)}, bf16[8,1024,128]{2,1,0:T(8,128)(2,1)}, u32[]{:S(2)}) copy-start(bf16[8,1024,128]{2,1,0:T(8,128)(2,1)} %copy-done.5) | copy-start | bytes 6291460
  31.9 12.1 %collective-permute-start.10 = (f32[2,2,128,128]{3,2,1,0:T(8,128)S(1)}, f32[2,2,128,128]{3,2,1,0:T(8,128)S(1)}, u32[]{:S(2)}, u32[]{:S(2)}) collective-permute-start(f32[2,2,128,128]{3,2,1,0:T(8,128)S(1)} %pad_maximum_fusion.rest_4_), channel_id=1, source_target_pairs={{0,8},{8,0},{16,24},{24,16},{32,40},{40,32},{48,56},{56,48},{64,72... | collective-permute-start | bytes 786440 | tf_op jit(solution)/shard_map/ppermute | solution.py:244
  34.0 12.1 %collective-permute-start.11 = (f32[2,2,128,128]{3,2,1,0:T(8,128)S(1)}, f32[2,2,128,128]{3,2,1,0:T(8,128)S(1)}, u32[]{:S(2)}, u32[]{:S(2)}) collective-permute-start(f32[2,2,128,128]{3,2,1,0:T(8,128)S(1)} %pad_maximum_fusion.rest_4_), channel_id=1, source_target_pairs={{0,24},{8,16},{16,8},{24,0},{32,56},{40,48},{48,40},{56,32},{64,88... | collective-permute-start | bytes 786440 | tf_op jit(solution)/shard_map/ppermute | solution.py:244
  36.6 19.7 %collective-permute-start.12 = (f32[8,128,128]{2,1,0:T(8,128)S(1)}, f32[8,128,128]{2,1,0:T(8,128)S(1)}, u32[]{:S(2)}, u32[]{:S(2)}) collective-permute-start(f32[8,128,128]{2,1,0:T(8,128)S(1)} %add.42), channel_id=1, source_target_pairs={{0,24},{8,16},{16,8},{24,0},{32,56},{40,48},{48,40},{56,32},{64,88... | collective-permute-start | bytes 1572872 | tf_op jit(solution)/shard_map/ppermute | solution.py:244
  38.0 3.4 %collective-permute-start.8 = (f32[1,128,128]{2,1,0:T(8,128)S(1)}, f32[1,128,128]{2,1,0:T(8,128)S(1)}, u32[]{:S(2)}, u32[]{:S(2)}) collective-permute-start(f32[1,128,128]{2,1,0:T(8,128)S(1)} %get-tuple-element.60), channel_id=1, source_target_pairs={{0,2},{1,3},{2,0},{3,1},{4,6},{5,7},{6,4},{7,5},{8,10},{9,11},{10,... | collective-permute-start | bytes 196616 | tf_op jit(solution)/shard_map/ppermute | solution.py:244
  41.4 4.7 %collective-permute-start.9 = (f32[1,128,128]{2,1,0:T(8,128)S(1)}, f32[1,128,128]{2,1,0:T(8,128)S(1)}, u32[]{:S(2)}, u32[]{:S(2)}) collective-permute-start(f32[1,128,128]{2,1,0:T(8,128)S(1)} %add.43), channel_id=1, source_target_pairs={{0,6},{1,7},{2,4},{3,5},{4,2},{5,3},{6,0},{7,1},{8,14},{9,15},{10,... | collective-permute-start | bytes 196616 | tf_op jit(solution)/shard_map/ppermute | solution.py:244
  46.1 10.2 %collective-permute-start.13 = (f32[2,2,128,128]{3,2,1,0:T(8,128)S(1)}, f32[2,2,128,128]{3,2,1,0:T(8,128)S(1)}, u32[]{:S(2)}, u32[]{:S(2)}) collective-permute-start(f32[2,2,128,128]{3,2,1,0:T(8,128)S(1)} %collective-permute-done.11.rest_7_), channel_id=1, source_target_pairs={{0,8},{8,0},{16,24},{24,16},{32,40},{40,32},{48,56},{56,48},{64,72... | collective-permute-start | bytes 786440 | tf_op jit(solution)/shard_map/ppermute | solution.py:244
  46.1 10.2 %copy-start.4 = (f32[4,128,1024]{2,1,0:T(8,128)S(1)}, f32[4,128,1024]{2,1,0:T(8,128)}, u32[]{:S(2)}) copy-start(f32[4,128,1024]{2,1,0:T(8,128)} %copy-done.3) | copy-start | bytes 6291460
  46.1 12.9 %collective-permute-start.14 = (f32[3,1,128,128]{3,2,1,0:T(8,128)S(1)}, f32[3,1,128,128]{3,2,1,0:T(8,128)S(1)}, u32[]{:S(2)}, u32[]{:S(2)}) collective-permute-start(f32[3,1,128,128]{3,2,1,0:T(8,128)S(1)} %pad_maximum_fusion.1.tie_ref.rest_1_), channel_id=1, source_target_pairs={{0,8},{8,0},{16,24},{24,16},{32,40},{40,32},{48,56},{56,48},{64,72... | collective-permute-start | bytes 589832 | tf_op jit(solution)/shard_map/ppermute | solution.py:244
  47.7 12.8 %collective-permute-start.15 = (f32[3,1,128,128]{3,2,1,0:T(8,128)S(1)}, f32[3,1,128,128]{3,2,1,0:T(8,128)S(1)}, u32[]{:S(2)}, u32[]{:S(2)}) collective-permute-start(f32[3,1,128,128]{3,2,1,0:T(8,128)S(1)} %pad_maximum_fusion.1.tie_ref.rest_1_), channel_id=1, source_target_pairs={{0,16},{8,24},{16,0},{24,8},{32,48},{40,56},{48,32},{56,40},{64,80... | collective-permute-start | bytes 589832 | tf_op jit(solution)/shard_map/ppermute | solution.py:244
  48.8 11.7 %collective-permute-start.16 = (f32[3,1,128,128]{3,2,1,0:T(8,128)S(1)}, f32[3,1,128,128]{3,2,1,0:T(8,128)S(1)}, u32[]{:S(2)}, u32[]{:S(2)}) collective-permute-start(f32[3,1,128,128]{3,2,1,0:T(8,128)S(1)} %pad_maximum_fusion.1.tie_ref.rest_1_), channel_id=1, source_target_pairs={{0,24},{8,16},{16,8},{24,0},{32,56},{40,48},{48,40},{56,32},{64,88... | collective-permute-start | bytes 589832 | tf_op jit(solution)/shard_map/ppermute | solution.py:244
  50.2 1.6 %copy-start.8 = (bf16[8,128,1024]{2,1,0:T(8,128)(2,1)S(1)}, bf16[8,128,1024]{2,1,0:T(8,128)(2,1)}, u32[]{:S(2)}) copy-start(bf16[8,128,1024]{2,1,0:T(8,128)(2,1)} %copy-done.7) | copy-start | bytes 6291460
  60.5 4.9 %collective-permute-start.17 = (f32[3,1,128,128]{3,2,1,0:T(8,128)S(1)}, f32[3,1,128,128]{3,2,1,0:T(8,128)S(1)}, u32[]{:S(2)}, u32[]{:S(2)}) collective-permute-start(f32[3,1,128,128]{3,2,1,0:T(8,128)S(1)} %pad_maximum_fusion.1.tie_ref.rest_1_), channel_id=1, source_target_pairs={{0,1},{1,0},{2,3},{3,2},{4,5},{5,4},{6,7},{7,6},{8,9},{9,8},{10,11... | collective-permute-start | bytes 589832 | tf_op jit(solution)/shard_map/ppermute | solution.py:244
  64.3 1.4 %collective-permute-start.18 = (f32[3,1,128,128]{3,2,1,0:T(8,128)S(1)}, f32[3,1,128,128]{3,2,1,0:T(8,128)S(1)}, u32[]{:S(2)}, u32[]{:S(2)}) collective-permute-start(f32[3,1,128,128]{3,2,1,0:T(8,128)S(1)} %collective-permute-done.14.rest_2_), channel_id=1, source_target_pairs={{0,1},{1,0},{2,3},{3,2},{4,5},{5,4},{6,7},{7,6},{8,9},{9,8},{10,11... | collective-permute-start | bytes 589832 | tf_op jit(solution)/shard_map/ppermute | solution.py:244
  64.3 1.7 %collective-permute-start.19 = (f32[3,1,128,128]{3,2,1,0:T(8,128)S(1)}, f32[3,1,128,128]{3,2,1,0:T(8,128)S(1)}, u32[]{:S(2)}, u32[]{:S(2)}) collective-permute-start(f32[3,1,128,128]{3,2,1,0:T(8,128)S(1)} %collective-permute-done.15.rest_3_), channel_id=1, source_target_pairs={{0,1},{1,0},{2,3},{3,2},{4,5},{5,4},{6,7},{7,6},{8,9},{9,8},{10,11... | collective-permute-start | bytes 589832 | tf_op jit(solution)/shard_map/ppermute | solution.py:244
  64.8 1.5 %collective-permute-start.20 = (f32[3,1,128,128]{3,2,1,0:T(8,128)S(1)}, f32[3,1,128,128]{3,2,1,0:T(8,128)S(1)}, u32[]{:S(2)}, u32[]{:S(2)}) collective-permute-start(f32[3,1,128,128]{3,2,1,0:T(8,128)S(1)} %collective-permute-done.16.rest_4_), channel_id=1, source_target_pairs={{0,1},{1,0},{2,3},{3,2},{4,5},{5,4},{6,7},{7,6},{8,9},{9,8},{10,11... | collective-permute-start | bytes 589832 | tf_op jit(solution)/shard_map/ppermute | solution.py:244

commit v6 on v5

--- a/solution.py
+++ b/solution.py
@@ -292,7 +292,7 @@
     first = tied(first, ring_z)
     facing = tied(facing, first)
     near_buckets = jnp.stack(buckets_of_ring(sums))
-    inner = [near_buckets, apart_y(near_buckets, 1), None, None]
+    inner = [near_buckets, apart_y(near_buckets, 1), None, apart_y(near_buckets, 3)]
 
     mine = lax.dynamic_slice_in_dim(ring_z, core, 1, 0)
     theirs = lax.dynamic_slice_in_dim(facing, core, 1, 0)
@@ -300,7 +300,6 @@
     chip_first = apart_x(chip, 1)
     pair = state + tied(first, chip)
     second = apart_y(pair, 3)
-    inner[3] = apart_y(tied(near_buckets, chip), 3)
     chip_first = tied(chip_first, pair)
     chip_second = apart_x(chip + chip_first, 3)
     chip_second = tied(chip_second, inner[1], inner[3])

time: 70.6 us -> 68.5 us (0.970)
  waiting for transfers between devices: 11.6 us -> 10.2 us
    ppermute x21, waiting for transfers between devices: 11.6 us -> 10.2 us  [along(): lax.ppermute(value, axis, [(i, hop(i)) for i in range(lax.axis_size(axis))])]
where the time goes in v6:
time: 68.5 us; the launch traced here: 68.2 us
  starting transfers between devices  25.7 us (38%)
  Pallas kernels  21.5 us (31%)
  waiting for transfers between devices  10.2 us (15%)
  local copies, waits for them, and re-layouts  7.76 us (11%)
  other arithmetic  2.72 us (4%)
    ppermute x21, starting transfers between devices, along(): lax.ppermute(value, axis, [(i, hop(i)) for i in range(lax.axis_size(axis))])  25.7 us
    ppermute x21, waiting for transfers between devices, along(): lax.ppermute(value, axis, [(i, hop(i)) for i in range(lax.axis_size(axis))])  10.2 us
    pallas_call x2, Pallas kernels, near_part(): pl.pallas_call(functools.partial(near_kernel, first), grid=(count,), in_s...  8.99 us
    unnamed x22, local copies, waits for them, and re-layouts  7.76 us
    pallas_call x2, Pallas kernels, far_part(): pl.pallas_call(functools.partial(far_kernel, plan, last, local_bits), in_...  6.45 us
    pallas_call x1, Pallas kernels, states(): pl.pallas_call(state_kernel, grid=(length // rows,), in_specs=[part, part...  3.79 us
    pallas_call x1, Pallas kernels, by_head(): pl.pallas_call(layout_kernel, grid=(length // rows,), in_specs=[part] * 3...  2.3 us
  transfers between devices with their start and end apart: 21, of which 10 were waited for; matrix products, arithmetic and copies ran while one was open for 4% of the time, Pallas kernels for 20%

profile of v6, /device:TPU:1, one launch (start us, length us, event | category | flops | bytes accessed | tf_op | source)
XLA Modules:
  0.0 68.2 jit_solution(2106545776879088062)
XLA Ops:
  0.0 3.8 %states.1 = (f32[8,128,128]{2,1,0:T(8,128)}, f32[2,128,128]{2,1,0:T(8,128)}, f32[2,128,128]{2,1,0:T(8,128)}, f32[2,128,128]{2,1,0:T(8,128)}, f32[2,128,128]{2,1,0:T(8,128)}) custom-call(bf16[1024,8,128]{2,1,0:T(8,128)(2,1)} %key_ref.3, bf16[1024,8,128]{2,1,0:T(8,128)(2,1)} %value_ref.3), custom_call_target="tpu_custom_call" | custom-call | flops 300000000 | bytes 5242880 | tf_op jit(solution)/shard_map/states/pallas_call | solution.py:65
  3.8 2.1 %collective-permute-start = (f32[2,128,128]{2,1,0:T(8,128)}, f32[2,128,128]{2,1,0:T(8,128)S(1)}, u32[]{:S(2)}, u32[]{:S(2)}) collective-permute-start(f32[2,128,128]{2,1,0:T(8,128)} %get-tuple-element.37), channel_id=1, source_target_pairs={{0,8},{8,0},{16,24},{24,16},{32,40},{40,32},{48,56},{56,48},{64,72... | collective-permute-start | bytes 393224 | tf_op jit(solution)/shard_map/ppermute | solution.py:244
  5.9 2.6 %collective-permute-start.1 = (f32[2,128,128]{2,1,0:T(8,128)}, f32[2,128,128]{2,1,0:T(8,128)S(1)}, u32[]{:S(2)}, u32[]{:S(2)}) collective-permute-start(f32[2,128,128]{2,1,0:T(8,128)} %get-tuple-element.38), channel_id=1, source_target_pairs={{0,16},{8,24},{16,0},{24,8},{32,48},{40,56},{48,32},{56,40},{64,80... | collective-permute-start | bytes 393224 | tf_op jit(solution)/shard_map/ppermute | solution.py:244
  8.5 0.0 collective-permute-start.2
  8.5 0.0 collective-permute-start.7
  8.6 1.6 %copy-done.1 = bf16[1024,8,128]{2,1,0:T(8,128)(2,1)S(1)} copy-done((bf16[1024,8,128]{2,1,0:T(8,128)(2,1)S(1)}, bf16[1024,8,128]{2,1,0:T(8,128)(2,1)}, u32[]{:S(2)}) %copy-start.1) | copy-done | bytes 2097176
  10.2 1.6 %copy-done.2 = bf16[1024,8,128]{2,1,0:T(8,128)(2,1)S(1)} copy-done((bf16[1024,8,128]{2,1,0:T(8,128)(2,1)S(1)}, bf16[1024,8,128]{2,1,0:T(8,128)(2,1)}, u32[]{:S(2)}) %copy-start.2) | copy-done | bytes 2097176
  11.8 1.6 %copy-done.9 = bf16[1024,8,128]{2,1,0:T(8,128)(2,1)S(1)} copy-done((bf16[1024,8,128]{2,1,0:T(8,128)(2,1)S(1)}, bf16[1024,8,128]{2,1,0:T(8,128)(2,1)}, u32[]{:S(2)}) %copy-start.9) | copy-done | bytes 2097176
  13.4 2.3 %by_head.1 = (bf16[8,1024,128]{2,1,0:T(8,128)(2,1)S(1)}, bf16[8,1024,128]{2,1,0:T(8,128)(2,1)S(1)}, bf16[8,128,1024]{2,1,0:T(8,128)(2,1)S(1)}) custom-call(bf16[1024,8,128]{2,1,0:T(8,128)(2,1)S(1)} %copy-done.9, bf16[1024,8,128]{2,1,0:T(8,128)(2,1)S(1)} %copy-done.1, bf16[1024,8,128]{2,1,0:T(8,128)(2,1)S(1)} %copy-done.2), custom_call_target="tpu_custom_call" | custom-call | flops 1000000 | bytes 10485 | tf_op jit(solution)/shard_map/by_head/pallas_call | solution.py:91
  15.7 0.0 copy-start.5
  15.7 0.0 copy-start.7
  15.7 0.0 collective-permute-done
  15.7 0.0 collective-permute-done.1
  15.8 1.2 %collective-permute-done.2 = f32[2,128,128]{2,1,0:T(8,128)S(1)} collective-permute-done((f32[2,128,128]{2,1,0:T(8,128)}, f32[2,128,128]{2,1,0:T(8,128)S(1)}, u32[]{:S(2)}, u32[]{:S(2)}) %collective-permute-start.2) | collective-permute-done | bytes 131104 | tf_op jit(solution)/shard_map/ppermute | solution.py:244
  17.0 0.0 copy-done.10
  17.0 1.7 %collective-permute-start.3 = (f32[2,128,128]{2,1,0:T(8,128)S(1)}, f32[2,128,128]{2,1,0:T(8,128)S(1)}, u32[]{:S(2)}, u32[]{:S(2)}) collective-permute-start(f32[2,128,128]{2,1,0:T(8,128)S(1)} %add_add_fusion.1.tie_ref), channel_id=1, source_target_pairs={{0,32},{8,40},{16,48},{24,56},{32,0},{40,8},{48,16},{56,24},{64,96... | collective-permute-start | bytes 393224 | tf_op jit(solution)/shard_map/ppermute | solution.py:244
  18.7 3.3 %collective-permute-start.4 = (f32[2,128,128]{2,1,0:T(8,128)S(1)}, f32[2,128,128]{2,1,0:T(8,128)S(1)}, u32[]{:S(2)}, u32[]{:S(2)}) collective-permute-start(f32[2,128,128]{2,1,0:T(8,128)S(1)} %add_add_fusion.1.tie_ref), channel_id=1, source_target_pairs={{0,64},{8,72},{16,80},{24,88},{32,96},{40,104},{48,112},{56,120},{... | collective-permute-start | bytes 393224 | tf_op jit(solution)/shard_map/ppermute | solution.py:244
  22.0 0.0 collective-permute-start.5
  22.0 0.0 copy-done
  22.0 4.5 %near.2.rest_0_ = f32[4,128,1024]{2,1,0:T(8,128)S(1)} custom-call(bf16[8,1024,128]{2,1,0:T(8,128)(2,1)S(1)} %get-tuple-element.33.query_ref, bf16[8,1024,128]{2,1,0:T(8,128)(2,1)S(1)} %get-tuple-element.34.key_ref, bf16[8,128,1024]{2,1,0:T(8,128)(2,1)S(1)} %get-tuple-element.35.value_ref, f32[20,8,1024]{2,1,0:T(8,128)S(1)} %bitcast.10, ...), custom_call_target="tpu_custom_call" | custom-call | flops 1000000 | bytes 10485 | tf_op jit(solution)/shard_map/near/pallas_call | solution.py:150
  26.5 0.0 copy-done.5
  26.5 0.0 copy-start.3
  26.6 1.3 %copy-done.3 = f32[4,128,1024]{2,1,0:T(8,128)} copy-done((f32[4,128,1024]{2,1,0:T(8,128)}, f32[4,128,1024]{2,1,0:T(8,128)S(1)}, u32[]{:S(2)}) %copy-start.3) | copy-done | bytes 2097176
  27.9 0.0 collective-permute-done.3
  27.9 0.0 collective-permute-done.4
  27.9 1.8 %collective-permute-done.5 = f32[2,128,128]{2,1,0:T(8,128)S(1)} collective-permute-done((f32[2,128,128]{2,1,0:T(8,128)S(1)}, f32[2,128,128]{2,1,0:T(8,128)S(1)}, u32[]{:S(2)}, u32[]{:S(2)}) %collective-permute-start.5) | collective-permute-done | bytes 131104 | tf_op jit(solution)/shard_map/ppermute | solution.py:244
  29.7 0.7 add_bitcast_fusion
  30.3 1.5 %collective-permute-start.6 = (f32[2,128,128]{2,1,0:T(8,128)}, f32[2,128,128]{2,1,0:T(8,128)}, u32[]{:S(2)}, u32[]{:S(2)}) collective-permute-start(f32[2,128,128]{2,1,0:T(8,128)} %get-tuple-element.60), channel_id=1, source_target_pairs={{0,1},{1,0},{2,3},{3,2},{4,5},{5,4},{6,7},{7,6},{8,9},{9,8},{10,11... | collective-permute-start | bytes 393224 | tf_op jit(solution)/shard_map/ppermute | solution.py:244
  31.9 0.1 collective-permute-start.10
  31.9 2.5 %collective-permute-start.11 = (f32[2,2,128,128]{3,2,1,0:T(8,128)S(1)}, f32[2,2,128,128]{3,2,1,0:T(8,128)S(1)}, u32[]{:S(2)}, u32[]{:S(2)}) collective-permute-start(f32[2,2,128,128]{3,2,1,0:T(8,128)S(1)} %pad_maximum_fusion.rest_4_), channel_id=1, source_target_pairs={{0,24},{8,16},{16,8},{24,0},{32,56},{40,48},{48,40},{56,32},{64,88... | collective-permute-start | bytes 786440 | tf_op jit(solution)/shard_map/ppermute | solution.py:244
  34.5 0.0 collective-permute-done.7
  34.5 0.0 collective-permute-done.6
  34.5 0.9 %select_bitcast_fusion = (f32[1,1,128,128]{3,2,1,0:T(8,128)S(1)}, f32[1,128,128]{2,1,0:T(8,128)S(1)}) fusion(f32[2,128,128]{2,1,0:T(8,128)} %collective-permute-done.6, s32[]{:T(128)S(6)} %select_n.13, f32[2,128,128]{2,1,0:T(8,128)} %get-tuple-element.60, pred[]{:T(512)S(6)} %eq.3), kind=kLoop, calls=%fused_computation.5 | loop fusion | flops 32768 | bytes 262149 | tf_op jit(solution)/shard_map/stack | solution.py:306
  35.4 1.1 %add.42 = f32[8,128,128]{2,1,0:T(8,128)S(1)} add(f32[8,128,128]{2,1,0:T(8,128)} %get-tuple-element.31, f32[8,128,128]{2,1,0:T(8,128)S(1)} %collective-permute-done.7) | non-fusion elementwise | flops 131072 | bytes 1572864 | tf_op jit(solution)/shard_map/add | solution.py:301
  36.5 0.3 collective-permute-start.12
  36.8 1.2 %collective-permute-start.8 = (f32[1,128,128]{2,1,0:T(8,128)S(1)}, f32[1,128,128]{2,1,0:T(8,128)S(1)}, u32[]{:S(2)}, u32[]{:S(2)}) collective-permute-start(f32[1,128,128]{2,1,0:T(8,128)S(1)} %get-tuple-element.58), channel_id=1, source_target_pairs={{0,2},{1,3},{2,0},{3,1},{4,6},{5,7},{6,4},{7,5},{8,10},{9,11},{10,... | collective-permute-start | bytes 196616 | tf_op jit(solution)/shard_map/ppermute | solution.py:244
  38.0 2.2 %collective-permute-done.8 = f32[1,128,128]{2,1,0:T(8,128)S(1)} collective-permute-done((f32[1,128,128]{2,1,0:T(8,128)S(1)}, f32[1,128,128]{2,1,0:T(8,128)S(1)}, u32[]{:S(2)}, u32[]{:S(2)}) %collective-permute-start.8) | collective-permute-done | bytes 65568 | tf_op jit(solution)/shard_map/ppermute | solution.py:244
  40.2 2.6 %collective-permute-start.9 = (f32[1,128,128]{2,1,0:T(8,128)S(1)}, f32[1,128,128]{2,1,0:T(8,128)S(1)}, u32[]{:S(2)}, u32[]{:S(2)}) collective-permute-start(f32[1,128,128]{2,1,0:T(8,128)S(1)} %add.43), channel_id=1, source_target_pairs={{0,6},{1,7},{2,4},{3,5},{4,2},{5,3},{6,0},{7,1},{8,14},{9,15},{10,... | collective-permute-start | bytes 196616 | tf_op jit(solution)/shard_map/ppermute | solution.py:244
  42.8 0.0 collective-permute-done.11.rest_7_
  42.8 0.4 collective-permute-start.13
  43.2 0.0 collective-permute-done.10.rest_5_
  43.2 1.8 %collective-permute-done.9 = f32[1,128,128]{2,1,0:T(8,128)S(1)} collective-permute-done((f32[1,128,128]{2,1,0:T(8,128)S(1)}, f32[1,128,128]{2,1,0:T(8,128)S(1)}, u32[]{:S(2)}, u32[]{:S(2)}) %collective-permute-start.9) | collective-permute-done | bytes 65568 | tf_op jit(solution)/shard_map/ppermute | solution.py:244
  44.9 0.0 copy-start.4
  45.0 0.2 collective-permute-start.14
  45.1 3.5 %collective-permute-start.15 = (f32[3,1,128,128]{3,2,1,0:T(8,128)S(1)}, f32[3,1,128,128]{3,2,1,0:T(8,128)S(1)}, u32[]{:S(2)}, u32[]{:S(2)}) collective-permute-start(f32[3,1,128,128]{3,2,1,0:T(8,128)S(1)} %pad_maximum_fusion.1.tie_ref.rest_1_), channel_id=1, source_target_pairs={{0,16},{8,24},{16,0},{24,8},{32,48},{40,56},{48,32},{56,40},{64,80... | collective-permute-start | bytes 589832 | tf_op jit(solution)/shard_map/ppermute | solution.py:244
  48.7 0.2 collective-permute-start.16
  48.9 1.6 %copy-done.8 = bf16[8,128,1024]{2,1,0:T(8,128)(2,1)S(1)} copy-done((bf16[8,128,1024]{2,1,0:T(8,128)(2,1)S(1)}, bf16[8,128,1024]{2,1,0:T(8,128)(2,1)}, u32[]{:S(2)}) %copy-start.8) | copy-done | bytes 2097176
  50.5 4.5 %near.3.rest_1_ = f32[4,128,1024]{2,1,0:T(8,128)S(1)} custom-call(bf16[8,1024,128]{2,1,0:T(8,128)(2,1)S(1)} %get-tuple-element.33.query_ref, bf16[8,1024,128]{2,1,0:T(8,128)(2,1)S(1)} %copy-done.6, bf16[8,128,1024]{2,1,0:T(8,128)(2,1)S(1)} %copy-done.8, f32[20,8,1024]{2,1,0:T(8,128)S(1)} %bitcast.11, f32[3,1,128,128]{3,2,1,0:T(8,128)S(1)} %pad_maximum_fusion.1.tie_ref.rest_1_), custom_call_target="tpu_custom_call" | custom-call | flops 1000000 | bytes 10485 | tf_op jit(solution)/shard_map/near/pallas_call | solution.py:150
  55.0 0.0 collective-permute-done.13.rest_6_
  55.0 0.0 collective-permute-done.12
  55.0 0.0 copy-done.4
  55.0 2.7 %far.1.rest_0_ = f32[8,128,1024]{2,1,0:T(8,128)S(1)} custom-call(bf16[8,1024,128]{2,1,0:T(8,128)(2,1)S(1)} %get-tuple-element.33.query_ref, f32[20,8,1024]{2,1,0:T(8,128)S(1)} %bitcast.12, f32[4,128,1024]{2,1,0:T(8,128)S(1)} %copy-done.4, f32[4,128,1024]{2,1,0:T(8,128)S(1)} %near.3.rest_1_, f32[1,8,128,128]{3,2,1,0:T(8,128)S(1)} %bitcast.14, ...), custom_call_target="tpu_custom_call" | custom-call | flops 1000000 | bytes 10485 | tf_op jit(solution)/shard_map/far/pallas_call | solution.py:229
  57.7 0.0 collective-permute-done.14.rest_2_
  57.7 1.2 %collective-permute-done.15.rest_3_ = f32[3,1,128,128]{3,2,1,0:T(8,128)S(1)} collective-permute-done((f32[3,1,128,128]{3,2,1,0:T(8,128)S(1)}, f32[3,1,128,128]{3,2,1,0:T(8,128)S(1)}, u32[]{:S(2)}, u32[]{:S(2)}) %collective-permute-start.15) | collective-permute-done | bytes 196640 | tf_op jit(solution)/shard_map/ppermute | solution.py:244
  58.9 0.5 collective-permute-done.16.rest_4_
  59.4 2.8 %collective-permute-start.17 = (f32[3,1,128,128]{3,2,1,0:T(8,128)S(1)}, f32[3,1,128,128]{3,2,1,0:T(8,128)S(1)}, u32[]{:S(2)}, u32[]{:S(2)}) collective-permute-start(f32[3,1,128,128]{3,2,1,0:T(8,128)S(1)} %pad_maximum_fusion.1.tie_ref.rest_1_), channel_id=1, source_target_pairs={{0,1},{1,0},{2,3},{3,2},{4,5},{5,4},{6,7},{7,6},{8,9},{9,8},{10,11... | collective-permute-start | bytes 589832 | tf_op jit(solution)/shard_map/ppermute | solution.py:244
  62.3 0.0 collective-permute-start.18
  62.3 0.5 collective-permute-start.19
  62.8 0.0 collective-permute-start.20
  62.8 0.6 collective-permute-done.17.rest_5_
  63.4 0.4 collective-permute-done.18.rest_6_
  63.7 0.3 collective-permute-done.19.rest_7_
  64.0 0.3 collective-permute-done.20.rest_8_
  64.3 3.8 %finish.1 = bf16[1024,8,128]{2,1,0:T(8,128)(2,1)} custom-call(bf16[8,1024,128]{2,1,0:T(8,128)(2,1)S(1)} %get-tuple-element.33.query_ref, f32[20,8,1024]{2,1,0:T(8,128)S(1)} %bitcast.13, f32[8,128,1024]{2,1,0:T(8,128)S(1)} %far.1.rest_0_, f32[3,1,128,128]{3,2,1,0:T(8,128)S(1)} %pad_maximum_fusion.1.tie_ref.rest_1_, ...), custom_call_target="tpu_custom_call" | custom-call | flops 1000000 | bytes 10485 | tf_op jit(solution)/shard_map/finish/pallas_call | solution.py:229
  (13 shorter events, 0.1 us)
Async XLA Ops:
  3.8 11.9 %collective-permute-start = (f32[2,128,128]{2,1,0:T(8,128)}, f32[2,128,128]{2,1,0:T(8,128)S(1)}, u32[]{:S(2)}, u32[]{:S(2)}) collective-permute-start(f32[2,128,128]{2,1,0:T(8,128)} %get-tuple-element.37), channel_id=1, source_target_pairs={{0,8},{8,0},{16,24},{24,16},{32,40},{40,32},{48,56},{56,48},{64,72... | collective-permute-start | bytes 393224 | tf_op jit(solution)/shard_map/ppermute | solution.py:244
  5.9 9.8 %collective-permute-start.1 = (f32[2,128,128]{2,1,0:T(8,128)}, f32[2,128,128]{2,1,0:T(8,128)S(1)}, u32[]{:S(2)}, u32[]{:S(2)}) collective-permute-start(f32[2,128,128]{2,1,0:T(8,128)} %get-tuple-element.38), channel_id=1, source_target_pairs={{0,16},{8,24},{16,0},{24,8},{32,48},{40,56},{48,32},{56,40},{64,80... | collective-permute-start | bytes 393224 | tf_op jit(solution)/shard_map/ppermute | solution.py:244
  8.5 8.4 %collective-permute-start.2 = (f32[2,128,128]{2,1,0:T(8,128)}, f32[2,128,128]{2,1,0:T(8,128)S(1)}, u32[]{:S(2)}, u32[]{:S(2)}) collective-permute-start(f32[2,128,128]{2,1,0:T(8,128)} %get-tuple-element.39), channel_id=1, source_target_pairs={{0,24},{8,16},{16,8},{24,0},{32,56},{40,48},{48,40},{56,32},{64,88... | collective-permute-start | bytes 393224 | tf_op jit(solution)/shard_map/ppermute | solution.py:244
  8.5 13.5 %copy-start = (f32[8,20,1024]{2,0,1:T(8,128)S(1)}, f32[8,20,1024]{2,0,1:T(8,128)}, u32[]{:S(2)}) copy-start(f32[8,20,1024]{2,0,1:T(8,128)} %param.7) | copy-start | bytes 1966084
  8.5 26.0 %collective-permute-start.7 = (f32[8,128,128]{2,1,0:T(8,128)}, f32[8,128,128]{2,1,0:T(8,128)S(1)}, u32[]{:S(2)}, u32[]{:S(2)}) collective-permute-start(f32[8,128,128]{2,1,0:T(8,128)} %get-tuple-element.31), channel_id=1, source_target_pairs={{0,8},{8,0},{16,24},{24,16},{32,40},{40,32},{48,56},{56,48},{64,72... | collective-permute-start | bytes 1572872 | tf_op jit(solution)/shard_map/ppermute | solution.py:244
  8.6 1.7 %copy-start.1 = (bf16[1024,8,128]{2,1,0:T(8,128)(2,1)S(1)}, bf16[1024,8,128]{2,1,0:T(8,128)(2,1)}, u32[]{:S(2)}) copy-start(bf16[1024,8,128]{2,1,0:T(8,128)(2,1)} %key_ref.3) | copy-start | bytes 6291460
  10.2 1.6 %copy-start.2 = (bf16[1024,8,128]{2,1,0:T(8,128)(2,1)S(1)}, bf16[1024,8,128]{2,1,0:T(8,128)(2,1)}, u32[]{:S(2)}) copy-start(bf16[1024,8,128]{2,1,0:T(8,128)(2,1)} %value_ref.3) | copy-start | bytes 6291460
  11.8 1.6 %copy-start.9 = (bf16[1024,8,128]{2,1,0:T(8,128)(2,1)S(1)}, bf16[1024,8,128]{2,1,0:T(8,128)(2,1)}, u32[]{:S(2)}) copy-start(bf16[1024,8,128]{2,1,0:T(8,128)(2,1)} %query_ref) | copy-start | bytes 6291460
  13.4 3.6 %copy-start.10 = (f32[2,128,128]{2,1,0:T(8,128)S(1)}, f32[2,128,128]{2,1,0:T(8,128)}, u32[]{:S(2)}) copy-start(f32[2,128,128]{2,1,0:T(8,128)} %get-tuple-element.40) | copy-start | bytes 393220
  15.7 10.8 %copy-start.5 = (bf16[8,1024,128]{2,1,0:T(8,128)(2,1)}, bf16[8,1024,128]{2,1,0:T(8,128)(2,1)S(1)}, u32[]{:S(2)}) copy-start(bf16[8,1024,128]{2,1,0:T(8,128)(2,1)S(1)} %get-tuple-element.34.key_ref) | copy-start | bytes 6291460
  15.7 10.8 %copy-start.7 = (bf16[8,128,1024]{2,1,0:T(8,128)(2,1)}, bf16[8,128,1024]{2,1,0:T(8,128)(2,1)S(1)}, u32[]{:S(2)}) copy-start(bf16[8,128,1024]{2,1,0:T(8,128)(2,1)S(1)} %get-tuple-element.35.value_ref) | copy-start | bytes 6291460
  17.0 10.9 %collective-permute-start.3 = (f32[2,128,128]{2,1,0:T(8,128)S(1)}, f32[2,128,128]{2,1,0:T(8,128)S(1)}, u32[]{:S(2)}, u32[]{:S(2)}) collective-permute-start(f32[2,128,128]{2,1,0:T(8,128)S(1)} %add_add_fusion.1.tie_ref), channel_id=1, source_target_pairs={{0,32},{8,40},{16,48},{24,56},{32,0},{40,8},{48,16},{56,24},{64,96... | collective-permute-start | bytes 393224 | tf_op jit(solution)/shard_map/ppermute | solution.py:244
  18.7 9.2 %collective-permute-start.4 = (f32[2,128,128]{2,1,0:T(8,128)S(1)}, f32[2,128,128]{2,1,0:T(8,128)S(1)}, u32[]{:S(2)}, u32[]{:S(2)}) collective-permute-start(f32[2,128,128]{2,1,0:T(8,128)S(1)} %add_add_fusion.1.tie_ref), channel_id=1, source_target_pairs={{0,64},{8,72},{16,80},{24,88},{32,96},{40,104},{48,112},{56,120},{... | collective-permute-start | bytes 393224 | tf_op jit(solution)/shard_map/ppermute | solution.py:244
  22.0 7.6 %collective-permute-start.5 = (f32[2,128,128]{2,1,0:T(8,128)S(1)}, f32[2,128,128]{2,1,0:T(8,128)S(1)}, u32[]{:S(2)}, u32[]{:S(2)}) collective-permute-start(f32[2,128,128]{2,1,0:T(8,128)S(1)} %add_add_fusion.1.tie_ref), channel_id=1, source_target_pairs={{0,96},{8,104},{16,112},{24,120},{32,64},{40,72},{48,80},{56,88},{... | collective-permute-start | bytes 393224 | tf_op jit(solution)/shard_map/ppermute | solution.py:244
  26.5 1.3 %copy-start.3 = (f32[4,128,1024]{2,1,0:T(8,128)}, f32[4,128,1024]{2,1,0:T(8,128)S(1)}, u32[]{:S(2)}) copy-start(f32[4,128,1024]{2,1,0:T(8,128)S(1)} %near.2.rest_0_) | copy-start | bytes 6291460
  30.3 4.2 %collective-permute-start.6 = (f32[2,128,128]{2,1,0:T(8,128)}, f32[2,128,128]{2,1,0:T(8,128)}, u32[]{:S(2)}, u32[]{:S(2)}) collective-permute-start(f32[2,128,128]{2,1,0:T(8,128)} %get-tuple-element.60), channel_id=1, source_target_pairs={{0,1},{1,0},{2,3},{3,2},{4,5},{5,4},{6,7},{7,6},{8,9},{9,8},{10,11... | collective-permute-start | bytes 393224 | tf_op jit(solution)/shard_map/ppermute | solution.py:244
  31.8 17.1 %copy-start.6 = (bf16[8,1024,128]{2,1,0:T(8,128)(2,1)S(1)}, bf16[8,1024,128]{2,1,0:T(8,128)(2,1)}, u32[]{:S(2)}) copy-start(bf16[8,1024,128]{2,1,0:T(8,128)(2,1)} %copy-done.5) | copy-start | bytes 6291460
  31.9 11.3 %collective-permute-start.10 = (f32[2,2,128,128]{3,2,1,0:T(8,128)S(1)}, f32[2,2,128,128]{3,2,1,0:T(8,128)S(1)}, u32[]{:S(2)}, u32[]{:S(2)}) collective-permute-start(f32[2,2,128,128]{3,2,1,0:T(8,128)S(1)} %pad_maximum_fusion.rest_4_), channel_id=1, source_target_pairs={{0,8},{8,0},{16,24},{24,16},{32,40},{40,32},{48,56},{56,48},{64,72... | collective-permute-start | bytes 786440 | tf_op jit(solution)/shard_map/ppermute | solution.py:244
  31.9 10.8 %collective-permute-start.11 = (f32[2,2,128,128]{3,2,1,0:T(8,128)S(1)}, f32[2,2,128,128]{3,2,1,0:T(8,128)S(1)}, u32[]{:S(2)}, u32[]{:S(2)}) collective-permute-start(f32[2,2,128,128]{3,2,1,0:T(8,128)S(1)} %pad_maximum_fusion.rest_4_), channel_id=1, source_target_pairs={{0,24},{8,16},{16,8},{24,0},{32,56},{40,48},{48,40},{56,32},{64,88... | collective-permute-start | bytes 786440 | tf_op jit(solution)/shard_map/ppermute | solution.py:244
  36.5 18.5 %collective-permute-start.12 = (f32[8,128,128]{2,1,0:T(8,128)S(1)}, f32[8,128,128]{2,1,0:T(8,128)S(1)}, u32[]{:S(2)}, u32[]{:S(2)}) collective-permute-start(f32[8,128,128]{2,1,0:T(8,128)S(1)} %add.42), channel_id=1, source_target_pairs={{0,24},{8,16},{16,8},{24,0},{32,56},{40,48},{48,40},{56,32},{64,88... | collective-permute-start | bytes 1572872 | tf_op jit(solution)/shard_map/ppermute | solution.py:244
  36.8 3.4 %collective-permute-start.8 = (f32[1,128,128]{2,1,0:T(8,128)S(1)}, f32[1,128,128]{2,1,0:T(8,128)S(1)}, u32[]{:S(2)}, u32[]{:S(2)}) collective-permute-start(f32[1,128,128]{2,1,0:T(8,128)S(1)} %get-tuple-element.58), channel_id=1, source_target_pairs={{0,2},{1,3},{2,0},{3,1},{4,6},{5,7},{6,4},{7,5},{8,10},{9,11},{10,... | collective-permute-start | bytes 196616 | tf_op jit(solution)/shard_map/ppermute | solution.py:244
  40.2 4.7 %collective-permute-start.9 = (f32[1,128,128]{2,1,0:T(8,128)S(1)}, f32[1,128,128]{2,1,0:T(8,128)S(1)}, u32[]{:S(2)}, u32[]{:S(2)}) collective-permute-start(f32[1,128,128]{2,1,0:T(8,128)S(1)} %add.43), channel_id=1, source_target_pairs={{0,6},{1,7},{2,4},{3,5},{4,2},{5,3},{6,0},{7,1},{8,14},{9,15},{10,... | collective-permute-start | bytes 196616 | tf_op jit(solution)/shard_map/ppermute | solution.py:244
  42.8 12.2 %collective-permute-start.13 = (f32[2,2,128,128]{3,2,1,0:T(8,128)S(1)}, f32[2,2,128,128]{3,2,1,0:T(8,128)S(1)}, u32[]{:S(2)}, u32[]{:S(2)}) collective-permute-start(f32[2,2,128,128]{3,2,1,0:T(8,128)S(1)} %collective-permute-done.11.rest_7_), channel_id=1, source_target_pairs={{0,8},{8,0},{16,24},{24,16},{32,40},{40,32},{48,56},{56,48},{64,72... | collective-permute-start | bytes 786440 | tf_op jit(solution)/shard_map/ppermute | solution.py:244
  44.9 10.1 %copy-start.4 = (f32[4,128,1024]{2,1,0:T(8,128)S(1)}, f32[4,128,1024]{2,1,0:T(8,128)}, u32[]{:S(2)}) copy-start(f32[4,128,1024]{2,1,0:T(8,128)} %copy-done.3) | copy-start | bytes 6291460
  45.0 12.8 %collective-permute-start.14 = (f32[3,1,128,128]{3,2,1,0:T(8,128)S(1)}, f32[3,1,128,128]{3,2,1,0:T(8,128)S(1)}, u32[]{:S(2)}, u32[]{:S(2)}) collective-permute-start(f32[3,1,128,128]{3,2,1,0:T(8,128)S(1)} %pad_maximum_fusion.1.tie_ref.rest_1_), channel_id=1, source_target_pairs={{0,8},{8,0},{16,24},{24,16},{32,40},{40,32},{48,56},{56,48},{64,72... | collective-permute-start | bytes 589832 | tf_op jit(solution)/shard_map/ppermute | solution.py:244
  45.1 13.8 %collective-permute-start.15 = (f32[3,1,128,128]{3,2,1,0:T(8,128)S(1)}, f32[3,1,128,128]{3,2,1,0:T(8,128)S(1)}, u32[]{:S(2)}, u32[]{:S(2)}) collective-permute-start(f32[3,1,128,128]{3,2,1,0:T(8,128)S(1)} %pad_maximum_fusion.1.tie_ref.rest_1_), channel_id=1, source_target_pairs={{0,16},{8,24},{16,0},{24,8},{32,48},{40,56},{48,32},{56,40},{64,80... | collective-permute-start | bytes 589832 | tf_op jit(solution)/shard_map/ppermute | solution.py:244
  48.7 10.8 %collective-permute-start.16 = (f32[3,1,128,128]{3,2,1,0:T(8,128)S(1)}, f32[3,1,128,128]{3,2,1,0:T(8,128)S(1)}, u32[]{:S(2)}, u32[]{:S(2)}) collective-permute-start(f32[3,1,128,128]{3,2,1,0:T(8,128)S(1)} %pad_maximum_fusion.1.tie_ref.rest_1_), channel_id=1, source_target_pairs={{0,24},{8,16},{16,8},{24,0},{32,56},{40,48},{48,40},{56,32},{64,88... | collective-permute-start | bytes 589832 | tf_op jit(solution)/shard_map/ppermute | solution.py:244
  48.9 1.6 %copy-start.8 = (bf16[8,128,1024]{2,1,0:T(8,128)(2,1)S(1)}, bf16[8,128,1024]{2,1,0:T(8,128)(2,1)}, u32[]{:S(2)}) copy-start(bf16[8,128,1024]{2,1,0:T(8,128)(2,1)} %copy-done.7) | copy-start | bytes 6291460
  59.4 3.9 %collective-permute-start.17 = (f32[3,1,128,128]{3,2,1,0:T(8,128)S(1)}, f32[3,1,128,128]{3,2,1,0:T(8,128)S(1)}, u32[]{:S(2)}, u32[]{:S(2)}) collective-permute-start(f32[3,1,128,128]{3,2,1,0:T(8,128)S(1)} %pad_maximum_fusion.1.tie_ref.rest_1_), channel_id=1, source_target_pairs={{0,1},{1,0},{2,3},{3,2},{4,5},{5,4},{6,7},{7,6},{8,9},{9,8},{10,11... | collective-permute-start | bytes 589832 | tf_op jit(solution)/shard_map/ppermute | solution.py:244
  62.3 1.4 %collective-permute-start.18 = (f32[3,1,128,128]{3,2,1,0:T(8,128)S(1)}, f32[3,1,128,128]{3,2,1,0:T(8,128)S(1)}, u32[]{:S(2)}, u32[]{:S(2)}) collective-permute-start(f32[3,1,128,128]{3,2,1,0:T(8,128)S(1)} %collective-permute-done.14.rest_2_), channel_id=1, source_target_pairs={{0,1},{1,0},{2,3},{3,2},{4,5},{5,4},{6,7},{7,6},{8,9},{9,8},{10,11... | collective-permute-start | bytes 589832 | tf_op jit(solution)/shard_map/ppermute | solution.py:244
  62.3 1.7 %collective-permute-start.19 = (f32[3,1,128,128]{3,2,1,0:T(8,128)S(1)}, f32[3,1,128,128]{3,2,1,0:T(8,128)S(1)}, u32[]{:S(2)}, u32[]{:S(2)}) collective-permute-start(f32[3,1,128,128]{3,2,1,0:T(8,128)S(1)} %collective-permute-done.15.rest_3_), channel_id=1, source_target_pairs={{0,1},{1,0},{2,3},{3,2},{4,5},{5,4},{6,7},{7,6},{8,9},{9,8},{10,11... | collective-permute-start | bytes 589832 | tf_op jit(solution)/shard_map/ppermute | solution.py:244
  62.8 1.5 %collective-permute-start.20 = (f32[3,1,128,128]{3,2,1,0:T(8,128)S(1)}, f32[3,1,128,128]{3,2,1,0:T(8,128)S(1)}, u32[]{:S(2)}, u32[]{:S(2)}) collective-permute-start(f32[3,1,128,128]{3,2,1,0:T(8,128)S(1)} %collective-permute-done.16.rest_4_), channel_id=1, source_target_pairs={{0,1},{1,0},{2,3},{3,2},{4,5},{5,4},{6,7},{7,6},{8,9},{9,8},{10,11... | collective-permute-start | bytes 589832 | tf_op jit(solution)/shard_map/ppermute | solution.py:244

commit v7 on v6

--- a/solution.py
+++ b/solution.py
@@ -14,7 +14,7 @@
 RING = 4
 CORES = 2
 TILE = 256
-EARLY_HEADS = 4
+EARLY_HEADS = 3
 ROWS = 512
 
 

time: 68.5 us -> 68.6 us (level)
  transfers between devices with their start and end apart: 21 -> 21, of which waited for: 10 -> 11; matrix products, arithmetic and copies ran while one was open for 4% -> 4% of each run, Pallas kernels for 20% -> 20%
where the time goes in v7:
time: 68.6 us; the launch traced here: 68.3 us
  starting transfers between devices  25.7 us (37%)
  Pallas kernels  21.6 us (31%)
  waiting for transfers between devices  10.4 us (15%)
  local copies, waits for them, and re-layouts  7.59 us (11%)
  other arithmetic  2.72 us (4%)
    ppermute x21, starting transfers between devices, along(): lax.ppermute(value, axis, [(i, hop(i)) for i in range(lax.axis_size(axis))])  25.7 us
    ppermute x21, waiting for transfers between devices, along(): lax.ppermute(value, axis, [(i, hop(i)) for i in range(lax.axis_size(axis))])  10.4 us
    pallas_call x2, Pallas kernels, near_part(): pl.pallas_call(functools.partial(near_kernel, first), grid=(count,), in_s...  8.99 us
    unnamed x22, local copies, waits for them, and re-layouts  7.59 us
    pallas_call x2, Pallas kernels, far_part(): pl.pallas_call(functools.partial(far_kernel, plan, last, local_bits), in_...  6.44 us
    pallas_call x1, Pallas kernels, states(): pl.pallas_call(state_kernel, grid=(length // rows,), in_specs=[part, part...  3.83 us
    pallas_call x1, Pallas kernels, by_head(): pl.pallas_call(layout_kernel, grid=(length // rows,), in_specs=[part] * 3...  2.3 us
  transfers between devices with their start and end apart: 21, of which 11 were waited for; matrix products, arithmetic and copies ran while one was open for 4% of the time, Pallas kernels for 20%

profile of v7, /device:TPU:1, one launch (start us, length us, event | category | flops | bytes accessed | tf_op | source)
XLA Modules:
  0.0 68.3 jit_solution(13252966949421544750)
XLA Ops:
  0.0 3.8 %states.1 = (f32[8,128,128]{2,1,0:T(8,128)}, f32[2,128,128]{2,1,0:T(8,128)}, f32[2,128,128]{2,1,0:T(8,128)}, f32[2,128,128]{2,1,0:T(8,128)}, f32[2,128,128]{2,1,0:T(8,128)}) custom-call(bf16[1024,8,128]{2,1,0:T(8,128)(2,1)} %key_ref.3, bf16[1024,8,128]{2,1,0:T(8,128)(2,1)} %value_ref.3), custom_call_target="tpu_custom_call" | custom-call | flops 300000000 | bytes 5242880 | tf_op jit(solution)/shard_map/states/pallas_call | solution.py:65
  3.8 2.1 %collective-permute-start = (f32[2,128,128]{2,1,0:T(8,128)}, f32[2,128,128]{2,1,0:T(8,128)S(1)}, u32[]{:S(2)}, u32[]{:S(2)}) collective-permute-start(f32[2,128,128]{2,1,0:T(8,128)} %get-tuple-element.37), channel_id=1, source_target_pairs={{0,8},{8,0},{16,24},{24,16},{32,40},{40,32},{48,56},{56,48},{64,72... | collective-permute-start | bytes 393224 | tf_op jit(solution)/shard_map/ppermute | solution.py:244
  6.0 2.6 %collective-permute-start.1 = (f32[2,128,128]{2,1,0:T(8,128)}, f32[2,128,128]{2,1,0:T(8,128)S(1)}, u32[]{:S(2)}, u32[]{:S(2)}) collective-permute-start(f32[2,128,128]{2,1,0:T(8,128)} %get-tuple-element.38), channel_id=1, source_target_pairs={{0,16},{8,24},{16,0},{24,8},{32,48},{40,56},{48,32},{56,40},{64,80... | collective-permute-start | bytes 393224 | tf_op jit(solution)/shard_map/ppermute | solution.py:244
  8.6 0.0 collective-permute-start.2
  8.6 0.0 collective-permute-start.7
  8.6 1.6 %copy-done.1 = bf16[1024,8,128]{2,1,0:T(8,128)(2,1)S(1)} copy-done((bf16[1024,8,128]{2,1,0:T(8,128)(2,1)S(1)}, bf16[1024,8,128]{2,1,0:T(8,128)(2,1)}, u32[]{:S(2)}) %copy-start.1) | copy-done | bytes 2097176
  10.3 1.6 %copy-done.2 = bf16[1024,8,128]{2,1,0:T(8,128)(2,1)S(1)} copy-done((bf16[1024,8,128]{2,1,0:T(8,128)(2,1)S(1)}, bf16[1024,8,128]{2,1,0:T(8,128)(2,1)}, u32[]{:S(2)}) %copy-start.2) | copy-done | bytes 2097176
  11.9 1.6 %copy-done.9 = bf16[1024,8,128]{2,1,0:T(8,128)(2,1)S(1)} copy-done((bf16[1024,8,128]{2,1,0:T(8,128)(2,1)S(1)}, bf16[1024,8,128]{2,1,0:T(8,128)(2,1)}, u32[]{:S(2)}) %copy-start.9) | copy-done | bytes 2097176
  13.5 2.3 %by_head.1 = (bf16[8,1024,128]{2,1,0:T(8,128)(2,1)S(1)}, bf16[8,1024,128]{2,1,0:T(8,128)(2,1)S(1)}, bf16[8,128,1024]{2,1,0:T(8,128)(2,1)S(1)}) custom-call(bf16[1024,8,128]{2,1,0:T(8,128)(2,1)S(1)} %copy-done.9, bf16[1024,8,128]{2,1,0:T(8,128)(2,1)S(1)} %copy-done.1, bf16[1024,8,128]{2,1,0:T(8,128)(2,1)S(1)} %copy-done.2), custom_call_target="tpu_custom_call" | custom-call | flops 1000000 | bytes 10485 | tf_op jit(solution)/shard_map/by_head/pallas_call | solution.py:91
  15.8 0.0 copy-start.3
  15.8 0.0 copy-start.5
  15.8 0.0 collective-permute-done
  15.8 0.0 collective-permute-done.1
  15.8 1.2 %collective-permute-done.2 = f32[2,128,128]{2,1,0:T(8,128)S(1)} collective-permute-done((f32[2,128,128]{2,1,0:T(8,128)}, f32[2,128,128]{2,1,0:T(8,128)S(1)}, u32[]{:S(2)}, u32[]{:S(2)}) %collective-permute-start.2) | collective-permute-done | bytes 131104 | tf_op jit(solution)/shard_map/ppermute | solution.py:244
  17.0 0.0 copy-done.10
  17.0 1.7 %collective-permute-start.3 = (f32[2,128,128]{2,1,0:T(8,128)S(1)}, f32[2,128,128]{2,1,0:T(8,128)S(1)}, u32[]{:S(2)}, u32[]{:S(2)}) collective-permute-start(f32[2,128,128]{2,1,0:T(8,128)S(1)} %add_add_fusion.1.tie_ref), channel_id=1, source_target_pairs={{0,32},{8,40},{16,48},{24,56},{32,0},{40,8},{48,16},{56,24},{64,96... | collective-permute-start | bytes 393224 | tf_op jit(solution)/shard_map/ppermute | solution.py:244
  18.8 3.3 %collective-permute-start.4 = (f32[2,128,128]{2,1,0:T(8,128)S(1)}, f32[2,128,128]{2,1,0:T(8,128)S(1)}, u32[]{:S(2)}, u32[]{:S(2)}) collective-permute-start(f32[2,128,128]{2,1,0:T(8,128)S(1)} %add_add_fusion.1.tie_ref), channel_id=1, source_target_pairs={{0,64},{8,72},{16,80},{24,88},{32,96},{40,104},{48,112},{56,120},{... | collective-permute-start | bytes 393224 | tf_op jit(solution)/shard_map/ppermute | solution.py:244
  22.1 0.0 collective-permute-start.5
  22.1 0.0 copy-done
  22.1 3.4 %near.2.rest_0_ = f32[3,128,1024]{2,1,0:T(8,128)S(1)} custom-call(bf16[8,1024,128]{2,1,0:T(8,128)(2,1)S(1)} %get-tuple-element.33.query_ref, bf16[8,1024,128]{2,1,0:T(8,128)(2,1)S(1)} %get-tuple-element.34.key_ref, bf16[8,128,1024]{2,1,0:T(8,128)(2,1)S(1)} %get-tuple-element.35.value_ref, f32[20,8,1024]{2,1,0:T(8,128)S(1)} %bitcast.10, ...), custom_call_target="tpu_custom_call" | custom-call | flops 1000000 | bytes 10485 | tf_op jit(solution)/shard_map/near/pallas_call | solution.py:150
  25.5 0.0 copy-done.3
  25.5 0.0 copy-done.5
  25.5 0.0 copy-start.7
  25.5 1.1 %copy-done.7 = f32[3,128,1024]{2,1,0:T(8,128)} copy-done((f32[3,128,1024]{2,1,0:T(8,128)}, f32[3,128,1024]{2,1,0:T(8,128)S(1)}, u32[]{:S(2)}) %copy-start.7) | copy-done | bytes 1572888
  26.6 0.0 collective-permute-done.3
  26.6 0.3 collective-permute-done.4
  26.9 2.8 %collective-permute-done.5 = f32[2,128,128]{2,1,0:T(8,128)S(1)} collective-permute-done((f32[2,128,128]{2,1,0:T(8,128)S(1)}, f32[2,128,128]{2,1,0:T(8,128)S(1)}, u32[]{:S(2)}, u32[]{:S(2)}) %collective-permute-start.5) | collective-permute-done | bytes 131104 | tf_op jit(solution)/shard_map/ppermute | solution.py:244
  29.7 0.7 add_bitcast_fusion
  30.4 1.5 %collective-permute-start.6 = (f32[2,128,128]{2,1,0:T(8,128)}, f32[2,128,128]{2,1,0:T(8,128)}, u32[]{:S(2)}, u32[]{:S(2)}) collective-permute-start(f32[2,128,128]{2,1,0:T(8,128)} %get-tuple-element.60), channel_id=1, source_target_pairs={{0,1},{1,0},{2,3},{3,2},{4,5},{5,4},{6,7},{7,6},{8,9},{9,8},{10,11... | collective-permute-start | bytes 393224 | tf_op jit(solution)/shard_map/ppermute | solution.py:244
  31.9 0.1 collective-permute-start.10
  32.0 2.6 %collective-permute-start.11 = (f32[2,2,128,128]{3,2,1,0:T(8,128)S(1)}, f32[2,2,128,128]{3,2,1,0:T(8,128)S(1)}, u32[]{:S(2)}, u32[]{:S(2)}) collective-permute-start(f32[2,2,128,128]{3,2,1,0:T(8,128)S(1)} %pad_maximum_fusion.rest_4_), channel_id=1, source_target_pairs={{0,24},{8,16},{16,8},{24,0},{32,56},{40,48},{48,40},{56,32},{64,88... | collective-permute-start | bytes 786440 | tf_op jit(solution)/shard_map/ppermute | solution.py:244
  34.5 0.0 collective-permute-done.7
  34.6 0.0 collective-permute-done.6
  34.6 0.9 %select_bitcast_fusion = (f32[1,1,128,128]{3,2,1,0:T(8,128)S(1)}, f32[1,128,128]{2,1,0:T(8,128)S(1)}) fusion(f32[2,128,128]{2,1,0:T(8,128)} %collective-permute-done.6, s32[]{:T(128)S(6)} %select_n.13, f32[2,128,128]{2,1,0:T(8,128)} %get-tuple-element.60, pred[]{:T(512)S(6)} %eq.3), kind=kLoop, calls=%fused_computation.5 | loop fusion | flops 32768 | bytes 262149 | tf_op jit(solution)/shard_map/stack | solution.py:306
  35.4 1.1 %add.42 = f32[8,128,128]{2,1,0:T(8,128)S(1)} add(f32[8,128,128]{2,1,0:T(8,128)} %get-tuple-element.31, f32[8,128,128]{2,1,0:T(8,128)S(1)} %collective-permute-done.7) | non-fusion elementwise | flops 131072 | bytes 1572864 | tf_op jit(solution)/shard_map/add | solution.py:301
  36.5 0.3 collective-permute-start.12
  36.9 1.2 %collective-permute-start.8 = (f32[1,128,128]{2,1,0:T(8,128)S(1)}, f32[1,128,128]{2,1,0:T(8,128)S(1)}, u32[]{:S(2)}, u32[]{:S(2)}) collective-permute-start(f32[1,128,128]{2,1,0:T(8,128)S(1)} %get-tuple-element.58), channel_id=1, source_target_pairs={{0,2},{1,3},{2,0},{3,1},{4,6},{5,7},{6,4},{7,5},{8,10},{9,11},{10,... | collective-permute-start | bytes 196616 | tf_op jit(solution)/shard_map/ppermute | solution.py:244
  38.1 2.2 %collective-permute-done.8 = f32[1,128,128]{2,1,0:T(8,128)S(1)} collective-permute-done((f32[1,128,128]{2,1,0:T(8,128)S(1)}, f32[1,128,128]{2,1,0:T(8,128)S(1)}, u32[]{:S(2)}, u32[]{:S(2)}) %collective-permute-start.8) | collective-permute-done | bytes 65568 | tf_op jit(solution)/shard_map/ppermute | solution.py:244
  40.3 2.6 %collective-permute-start.9 = (f32[1,128,128]{2,1,0:T(8,128)S(1)}, f32[1,128,128]{2,1,0:T(8,128)S(1)}, u32[]{:S(2)}, u32[]{:S(2)}) collective-permute-start(f32[1,128,128]{2,1,0:T(8,128)S(1)} %add.43), channel_id=1, source_target_pairs={{0,6},{1,7},{2,4},{3,5},{4,2},{5,3},{6,0},{7,1},{8,14},{9,15},{10,... | collective-permute-start | bytes 196616 | tf_op jit(solution)/shard_map/ppermute | solution.py:244
  42.8 0.0 collective-permute-done.11.rest_7_
  42.8 0.4 collective-permute-start.13
  43.2 0.0 collective-permute-done.10.rest_5_
  43.2 1.8 %collective-permute-done.9 = f32[1,128,128]{2,1,0:T(8,128)S(1)} collective-permute-done((f32[1,128,128]{2,1,0:T(8,128)S(1)}, f32[1,128,128]{2,1,0:T(8,128)S(1)}, u32[]{:S(2)}, u32[]{:S(2)}) %collective-permute-start.9) | collective-permute-done | bytes 65568 | tf_op jit(solution)/shard_map/ppermute | solution.py:244
  45.0 0.2 collective-permute-start.14
  45.2 3.5 %collective-permute-start.15 = (f32[3,1,128,128]{3,2,1,0:T(8,128)S(1)}, f32[3,1,128,128]{3,2,1,0:T(8,128)S(1)}, u32[]{:S(2)}, u32[]{:S(2)}) collective-permute-start(f32[3,1,128,128]{3,2,1,0:T(8,128)S(1)} %pad_maximum_fusion.1.tie_ref.rest_1_), channel_id=1, source_target_pairs={{0,16},{8,24},{16,0},{24,8},{32,48},{40,56},{48,32},{56,40},{64,80... | collective-permute-start | bytes 589832 | tf_op jit(solution)/shard_map/ppermute | solution.py:244
  48.7 0.2 collective-permute-start.16
  48.9 1.6 %copy-done.6 = bf16[8,128,1024]{2,1,0:T(8,128)(2,1)S(1)} copy-done((bf16[8,128,1024]{2,1,0:T(8,128)(2,1)S(1)}, bf16[8,128,1024]{2,1,0:T(8,128)(2,1)}, u32[]{:S(2)}) %copy-start.6) | copy-done | bytes 2097176
  50.5 5.6 %near.3.rest_1_ = f32[5,128,1024]{2,1,0:T(8,128)S(1)} custom-call(bf16[8,1024,128]{2,1,0:T(8,128)(2,1)S(1)} %get-tuple-element.33.query_ref, bf16[8,1024,128]{2,1,0:T(8,128)(2,1)S(1)} %copy-done.4, bf16[8,128,1024]{2,1,0:T(8,128)(2,1)S(1)} %copy-done.6, f32[20,8,1024]{2,1,0:T(8,128)S(1)} %bitcast.11, f32[3,1,128,128]{3,2,1,0:T(8,128)S(1)} %pad_maximum_fusion.1.tie_ref.rest_1_), custom_call_target="tpu_custom_call" | custom-call | flops 1000000 | bytes 10485 | tf_op jit(solution)/shard_map/near/pallas_call | solution.py:150
  56.2 0.0 collective-permute-done.13.rest_6_
  56.2 0.0 collective-permute-done.12
  56.2 0.0 copy-done.8
  56.2 2.7 %far.1.rest_0_ = f32[8,128,1024]{2,1,0:T(8,128)S(1)} custom-call(bf16[8,1024,128]{2,1,0:T(8,128)(2,1)S(1)} %get-tuple-element.33.query_ref, f32[20,8,1024]{2,1,0:T(8,128)S(1)} %bitcast.12, f32[3,128,1024]{2,1,0:T(8,128)S(1)} %copy-done.8, f32[5,128,1024]{2,1,0:T(8,128)S(1)} %near.3.rest_1_, f32[1,8,128,128]{3,2,1,0:T(8,128)S(1)} %bitcast.14, ...), custom_call_target="tpu_custom_call" | custom-call | flops 1000000 | bytes 10485 | tf_op jit(solution)/shard_map/far/pallas_call | solution.py:229
  58.9 0.0 collective-permute-done.14.rest_2_
  58.9 0.1 collective-permute-done.15.rest_3_
  58.9 0.5 collective-permute-done.16.rest_4_
  59.5 2.8 %collective-permute-start.17 = (f32[3,1,128,128]{3,2,1,0:T(8,128)S(1)}, f32[3,1,128,128]{3,2,1,0:T(8,128)S(1)}, u32[]{:S(2)}, u32[]{:S(2)}) collective-permute-start(f32[3,1,128,128]{3,2,1,0:T(8,128)S(1)} %pad_maximum_fusion.1.tie_ref.rest_1_), channel_id=1, source_target_pairs={{0,1},{1,0},{2,3},{3,2},{4,5},{5,4},{6,7},{7,6},{8,9},{9,8},{10,11... | collective-permute-start | bytes 589832 | tf_op jit(solution)/shard_map/ppermute | solution.py:244
  62.3 0.0 collective-permute-start.18
  62.3 0.5 collective-permute-start.19
  62.8 0.0 collective-permute-start.20
  62.8 0.6 collective-permute-done.17.rest_5_
  63.4 0.4 collective-permute-done.18.rest_6_
  63.8 0.3 collective-permute-done.19.rest_7_
  64.1 0.3 collective-permute-done.20.rest_8_
  64.3 3.8 %finish.1 = bf16[1024,8,128]{2,1,0:T(8,128)(2,1)} custom-call(bf16[8,1024,128]{2,1,0:T(8,128)(2,1)S(1)} %get-tuple-element.33.query_ref, f32[20,8,1024]{2,1,0:T(8,128)S(1)} %bitcast.13, f32[8,128,1024]{2,1,0:T(8,128)S(1)} %far.1.rest_0_, f32[3,1,128,128]{3,2,1,0:T(8,128)S(1)} %pad_maximum_fusion.1.tie_ref.rest_1_, ...), custom_call_target="tpu_custom_call" | custom-call | flops 1000000 | bytes 10485 | tf_op jit(solution)/shard_map/finish/pallas_call | solution.py:229
  (13 shorter events, 0.1 us)
Async XLA Ops:
  3.8 11.9 %collective-permute-start = (f32[2,128,128]{2,1,0:T(8,128)}, f32[2,128,128]{2,1,0:T(8,128)S(1)}, u32[]{:S(2)}, u32[]{:S(2)}) collective-permute-start(f32[2,128,128]{2,1,0:T(8,128)} %get-tuple-element.37), channel_id=1, source_target_pairs={{0,8},{8,0},{16,24},{24,16},{32,40},{40,32},{48,56},{56,48},{64,72... | collective-permute-start | bytes 393224 | tf_op jit(solution)/shard_map/ppermute | solution.py:244
  6.0 9.8 %collective-permute-start.1 = (f32[2,128,128]{2,1,0:T(8,128)}, f32[2,128,128]{2,1,0:T(8,128)S(1)}, u32[]{:S(2)}, u32[]{:S(2)}) collective-permute-start(f32[2,128,128]{2,1,0:T(8,128)} %get-tuple-element.38), channel_id=1, source_target_pairs={{0,16},{8,24},{16,0},{24,8},{32,48},{40,56},{48,32},{56,40},{64,80... | collective-permute-start | bytes 393224 | tf_op jit(solution)/shard_map/ppermute | solution.py:244
  8.6 8.4 %collective-permute-start.2 = (f32[2,128,128]{2,1,0:T(8,128)}, f32[2,128,128]{2,1,0:T(8,128)S(1)}, u32[]{:S(2)}, u32[]{:S(2)}) collective-permute-start(f32[2,128,128]{2,1,0:T(8,128)} %get-tuple-element.39), channel_id=1, source_target_pairs={{0,24},{8,16},{16,8},{24,0},{32,56},{40,48},{48,40},{56,32},{64,88... | collective-permute-start | bytes 393224 | tf_op jit(solution)/shard_map/ppermute | solution.py:244
  8.6 13.5 %copy-start = (f32[8,20,1024]{2,0,1:T(8,128)S(1)}, f32[8,20,1024]{2,0,1:T(8,128)}, u32[]{:S(2)}) copy-start(f32[8,20,1024]{2,0,1:T(8,128)} %param.7) | copy-start | bytes 1966084
  8.6 26.0 %collective-permute-start.7 = (f32[8,128,128]{2,1,0:T(8,128)}, f32[8,128,128]{2,1,0:T(8,128)S(1)}, u32[]{:S(2)}, u32[]{:S(2)}) collective-permute-start(f32[8,128,128]{2,1,0:T(8,128)} %get-tuple-element.31), channel_id=1, source_target_pairs={{0,8},{8,0},{16,24},{24,16},{32,40},{40,32},{48,56},{56,48},{64,72... | collective-permute-start | bytes 1572872 | tf_op jit(solution)/shard_map/ppermute | solution.py:244
  8.6 1.7 %copy-start.1 = (bf16[1024,8,128]{2,1,0:T(8,128)(2,1)S(1)}, bf16[1024,8,128]{2,1,0:T(8,128)(2,1)}, u32[]{:S(2)}) copy-start(bf16[1024,8,128]{2,1,0:T(8,128)(2,1)} %key_ref.3) | copy-start | bytes 6291460
  10.3 1.6 %copy-start.2 = (bf16[1024,8,128]{2,1,0:T(8,128)(2,1)S(1)}, bf16[1024,8,128]{2,1,0:T(8,128)(2,1)}, u32[]{:S(2)}) copy-start(bf16[1024,8,128]{2,1,0:T(8,128)(2,1)} %value_ref.3) | copy-start | bytes 6291460
  11.9 1.6 %copy-start.9 = (bf16[1024,8,128]{2,1,0:T(8,128)(2,1)S(1)}, bf16[1024,8,128]{2,1,0:T(8,128)(2,1)}, u32[]{:S(2)}) copy-start(bf16[1024,8,128]{2,1,0:T(8,128)(2,1)} %query_ref) | copy-start | bytes 6291460
  13.5 3.6 %copy-start.10 = (f32[2,128,128]{2,1,0:T(8,128)S(1)}, f32[2,128,128]{2,1,0:T(8,128)}, u32[]{:S(2)}) copy-start(f32[2,128,128]{2,1,0:T(8,128)} %get-tuple-element.40) | copy-start | bytes 393220
  15.8 9.7 %copy-start.3 = (bf16[8,1024,128]{2,1,0:T(8,128)(2,1)}, bf16[8,1024,128]{2,1,0:T(8,128)(2,1)S(1)}, u32[]{:S(2)}) copy-start(bf16[8,1024,128]{2,1,0:T(8,128)(2,1)S(1)} %get-tuple-element.34.key_ref) | copy-start | bytes 6291460
  15.8 9.7 %copy-start.5 = (bf16[8,128,1024]{2,1,0:T(8,128)(2,1)}, bf16[8,128,1024]{2,1,0:T(8,128)(2,1)S(1)}, u32[]{:S(2)}) copy-start(bf16[8,128,1024]{2,1,0:T(8,128)(2,1)S(1)} %get-tuple-element.35.value_ref) | copy-start | bytes 6291460
  17.0 9.6 %collective-permute-start.3 = (f32[2,128,128]{2,1,0:T(8,128)S(1)}, f32[2,128,128]{2,1,0:T(8,128)S(1)}, u32[]{:S(2)}, u32[]{:S(2)}) collective-permute-start(f32[2,128,128]{2,1,0:T(8,128)S(1)} %add_add_fusion.1.tie_ref), channel_id=1, source_target_pairs={{0,32},{8,40},{16,48},{24,56},{32,0},{40,8},{48,16},{56,24},{64,96... | collective-permute-start | bytes 393224 | tf_op jit(solution)/shard_map/ppermute | solution.py:244
  18.8 8.1 %collective-permute-start.4 = (f32[2,128,128]{2,1,0:T(8,128)S(1)}, f32[2,128,128]{2,1,0:T(8,128)S(1)}, u32[]{:S(2)}, u32[]{:S(2)}) collective-permute-start(f32[2,128,128]{2,1,0:T(8,128)S(1)} %add_add_fusion.1.tie_ref), channel_id=1, source_target_pairs={{0,64},{8,72},{16,80},{24,88},{32,96},{40,104},{48,112},{56,120},{... | collective-permute-start | bytes 393224 | tf_op jit(solution)/shard_map/ppermute | solution.py:244
  22.1 7.6 %collective-permute-start.5 = (f32[2,128,128]{2,1,0:T(8,128)S(1)}, f32[2,128,128]{2,1,0:T(8,128)S(1)}, u32[]{:S(2)}, u32[]{:S(2)}) collective-permute-start(f32[2,128,128]{2,1,0:T(8,128)S(1)} %add_add_fusion.1.tie_ref), channel_id=1, source_target_pairs={{0,96},{8,104},{16,112},{24,120},{32,64},{40,72},{48,80},{56,88},{... | collective-permute-start | bytes 393224 | tf_op jit(solution)/shard_map/ppermute | solution.py:244
  25.5 1.1 %copy-start.7 = (f32[3,128,1024]{2,1,0:T(8,128)}, f32[3,128,1024]{2,1,0:T(8,128)S(1)}, u32[]{:S(2)}) copy-start(f32[3,128,1024]{2,1,0:T(8,128)S(1)} %near.2.rest_0_) | copy-start | bytes 4718596
  30.4 4.2 %collective-permute-start.6 = (f32[2,128,128]{2,1,0:T(8,128)}, f32[2,128,128]{2,1,0:T(8,128)}, u32[]{:S(2)}, u32[]{:S(2)}) collective-permute-start(f32[2,128,128]{2,1,0:T(8,128)} %get-tuple-element.60), channel_id=1, source_target_pairs={{0,1},{1,0},{2,3},{3,2},{4,5},{5,4},{6,7},{7,6},{8,9},{9,8},{10,11... | collective-permute-start | bytes 393224 | tf_op jit(solution)/shard_map/ppermute | solution.py:244
  31.9 17.1 %copy-start.4 = (bf16[8,1024,128]{2,1,0:T(8,128)(2,1)S(1)}, bf16[8,1024,128]{2,1,0:T(8,128)(2,1)}, u32[]{:S(2)}) copy-start(bf16[8,1024,128]{2,1,0:T(8,128)(2,1)} %copy-done.3) | copy-start | bytes 6291460
  31.9 11.3 %collective-permute-start.10 = (f32[2,2,128,128]{3,2,1,0:T(8,128)S(1)}, f32[2,2,128,128]{3,2,1,0:T(8,128)S(1)}, u32[]{:S(2)}, u32[]{:S(2)}) collective-permute-start(f32[2,2,128,128]{3,2,1,0:T(8,128)S(1)} %pad_maximum_fusion.rest_4_), channel_id=1, source_target_pairs={{0,8},{8,0},{16,24},{24,16},{32,40},{40,32},{48,56},{56,48},{64,72... | collective-permute-start | bytes 786440 | tf_op jit(solution)/shard_map/ppermute | solution.py:244
  32.0 10.8 %collective-permute-start.11 = (f32[2,2,128,128]{3,2,1,0:T(8,128)S(1)}, f32[2,2,128,128]{3,2,1,0:T(8,128)S(1)}, u32[]{:S(2)}, u32[]{:S(2)}) collective-permute-start(f32[2,2,128,128]{3,2,1,0:T(8,128)S(1)} %pad_maximum_fusion.rest_4_), channel_id=1, source_target_pairs={{0,24},{8,16},{16,8},{24,0},{32,56},{40,48},{48,40},{56,32},{64,88... | collective-permute-start | bytes 786440 | tf_op jit(solution)/shard_map/ppermute | solution.py:244
  36.5 19.6 %collective-permute-start.12 = (f32[8,128,128]{2,1,0:T(8,128)S(1)}, f32[8,128,128]{2,1,0:T(8,128)S(1)}, u32[]{:S(2)}, u32[]{:S(2)}) collective-permute-start(f32[8,128,128]{2,1,0:T(8,128)S(1)} %add.42), channel_id=1, source_target_pairs={{0,24},{8,16},{16,8},{24,0},{32,56},{40,48},{48,40},{56,32},{64,88... | collective-permute-start | bytes 1572872 | tf_op jit(solution)/shard_map/ppermute | solution.py:244
  36.9 3.4 %collective-permute-start.8 = (f32[1,128,128]{2,1,0:T(8,128)S(1)}, f32[1,128,128]{2,1,0:T(8,128)S(1)}, u32[]{:S(2)}, u32[]{:S(2)}) collective-permute-start(f32[1,128,128]{2,1,0:T(8,128)S(1)} %get-tuple-element.58), channel_id=1, source_target_pairs={{0,2},{1,3},{2,0},{3,1},{4,6},{5,7},{6,4},{7,5},{8,10},{9,11},{10,... | collective-permute-start | bytes 196616 | tf_op jit(solution)/shard_map/ppermute | solution.py:244
  40.3 4.7 %collective-permute-start.9 = (f32[1,128,128]{2,1,0:T(8,128)S(1)}, f32[1,128,128]{2,1,0:T(8,128)S(1)}, u32[]{:S(2)}, u32[]{:S(2)}) collective-permute-start(f32[1,128,128]{2,1,0:T(8,128)S(1)} %add.43), channel_id=1, source_target_pairs={{0,6},{1,7},{2,4},{3,5},{4,2},{5,3},{6,0},{7,1},{8,14},{9,15},{10,... | collective-permute-start | bytes 196616 | tf_op jit(solution)/shard_map/ppermute | solution.py:244
  42.8 13.3 %collective-permute-start.13 = (f32[2,2,128,128]{3,2,1,0:T(8,128)S(1)}, f32[2,2,128,128]{3,2,1,0:T(8,128)S(1)}, u32[]{:S(2)}, u32[]{:S(2)}) collective-permute-start(f32[2,2,128,128]{3,2,1,0:T(8,128)S(1)} %collective-permute-done.11.rest_7_), channel_id=1, source_target_pairs={{0,8},{8,0},{16,24},{24,16},{32,40},{40,32},{48,56},{56,48},{64,72... | collective-permute-start | bytes 786440 | tf_op jit(solution)/shard_map/ppermute | solution.py:244
  45.0 13.9 %collective-permute-start.14 = (f32[3,1,128,128]{3,2,1,0:T(8,128)S(1)}, f32[3,1,128,128]{3,2,1,0:T(8,128)S(1)}, u32[]{:S(2)}, u32[]{:S(2)}) collective-permute-start(f32[3,1,128,128]{3,2,1,0:T(8,128)S(1)} %pad_maximum_fusion.1.tie_ref.rest_1_), channel_id=1, source_target_pairs={{0,8},{8,0},{16,24},{24,16},{32,40},{40,32},{48,56},{56,48},{64,72... | collective-permute-start | bytes 589832 | tf_op jit(solution)/shard_map/ppermute | solution.py:244
  45.2 13.8 %collective-permute-start.15 = (f32[3,1,128,128]{3,2,1,0:T(8,128)S(1)}, f32[3,1,128,128]{3,2,1,0:T(8,128)S(1)}, u32[]{:S(2)}, u32[]{:S(2)}) collective-permute-start(f32[3,1,128,128]{3,2,1,0:T(8,128)S(1)} %pad_maximum_fusion.1.tie_ref.rest_1_), channel_id=1, source_target_pairs={{0,16},{8,24},{16,0},{24,8},{32,48},{40,56},{48,32},{56,40},{64,80... | collective-permute-start | bytes 589832 | tf_op jit(solution)/shard_map/ppermute | solution.py:244
  48.7 10.8 %collective-permute-start.16 = (f32[3,1,128,128]{3,2,1,0:T(8,128)S(1)}, f32[3,1,128,128]{3,2,1,0:T(8,128)S(1)}, u32[]{:S(2)}, u32[]{:S(2)}) collective-permute-start(f32[3,1,128,128]{3,2,1,0:T(8,128)S(1)} %pad_maximum_fusion.1.tie_ref.rest_1_), channel_id=1, source_target_pairs={{0,24},{8,16},{16,8},{24,0},{32,56},{40,48},{48,40},{56,32},{64,88... | collective-permute-start | bytes 589832 | tf_op jit(solution)/shard_map/ppermute | solution.py:244
  48.9 1.6 %copy-start.6 = (bf16[8,128,1024]{2,1,0:T(8,128)(2,1)S(1)}, bf16[8,128,1024]{2,1,0:T(8,128)(2,1)}, u32[]{:S(2)}) copy-start(bf16[8,128,1024]{2,1,0:T(8,128)(2,1)} %copy-done.5) | copy-start | bytes 6291460
  50.5 5.7 %copy-start.8 = (f32[3,128,1024]{2,1,0:T(8,128)S(1)}, f32[3,128,1024]{2,1,0:T(8,128)}, u32[]{:S(2)}) copy-start(f32[3,128,1024]{2,1,0:T(8,128)} %copy-done.7) | copy-start | bytes 4718596
  59.5 3.9 %collective-permute-start.17 = (f32[3,1,128,128]{3,2,1,0:T(8,128)S(1)}, f32[3,1,128,128]{3,2,1,0:T(8,128)S(1)}, u32[]{:S(2)}, u32[]{:S(2)}) collective-permute-start(f32[3,1,128,128]{3,2,1,0:T(8,128)S(1)} %pad_maximum_fusion.1.tie_ref.rest_1_), channel_id=1, source_target_pairs={{0,1},{1,0},{2,3},{3,2},{4,5},{5,4},{6,7},{7,6},{8,9},{9,8},{10,11... | collective-permute-start | bytes 589832 | tf_op jit(solution)/shard_map/ppermute | solution.py:244
  62.3 1.4 %collective-permute-start.18 = (f32[3,1,128,128]{3,2,1,0:T(8,128)S(1)}, f32[3,1,128,128]{3,2,1,0:T(8,128)S(1)}, u32[]{:S(2)}, u32[]{:S(2)}) collective-permute-start(f32[3,1,128,128]{3,2,1,0:T(8,128)S(1)} %collective-permute-done.14.rest_2_), channel_id=1, source_target_pairs={{0,1},{1,0},{2,3},{3,2},{4,5},{5,4},{6,7},{7,6},{8,9},{9,8},{10,11... | collective-permute-start | bytes 589832 | tf_op jit(solution)/shard_map/ppermute | solution.py:244
  62.3 1.7 %collective-permute-start.19 = (f32[3,1,128,128]{3,2,1,0:T(8,128)S(1)}, f32[3,1,128,128]{3,2,1,0:T(8,128)S(1)}, u32[]{:S(2)}, u32[]{:S(2)}) collective-permute-start(f32[3,1,128,128]{3,2,1,0:T(8,128)S(1)} %collective-permute-done.15.rest_3_), channel_id=1, source_target_pairs={{0,1},{1,0},{2,3},{3,2},{4,5},{5,4},{6,7},{7,6},{8,9},{9,8},{10,11... | collective-permute-start | bytes 589832 | tf_op jit(solution)/shard_map/ppermute | solution.py:244
  62.8 1.5 %collective-permute-start.20 = (f32[3,1,128,128]{3,2,1,0:T(8,128)S(1)}, f32[3,1,128,128]{3,2,1,0:T(8,128)S(1)}, u32[]{:S(2)}, u32[]{:S(2)}) collective-permute-start(f32[3,1,128,128]{3,2,1,0:T(8,128)S(1)} %collective-permute-done.16.rest_4_), channel_id=1, source_target_pairs={{0,1},{1,0},{2,3},{3,2},{4,5},{5,4},{6,7},{7,6},{8,9},{9,8},{10,11... | collective-permute-start | bytes 589832 | tf_op jit(solution)/shard_map/ppermute | solution.py:244
